TPU v7x, 128 devices: a whole 4x4x4 slice. The times are simulated.
128 devices in a mesh: row: 8 (over y, z_lo), col: 16 (over x, z_hi, core).
Axes of the slice: x: 4, y: 4, z: 4 (z_hi: 2, z_lo: 2; z = z_hi * 2 + z_lo), core: 2. Of those that a mesh axis runs over, the one named last changes fastest.
Arguments:
- projections: float32 [24576, 256], P(('row', 'col')), may hold values from -1.5 to 1.5
- partner: int32 [24576], P(('row', 'col')), may hold values from 0 to 24575, as said below
Outputs:
- mean_objective: float32 [], replicated
- grad_projections: float32 [24576, 256], P(('row', 'col'))
Inputs may be any that keep to these rules, and one draw needn't show every extreme that they name: partner pairs the views: partner[partner[i]] == i and partner[i] != i for every view i.
All inputs are finite; a program needn't handle non-finite values.
Results may differ from a plain program's by a relative error of at most 0.0003.
Values sent between devices are 32-bit elements; how exact they have to be, the bound alone decides.
No kernel may reach another device: no remote copies, remote signals or barrier semaphores. Data moves between devices by JAX's collectives and lax.ppermute only.
A program may use at most 128 MiB of HBM per device.

v0:
```python
import jax
import jax.numpy as jnp
from jax import lax
from jax.sharding import PartitionSpec as P

logit_divisor = 0.1


def normalize(rows):
    scale = lax.rsqrt(jnp.sum(rows * rows, axis=-1, keepdims=True) + 1e-06)
    return (rows * scale, scale)


def scores_of(source_tile, target_tile):
    return (
        lax.dot_general(
            source_tile,
            target_tile,
            (((1,), (1,)), ((), ())),
            precision=lax.Precision.HIGHEST,
            preferred_element_type=jnp.float32,
        )
        / logit_divisor
    )


def span_ids(first, n_col, per_dev, view_tally):
    return first * n_col * per_dev + jnp.arange(view_tally, dtype=jnp.int32)


def strided_ids(second, n_col, per_dev, view_tally):
    place = jnp.arange(view_tally, dtype=jnp.int32)
    return place // per_dev * (n_col * per_dev) + second * per_dev + place % per_dev


def block_rows():
    return 512


def tile_expo(z_blk, anchor_tile_number, z_cols, column_indices):
    cosine_matrix = scores_of(z_blk, z_cols)
    exponentiated_logits = jnp.where(
        column_indices[None, :] == anchor_tile_number[:, None],
        jnp.float32(0.0),
        jnp.exp(cosine_matrix - 1.0 / logit_divisor),
    )
    return (cosine_matrix, exponentiated_logits)


def panel_stats(z_rows, p_rows, r_ids, z_cols, column_indices):
    view_tally = z_rows.shape[0]
    block = block_rows()
    number = view_tally // block
    c_float = column_indices.astype(jnp.float32)

    def stats(args):
        z_blk, p_blk, anchor_tile_number = args
        cosine_matrix, exponentiated_logits = tile_expo(
            z_blk, anchor_tile_number, z_cols, column_indices
        )
        anchor_partition_value = jnp.sum(exponentiated_logits, axis=1)
        partner_logit = jnp.sum(
            jnp.where(c_float[None, :] == p_blk[:, None], cosine_matrix, jnp.float32(0.0)), axis=1
        )
        return (anchor_partition_value, partner_logit, exponentiated_logits)

    anchor_partition_value, partner_logit, expo_blocks = lax.map(
        stats,
        (
            z_rows.reshape(number, block, -1),
            p_rows.reshape(number, block),
            r_ids.reshape(number, block),
        ),
    )
    return (
        anchor_partition_value.reshape(view_tally),
        partner_logit.reshape(view_tally),
        expo_blocks,
    )


def strip_derivatives(z_rows, p_rows, expo_blocks, anchor_partition_value, z_cols, column_indices):
    view_tally = z_rows.shape[0]
    tile_span_length = z_rows.shape[1]
    block = block_rows()
    number = view_tally // block
    c_float = column_indices.astype(jnp.float32)

    def derivative_list(carry, args):
        z_blk, p_blk, e_blk, r_blk = args
        g = e_blk / r_blk[:, None] - jnp.where(
            c_float[None, :] == p_blk[:, None], jnp.float32(1.0), jnp.float32(0.0)
        )
        a_blk = jnp.dot(
            g, z_cols, precision=lax.Precision.HIGHEST, preferred_element_type=jnp.float32
        )
        carry = carry + lax.dot_general(
            g,
            z_blk,
            (((0,), (0,)), ((), ())),
            precision=lax.Precision.HIGHEST,
            preferred_element_type=jnp.float32,
        )
        return (carry, a_blk)

    offset_first = jnp.zeros((z_cols.shape[0], tile_span_length), jnp.float32)
    target_contributions, source_contributions = lax.scan(
        derivative_list,
        offset_first,
        (
            z_rows.reshape(number, block, tile_span_length),
            p_rows.reshape(number, block),
            expo_blocks,
            anchor_partition_value.reshape(number, block),
        ),
    )
    return (source_contributions.reshape(view_tally, tile_span_length), target_contributions)


def shards(projections, partner):
    per_dev = projections.shape[0]
    z, scale = normalize(projections)
    p_float = partner.astype(jnp.float32)
    n_row = lax.axis_size("row")
    n_col = lax.axis_size("col")
    row_pos = lax.axis_index("row")
    col_pos = lax.axis_index("col")
    z_rows, p_rows = (
        lax.all_gather(z, "col", axis=0, tiled=True),
        lax.all_gather(p_float, "col", axis=0, tiled=True),
    )
    z_cols = lax.all_gather(z, "row", axis=0, tiled=True)
    r_ids = span_ids(row_pos, n_col, per_dev, z_rows.shape[0])
    column_indices = strided_ids(col_pos, n_col, per_dev, z_cols.shape[0])
    anchor_partition_value, partner_logit, expo_blocks = panel_stats(
        z_rows, p_rows, r_ids, z_cols, column_indices
    )
    anchor_partition_value, partner_logit = lax.psum((anchor_partition_value, partner_logit), "col")
    source_contributions, target_contributions = strip_derivatives(
        z_rows, p_rows, expo_blocks, anchor_partition_value, z_cols, column_indices
    )
    diagonal_sources = lax.psum_scatter(
        source_contributions, "col", scatter_dimension=0, tiled=True
    )
    diagonal_targets = lax.psum_scatter(
        target_contributions, "row", scatter_dimension=0, tiled=True
    )
    diagonal_aggregate = lax.dynamic_slice_in_dim(
        anchor_partition_value, col_pos * per_dev, per_dev
    )
    diagonal_partner = lax.dynamic_slice_in_dim(partner_logit, col_pos * per_dev, per_dev)
    resident_tile = jnp.sum(jnp.log(diagonal_aggregate) + 1.0 / logit_divisor - diagonal_partner)
    overall_aggregate = lax.psum(resident_tile, ("row", "col"))
    mean_objective = overall_aggregate / jnp.float32(per_dev * n_row * n_col)
    embedding_derivative = (diagonal_sources + diagonal_targets) / logit_divisor
    grad = (
        embedding_derivative - z * jnp.sum(z * embedding_derivative, axis=-1, keepdims=True)
    ) * scale
    return (mean_objective, grad)


def solution(mesh):
    placed = (P(("row", "col"), None), P(("row", "col")))
    return jax.shard_map(
        shards,
        mesh=mesh,
        in_specs=placed,
        out_specs=(P(), P(("row", "col"), None)),
        check_vma=False,
    )
```

profile of v0, /device:TPU:0, one launch (start us, length us, event | category | flops | bytes accessed | tf_op | source)
XLA Modules:
  0.0 445.3 jit_solution(14858697504737379852)
XLA Ops:
  13.7 71.1 %all-reduce = f32[3072]{0:T(1024)S(1)} all-reduce(f32[3072]{0:T(1024)S(1)} %convert_dynamic-update-slice_fusion), channel_id=1, replica_groups=mesh['row'=8,'col'=16] {'col'}, use_global_device_ids=true, to_apply=%add | all-reduce | flops 3072 | bytes 24576
  84.8 27.2 %all-gather.3.cloned.1.call-done = f32[3072,256]{1,0:T(8,128)} async-done(((f32[192,256]{1,0:T(8,128)}), f32[3072,256]{1,0:T(8,128)}) %all-gather.3.cloned.1.call-update) | async-done | bytes 3145744 | tf_op jit(solution)/shard_map/all_gather | solution.py:129
  112.0 46.7 %while.32 = (s32[]{:T(128)}, f32[6,512]{1,0:T(8,128)S(1)}, f32[6,512]{1,0:T(8,128)S(1)}, f32[6,512,1536]{2,1,0:T(8,128)}, s32[6,512]{1,0:T(8,128)S(1)}, /*index=...) while((s32[]{:T(128)}, f32[6,512]{1,0:T(8,128)S(1)}, ...), condition=%wide.region_4.5_spmd.clone.clone, body=%wide.region_1.4_spmd.clone.clone.sunk | while | flops 2424593408 | bytes 11591825 | solution.py:67
  112.1 5.4 %select_reduce_fusion.2 = (f32[512]{0:T(512)S(1)}, f32[512]{0:T(512)S(1)}, f32[512,1536]{1,0:T(8,128)S(1)}) fusion(f32[1536]{0:T(1024)S(1)} %get-tuple-element.427, f32[512]{0:T(512)S(1)} %bitcast.75, s32[512]{0:T(512)S(1)} %bitcast.68, s32[1536]{0:T(1024)S(1)} %get-tuple-element.428, f32[1536,256]{1,0:T(8,128)} %get-tuple-element.460, ...), kind=kOutput, calls=%fused_computation.55.clone.1 | convolution fusion | flops 2422209536 | bytes 5263364 | tf_op jit(solution)/shard_map/while/body/eval_jaxpr/dot_general | solution.py:16
  119.9 5.4 %select_reduce_fusion.2 = (f32[512]{0:T(512)S(1)}, f32[512]{0:T(512)S(1)}, f32[512,1536]{1,0:T(8,128)S(1)}) fusion(f32[1536]{0:T(1024)S(1)} %get-tuple-element.427, f32[512]{0:T(512)S(1)} %bitcast.75, s32[512]{0:T(512)S(1)} %bitcast.68, s32[1536]{0:T(1024)S(1)} %get-tuple-element.428, f32[1536,256]{1,0:T(8,128)} %get-tuple-element.460, ...), kind=kOutput, calls=%fused_computation.55.clone.1 | convolution fusion | flops 2422209536 | bytes 5263364 | tf_op jit(solution)/shard_map/while/body/eval_jaxpr/dot_general | solution.py:16
  127.7 5.4 %select_reduce_fusion.2 = (f32[512]{0:T(512)S(1)}, f32[512]{0:T(512)S(1)}, f32[512,1536]{1,0:T(8,128)S(1)}) fusion(f32[1536]{0:T(1024)S(1)} %get-tuple-element.427, f32[512]{0:T(512)S(1)} %bitcast.75, s32[512]{0:T(512)S(1)} %bitcast.68, s32[1536]{0:T(1024)S(1)} %get-tuple-element.428, f32[1536,256]{1,0:T(8,128)} %get-tuple-element.460, ...), kind=kOutput, calls=%fused_computation.55.clone.1 | convolution fusion | flops 2422209536 | bytes 5263364 | tf_op jit(solution)/shard_map/while/body/eval_jaxpr/dot_general | solution.py:16
  143.2 5.4 %select_reduce_fusion.2 = (f32[512]{0:T(512)S(1)}, f32[512]{0:T(512)S(1)}, f32[512,1536]{1,0:T(8,128)S(1)}) fusion(f32[1536]{0:T(1024)S(1)} %get-tuple-element.427, f32[512]{0:T(512)S(1)} %bitcast.75, s32[512]{0:T(512)S(1)} %bitcast.68, s32[1536]{0:T(1024)S(1)} %get-tuple-element.428, f32[1536,256]{1,0:T(8,128)} %get-tuple-element.460, ...), kind=kOutput, calls=%fused_computation.55.clone.1 | convolution fusion | flops 2422209536 | bytes 5263364 | tf_op jit(solution)/shard_map/while/body/eval_jaxpr/dot_general | solution.py:16
  151.0 5.4 %select_reduce_fusion.2 = (f32[512]{0:T(512)S(1)}, f32[512]{0:T(512)S(1)}, f32[512,1536]{1,0:T(8,128)S(1)}) fusion(f32[1536]{0:T(1024)S(1)} %get-tuple-element.427, f32[512]{0:T(512)S(1)} %bitcast.75, s32[512]{0:T(512)S(1)} %bitcast.68, s32[1536]{0:T(1024)S(1)} %get-tuple-element.428, f32[1536,256]{1,0:T(8,128)} %get-tuple-element.460, ...), kind=kOutput, calls=%fused_computation.55.clone.1 | convolution fusion | flops 2422209536 | bytes 5263364 | tf_op jit(solution)/shard_map/while/body/eval_jaxpr/dot_general | solution.py:16
  158.7 66.8 %all-reduce.1 = (f32[3072]{0:T(1024)S(1)}, f32[3072]{0:T(1024)S(1)}) all-reduce(f32[3072]{0:T(1024)S(1)} %reshape.105, f32[3072]{0:T(1024)S(1)} %reshape.104), channel_id=1, replica_groups=mesh['row'=8,'col'=16] {'col'}, use_global_device_ids=true, to_apply=%region_6.7 | all-reduce | flops 6144 | bytes 49152 | tf_op jit(solution)/shard_map/psum | solution.py:138
  225.5 88.2 %while.31 = (s32[]{:T(128)}, f32[1536,256]{1,0:T(8,128)}, f32[6,512,256]{2,1,0:T(8,128)}, f32[6,512,1536]{2,1,0:T(8,128)}, f32[6,512]{1,0:T(8,128)S(1)}, /*index...) while((s32[]{:T(128)}, f32[1536,256]{1,0:T(8,128)}, ...), condition=%wide.region_10.11_spmd.clone, body=%wide.region_9.10_spmd.clone.sunk | while | flops 4838940672 | bytes 18387616 | solution.py:107
  225.6 8.5 %fusion.87 = f32[1536,256]{1,0:T(8,128)} fusion(f32[6,512,1536]{2,1,0:T(8,128)} %get-tuple-element.490, s32[]{:T(128)S(6)} %copy.24, f32[1536,256]{1,0:T(8,128)} %get-tuple-element.477, f32[1536]{0:T(1024)S(1)} %fusion.86, f32[512]{0:T(512)S(1)} %bitcast.72, f32[512]{0:T(512)S(1)} %bitcast.70, pred[]{:T(512)S(6)} %compare.3, ...), kind=kOutput, calls=%fused_computation.15.clone.1 | convolution fusion | flops 2419851264 | bytes 6827520 | tf_op jit(solution)/shard_map/while/body/eval_jaxpr/dot_general | solution.py:97
  234.1 5.7 %fusion.88 = f32[6,512,256]{2,1,0:T(8,128)} fusion(f32[6,512,256]{2,1,0:T(8,128)} %get-tuple-element.478, s32[]{:T(128)S(6)} %copy.24, f32[1536,256]{1,0:T(8,128)S(1)} %copy-done.1, f32[6,512,1536]{2,1,0:T(8,128)} %get-tuple-element.490, f32[1536]{0:T(1024)S(1)} %fusion.86, f32[512]{0:T(512)S(1)} %bitcast.73, f32[512]{0:T(512)S(1)} %bitcast.71), kind=kOutput, calls=%fused_computation.27.clone.1 | convolution fusion | flops 2419064832 | bytes 5254144 | tf_op jit(solution)/shard_map/while/body/eval_jaxpr/dot_general | solution.py:94
  239.9 9.0 %fusion.87 = f32[1536,256]{1,0:T(8,128)} fusion(f32[6,512,1536]{2,1,0:T(8,128)} %get-tuple-element.490, s32[]{:T(128)S(6)} %copy.24, f32[1536,256]{1,0:T(8,128)} %get-tuple-element.477, f32[1536]{0:T(1024)S(1)} %fusion.86, f32[512]{0:T(512)S(1)} %bitcast.72, f32[512]{0:T(512)S(1)} %bitcast.70, pred[]{:T(512)S(6)} %compare.3, ...), kind=kOutput, calls=%fused_computation.15.clone.1 | convolution fusion | flops 2419851264 | bytes 6827520 | tf_op jit(solution)/shard_map/while/body/eval_jaxpr/dot_general | solution.py:97
  248.9 5.7 %fusion.88 = f32[6,512,256]{2,1,0:T(8,128)} fusion(f32[6,512,256]{2,1,0:T(8,128)} %get-tuple-element.478, s32[]{:T(128)S(6)} %copy.24, f32[1536,256]{1,0:T(8,128)S(1)} %copy-done.1, f32[6,512,1536]{2,1,0:T(8,128)} %get-tuple-element.490, f32[1536]{0:T(1024)S(1)} %fusion.86, f32[512]{0:T(512)S(1)} %bitcast.73, f32[512]{0:T(512)S(1)} %bitcast.71), kind=kOutput, calls=%fused_computation.27.clone.1 | convolution fusion | flops 2419064832 | bytes 5254144 | tf_op jit(solution)/shard_map/while/body/eval_jaxpr/dot_general | solution.py:94
  254.7 9.0 %fusion.87 = f32[1536,256]{1,0:T(8,128)} fusion(f32[6,512,1536]{2,1,0:T(8,128)} %get-tuple-element.490, s32[]{:T(128)S(6)} %copy.24, f32[1536,256]{1,0:T(8,128)} %get-tuple-element.477, f32[1536]{0:T(1024)S(1)} %fusion.86, f32[512]{0:T(512)S(1)} %bitcast.72, f32[512]{0:T(512)S(1)} %bitcast.70, pred[]{:T(512)S(6)} %compare.3, ...), kind=kOutput, calls=%fused_computation.15.clone.1 | convolution fusion | flops 2419851264 | bytes 6827520 | tf_op jit(solution)/shard_map/while/body/eval_jaxpr/dot_general | solution.py:97
  263.7 5.7 %fusion.88 = f32[6,512,256]{2,1,0:T(8,128)} fusion(f32[6,512,256]{2,1,0:T(8,128)} %get-tuple-element.478, s32[]{:T(128)S(6)} %copy.24, f32[1536,256]{1,0:T(8,128)S(1)} %copy-done.1, f32[6,512,1536]{2,1,0:T(8,128)} %get-tuple-element.490, f32[1536]{0:T(1024)S(1)} %fusion.86, f32[512]{0:T(512)S(1)} %bitcast.73, f32[512]{0:T(512)S(1)} %bitcast.71), kind=kOutput, calls=%fused_computation.27.clone.1 | convolution fusion | flops 2419064832 | bytes 5254144 | tf_op jit(solution)/shard_map/while/body/eval_jaxpr/dot_general | solution.py:94
  269.5 9.0 %fusion.87 = f32[1536,256]{1,0:T(8,128)} fusion(f32[6,512,1536]{2,1,0:T(8,128)} %get-tuple-element.490, s32[]{:T(128)S(6)} %copy.24, f32[1536,256]{1,0:T(8,128)} %get-tuple-element.477, f32[1536]{0:T(1024)S(1)} %fusion.86, f32[512]{0:T(512)S(1)} %bitcast.72, f32[512]{0:T(512)S(1)} %bitcast.70, pred[]{:T(512)S(6)} %compare.3, ...), kind=kOutput, calls=%fused_computation.15.clone.1 | convolution fusion | flops 2419851264 | bytes 6827520 | tf_op jit(solution)/shard_map/while/body/eval_jaxpr/dot_general | solution.py:97
  278.5 5.7 %fusion.88 = f32[6,512,256]{2,1,0:T(8,128)} fusion(f32[6,512,256]{2,1,0:T(8,128)} %get-tuple-element.478, s32[]{:T(128)S(6)} %copy.24, f32[1536,256]{1,0:T(8,128)S(1)} %copy-done.1, f32[6,512,1536]{2,1,0:T(8,128)} %get-tuple-element.490, f32[1536]{0:T(1024)S(1)} %fusion.86, f32[512]{0:T(512)S(1)} %bitcast.73, f32[512]{0:T(512)S(1)} %bitcast.71), kind=kOutput, calls=%fused_computation.27.clone.1 | convolution fusion | flops 2419064832 | bytes 5254144 | tf_op jit(solution)/shard_map/while/body/eval_jaxpr/dot_general | solution.py:94
  284.3 9.0 %fusion.87 = f32[1536,256]{1,0:T(8,128)} fusion(f32[6,512,1536]{2,1,0:T(8,128)} %get-tuple-element.490, s32[]{:T(128)S(6)} %copy.24, f32[1536,256]{1,0:T(8,128)} %get-tuple-element.477, f32[1536]{0:T(1024)S(1)} %fusion.86, f32[512]{0:T(512)S(1)} %bitcast.72, f32[512]{0:T(512)S(1)} %bitcast.70, pred[]{:T(512)S(6)} %compare.3, ...), kind=kOutput, calls=%fused_computation.15.clone.1 | convolution fusion | flops 2419851264 | bytes 6827520 | tf_op jit(solution)/shard_map/while/body/eval_jaxpr/dot_general | solution.py:97
  293.3 5.7 %fusion.88 = f32[6,512,256]{2,1,0:T(8,128)} fusion(f32[6,512,256]{2,1,0:T(8,128)} %get-tuple-element.478, s32[]{:T(128)S(6)} %copy.24, f32[1536,256]{1,0:T(8,128)S(1)} %copy-done.1, f32[6,512,1536]{2,1,0:T(8,128)} %get-tuple-element.490, f32[1536]{0:T(1024)S(1)} %fusion.86, f32[512]{0:T(512)S(1)} %bitcast.73, f32[512]{0:T(512)S(1)} %bitcast.71), kind=kOutput, calls=%fused_computation.27.clone.1 | convolution fusion | flops 2419064832 | bytes 5254144 | tf_op jit(solution)/shard_map/while/body/eval_jaxpr/dot_general | solution.py:94
  299.0 9.0 %fusion.87 = f32[1536,256]{1,0:T(8,128)} fusion(f32[6,512,1536]{2,1,0:T(8,128)} %get-tuple-element.490, s32[]{:T(128)S(6)} %copy.24, f32[1536,256]{1,0:T(8,128)} %get-tuple-element.477, f32[1536]{0:T(1024)S(1)} %fusion.86, f32[512]{0:T(512)S(1)} %bitcast.72, f32[512]{0:T(512)S(1)} %bitcast.70, pred[]{:T(512)S(6)} %compare.3, ...), kind=kOutput, calls=%fused_computation.15.clone.1 | convolution fusion | flops 2419851264 | bytes 6827520 | tf_op jit(solution)/shard_map/while/body/eval_jaxpr/dot_general | solution.py:97
  308.1 5.7 %fusion.88 = f32[6,512,256]{2,1,0:T(8,128)} fusion(f32[6,512,256]{2,1,0:T(8,128)} %get-tuple-element.478, s32[]{:T(128)S(6)} %copy.24, f32[1536,256]{1,0:T(8,128)S(1)} %copy-done.1, f32[6,512,1536]{2,1,0:T(8,128)} %get-tuple-element.490, f32[1536]{0:T(1024)S(1)} %fusion.86, f32[512]{0:T(512)S(1)} %bitcast.73, f32[512]{0:T(512)S(1)} %bitcast.71), kind=kOutput, calls=%fused_computation.27.clone.1 | convolution fusion | flops 2419064832 | bytes 5254144 | tf_op jit(solution)/shard_map/while/body/eval_jaxpr/dot_general | solution.py:94
  315.1 66.9 %psum.23 = f32[]{:T(128)} all-reduce(f32[]{:T(128)} %subtract_reduce_fusion), channel_id=1, replica_groups=mesh['row'=8,'col'=16] {'row','col'}, use_global_device_ids=true, to_apply=%region_8.9 | all-reduce | flops 1 | bytes 8 | tf_op jit(solution)/shard_map/psum | solution.py:153
  382.7 51.9 %reduce-scatter.3.cloned.1.call-done = f32[192,256]{1,0:T(8,128)} async-done(((f32[3072,256]{1,0:T(8,128)}), f32[192,256]{1,0:T(8,128)}) %reduce-scatter.3.cloned.1.call-update) | async-done | bytes 196624 | tf_op jit(solution)/shard_map/reduce_scatter | solution.py:142
  (92 shorter events, 29.8 us)
Async XLA Ops:
  7.2 77.6 %all-gather.5.cloned.1.call-start = ((), (), s32[]{:S(2)}) async-start(), calls=%async_computation.3 | async-start | bytes 1769472 | tf_op jit(solution)/shard_map/all_gather | solution.py:132
  10.0 102.0 %all-gather.3.cloned.1.call-start = ((), (), s32[]{:S(2)}) async-start(), calls=%async_computation.2 | async-start | bytes 3342336 | tf_op jit(solution)/shard_map/all_gather | solution.py:129
  10.7 371.9 %reduce-scatter.5.cloned.1.call-start = ((), (), s32[]{:S(2)}) async-start(), calls=%async_computation.5 | async-start | bytes 1769472 | tf_op jit(solution)/shard_map/reduce_scatter | solution.py:145
  225.6 8.5 %copy-start.1 = (f32[1536,256]{1,0:T(8,128)S(1)}, f32[1536,256]{1,0:T(8,128)}, u32[]{:S(2)}) copy-start(f32[1536,256]{1,0:T(8,128)} %get-tuple-element.494) | copy-start | bytes 4718596 | tf_op jit(solution)/shard_map/while
  239.9 9.1 %copy-start.1 = (f32[1536,256]{1,0:T(8,128)S(1)}, f32[1536,256]{1,0:T(8,128)}, u32[]{:S(2)}) copy-start(f32[1536,256]{1,0:T(8,128)} %get-tuple-element.494) | copy-start | bytes 4718596 | tf_op jit(solution)/shard_map/while
  254.7 9.1 %copy-start.1 = (f32[1536,256]{1,0:T(8,128)S(1)}, f32[1536,256]{1,0:T(8,128)}, u32[]{:S(2)}) copy-start(f32[1536,256]{1,0:T(8,128)} %get-tuple-element.494) | copy-start | bytes 4718596 | tf_op jit(solution)/shard_map/while
  269.4 9.1 %copy-start.1 = (f32[1536,256]{1,0:T(8,128)S(1)}, f32[1536,256]{1,0:T(8,128)}, u32[]{:S(2)}) copy-start(f32[1536,256]{1,0:T(8,128)} %get-tuple-element.494) | copy-start | bytes 4718596 | tf_op jit(solution)/shard_map/while
  284.2 9.1 %copy-start.1 = (f32[1536,256]{1,0:T(8,128)S(1)}, f32[1536,256]{1,0:T(8,128)}, u32[]{:S(2)}) copy-start(f32[1536,256]{1,0:T(8,128)} %get-tuple-element.494) | copy-start | bytes 4718596 | tf_op jit(solution)/shard_map/while
  299.0 9.1 %copy-start.1 = (f32[1536,256]{1,0:T(8,128)S(1)}, f32[1536,256]{1,0:T(8,128)}, u32[]{:S(2)}) copy-start(f32[1536,256]{1,0:T(8,128)} %get-tuple-element.494) | copy-start | bytes 4718596 | tf_op jit(solution)/shard_map/while
  313.8 120.8 %copy-start = (f32[192,256]{1,0:T(8,128)S(1)}, f32[192,256]{1,0:T(8,128)}, u32[]{:S(2)}) copy-start(f32[192,256]{1,0:T(8,128)} %param.6) | copy-start | bytes 589828
  313.8 120.8 %reduce-scatter.3.cloned.1.call-start = ((), (), s32[]{:S(2)}) async-start(), calls=%async_computation.4 | async-start | bytes 3342336 | tf_op jit(solution)/shard_map/reduce_scatter | solution.py:142
Sparse Core Ops, SparseCore 0:
  10.2 46.9 all-gather.4
  60.2 51.8 all-gather.2
  313.9 42.2 reduce-scatter.4
  360.1 74.4 reduce-scatter.2
where the time goes:
time: 446 us; the launch traced here: 445 us
  blocking collectives  205 us (46%)
  matrix products  120 us (27%)
  waiting for transfers between devices  80.5 us (18%)
  other arithmetic  20.7 us (5%)
  between operations  16.3 us (4%)
    unnamed x1, blocking collectives  71.1 us
    psum x1, blocking collectives, shards(): overall_aggregate = lax.psum(resident_tile, ('row', 'col'))  66.9 us
    psum x1, blocking collectives, shards(): lax.psum((anchor_partition_value, partner_logit), 'col')  66.8 us
    dot_general x6, matrix products, derivative_list(): lax.dot_general(g, z_blk, (((0,), (0,)), ((), ())), precision=lax.Precisi...  53.8 us
    reduce_scatter x1, waiting for transfers between devices, shards(): lax.psum_scatter(source_contributions, 'col', scatter_dimension=0, tiled=...  51.9 us
    dot_general x6, matrix products, derivative_list(): jnp.dot(g, z_cols, precision=lax.Precision.HIGHEST, preferred_element_typ...  34.1 us
    dot_general x6, matrix products, scores_of(): lax.dot_general(source_tile, target_tile, (((1,), (1,)), ((), ())), preci...  32.3 us
    all_gather x1, waiting for transfers between devices, shards(): lax.all_gather(z, 'col', axis=0, tiled=True)  27.2 us
  transfers between devices with their start and end apart: 4, of which 2 were waited for; matrix products, arithmetic and copies ran while one was open for 1% of the time, Pallas kernels for 0%

commit v1 on v0

v1 whole, which is shorter than its diff:
```python
import functools

import jax
import jax.numpy as jnp
from jax import lax
from jax.experimental import pallas as pl
from jax.experimental.pallas import tpu as pltpu
from jax.sharding import Mesh, PartitionSpec as P

f32, bf16 = jnp.float32, jnp.bfloat16
PER = 192
D = 256
VIEWS = 24576
C_BLOCKS = 8
R_BLOCKS = 16
C = C_BLOCKS * PER
R = R_BLOCKS * PER
SPAN = 768
STEPS = R // SPAN
LANES = 256
BLOCK = 200
TEMPERATURE = 0.1
LOG2E = 1.4426950408889634
LN2 = 0.6931471805599453
NT = (((1,), (1,)), ((), ()))
ROW = ("y", "zl")
COL = ("x", "zh", "core")
ALL = ROW + COL


def unit(rows):
    return rows * lax.rsqrt(jnp.sum(rows * rows, axis=-1, keepdims=True) + 1e-06)


def halves(a):
    hi = a.astype(bf16)
    return hi, (a - hi.astype(f32)).astype(bf16)


def score_kernel(
    first_ref, xc_ref, own_ref, other_ref, ids_ref, partner_ref,
    e_ref, zr_ref, rsum_ref, csum_ref, pos_ref, cid_ref,
    a_ref, b_ref, cacc_ref, pacc_ref,
):
    k = pl.program_id(0)
    nb = SPAN // PER

    @pl.when(k == 0)
    def _():
        cacc_ref[...] = jnp.zeros_like(cacc_ref)
        pacc_ref[...] = jnp.zeros_like(pacc_ref)

        @pl.loop(0, C_BLOCKS)
        def _(b):
            rows = pl.ds(pl.multiple_of(b * PER, PER), PER)
            hi, lo = halves(unit(xc_ref[b]) * (LOG2E / TEMPERATURE))
            a_ref[rows, 0:D] = hi
            a_ref[rows, D : 2 * D] = lo
            a_ref[rows, 2 * D : 3 * D] = hi
            cid_ref[rows, :] = (
                first_ref[0] + b * (R_BLOCKS * PER) + lax.broadcasted_iota(jnp.int32, (PER, 128), 0)
            )

    def prepare(blocks_ref):
        for b in range(nb):
            hi, lo = halves(unit(blocks_ref[b, 0:PER, :]))
            rows = pl.ds(b * PER, PER)
            b_ref[rows, 0:D] = hi
            b_ref[rows, D : 2 * D] = hi
            b_ref[rows, 2 * D : 3 * D] = lo
            zr_ref[rows, 0:D] = hi
            zr_ref[rows, D : 2 * D] = lo

    @pl.when(k < STEPS // 2)
    def _():
        prepare(own_ref)

    @pl.when(k >= STEPS // 2)
    def _():
        prepare(other_ref)

    cid = cid_ref[...]
    for n in range(SPAN // LANES):
        cols = pl.ds(n * LANES, LANES)
        s = lax.dot_general(a_ref[...], b_ref[cols, :], NT, preferred_element_type=f32)
        row_total = None
        for h in range(LANES // 128):
            lanes = pl.ds(n * LANES + h * 128, 128)
            part = s[:, h * 128 : (h + 1) * 128]
            e = jnp.where(cid == ids_ref[:, lanes], 0.0, jnp.exp2(part))
            hit = jnp.where(cid == partner_ref[:, lanes], part, 0.0)
            e_ref[:, lanes] = e
            rsum_ref[:, lanes] = jnp.sum(e, axis=0, keepdims=True)
            pacc_ref[...] += jnp.sum(hit.reshape(C // 8, 8, 128), axis=0)
            row_total = e if row_total is None else row_total + e
        cacc_ref[...] += row_total

    @pl.when(k == STEPS - 1)
    def _():
        csum_ref[...] = lax.dot_general(
            jnp.ones((8, 128), f32), cacc_ref[...], NT, precision=lax.Precision.HIGHEST, preferred_element_type=f32
        )
        pos_ref[...] = pacc_ref[...]


def scores(first, xc, own, other, ids, partner):
    half = STEPS // 2
    nb = SPAN // PER
    whole = lambda k: (0, 0)
    return pl.pallas_call(
        score_kernel,
        grid=(STEPS,),
        in_specs=[
            pl.BlockSpec(memory_space=pltpu.SMEM),
            pl.BlockSpec((C_BLOCKS, PER, D), lambda k: (0, 0, 0)),
            pl.BlockSpec((nb, BLOCK, D), lambda k: (jnp.minimum(k, half - 1), 0, 0)),
            pl.BlockSpec((nb, BLOCK, D), lambda k: (jnp.maximum(k - half, 0), 0, 0)),
            pl.BlockSpec((1, SPAN), lambda k: (0, k)),
            pl.BlockSpec((1, SPAN), lambda k: (0, k)),
        ],
        out_specs=[
            pl.BlockSpec((C, SPAN), lambda k: (0, k)),
            pl.BlockSpec((SPAN, 2 * D), lambda k: (k, 0)),
            pl.BlockSpec((1, SPAN), lambda k: (0, k)),
            pl.BlockSpec((8, C), whole),
            pl.BlockSpec((8, 128), whole),
            pl.BlockSpec((C, 128), whole),
        ],
        out_shape=[
            jax.ShapeDtypeStruct((C, R), f32),
            jax.ShapeDtypeStruct((R, 2 * D), bf16),
            jax.ShapeDtypeStruct((1, R), f32),
            jax.ShapeDtypeStruct((8, C), f32),
            jax.ShapeDtypeStruct((8, 128), f32),
            jax.ShapeDtypeStruct((C, 128), jnp.int32),
        ],
        scratch_shapes=[
            pltpu.VMEM((C, 3 * D), bf16),
            pltpu.VMEM((SPAN, 3 * D), bf16),
            pltpu.VMEM((C, 128), f32),
            pltpu.VMEM((8, 128), f32),
        ],
        compiler_params=pltpu.CompilerParams(vmem_limit_bytes=56 << 20),
    )(first, xc, own, other, ids, partner)


def gradient_kernel(
    logs_ref, e_ref, z_ref, ur_ref, uc_ref, partner_ref, cid_ref,
    out_ref,
    g_ref, w_ref, acc_ref,
):
    k = pl.program_id(0)

    @pl.when(k == 0)
    def _():
        acc_ref[...] = jnp.zeros_like(acc_ref)

    w_ref[0:SPAN, :] = z_ref[:, 0:D]
    w_ref[SPAN : 2 * SPAN, :] = z_ref[:, 0:D]
    w_ref[2 * SPAN : 3 * SPAN, :] = z_ref[:, D : 2 * D]
    for h in range(SPAN // 128):
        lanes = pl.ds(h * 128, 128)
        g = e_ref[:, lanes] * (uc_ref[...] + ur_ref[:, lanes])
        g = g - jnp.where(cid_ref[...] == partner_ref[:, lanes], 2.0, 0.0)
        hi, lo = halves(g)
        g_ref[:, lanes] = hi
        g_ref[:, pl.ds(SPAN + h * 128, 128)] = lo
        g_ref[:, pl.ds(2 * SPAN + h * 128, 128)] = hi
    acc_ref[...] += jnp.dot(g_ref[...], w_ref[...], preferred_element_type=f32)

    @pl.when(k == STEPS - 1)
    def _():
        for b in range(C_BLOCKS):
            out_ref[b, 0:PER, :] = acc_ref[b * PER : (b + 1) * PER, :]
            out_ref[b, PER:BLOCK, :] = jnp.full((BLOCK - PER, D), logs_ref[0], f32)


def gradients(logs, e, z, ur, uc, partner, cid):
    whole = lambda k: (0, 0)
    return pl.pallas_call(
        gradient_kernel,
        grid=(STEPS,),
        in_specs=[
            pl.BlockSpec(memory_space=pltpu.SMEM),
            pl.BlockSpec((C, SPAN), lambda k: (0, k)),
            pl.BlockSpec((SPAN, 2 * D), lambda k: (k, 0)),
            pl.BlockSpec((1, SPAN), lambda k: (0, k)),
            pl.BlockSpec((C, 128), whole),
            pl.BlockSpec((1, SPAN), lambda k: (0, k)),
            pl.BlockSpec((C, 128), whole),
        ],
        out_specs=pl.BlockSpec((C_BLOCKS, BLOCK, D), lambda k: (0, 0, 0)),
        out_shape=jax.ShapeDtypeStruct((C_BLOCKS, BLOCK, D), f32),
        scratch_shapes=[
            pltpu.VMEM((C, 3 * SPAN), bf16),
            pltpu.VMEM((3 * SPAN, D), bf16),
            pltpu.VMEM((C, D), f32),
        ],
        compiler_params=pltpu.CompilerParams(vmem_limit_bytes=60 << 20),
    )(logs, e, z, ur, uc, partner, cid)


def by_core(pair, core):
    return jnp.where(core == 0, pair, pair[::-1])


def shards(projections, partner):
    row = lax.axis_index(ROW)
    col = lax.axis_index(COL)
    core = lax.axis_index("core")

    xc = jnp.broadcast_to(projections[None], (C_BLOCKS, PER, D)).reshape(C, D)
    xc = lax.all_to_all(xc, ROW, 0, 0, tiled=True).reshape(C_BLOCKS, PER, D)
    tail = jnp.pad(partner.astype(f32)[None], ((0, BLOCK - PER - 1), (0, D - PER)))
    block = jnp.concatenate([projections, tail])
    own = jnp.broadcast_to(block[None], (8, BLOCK, D)).reshape(8 * BLOCK, D)
    own = lax.all_to_all(own, ("x", "zh"), 0, 0, tiled=True)
    other = lax.ppermute(own, "core", [(0, 1), (1, 0)])
    own, other = own.reshape(8, BLOCK, D), other.reshape(8, BLOCK, D)

    partner_r = jnp.stack([own[:, PER, :PER], other[:, PER, :PER]]).reshape(1, R).astype(jnp.int32)
    blocks = 2 * jnp.arange(8, dtype=jnp.int32)
    blocks = jnp.stack([blocks + core, blocks + 1 - core]) + row * R_BLOCKS
    ids = (blocks[:, :, None] * PER + jnp.arange(PER, dtype=jnp.int32)).reshape(1, R)

    first = (col * PER).astype(jnp.int32).reshape(1)
    e, z, rsum, csum, pos, cid = scores(first, xc, own, other, ids, partner_r)

    to_rows = by_core(rsum.reshape(2, 8, PER), core).transpose(1, 0, 2).reshape(1, R_BLOCKS, PER)
    sums = jnp.concatenate(
        [
            jnp.broadcast_to(csum[0].reshape(C_BLOCKS, 1, PER), (C_BLOCKS, R_BLOCKS, PER)),
            jnp.broadcast_to(to_rows, (C_BLOCKS, R_BLOCKS, PER)),
            jnp.broadcast_to(jnp.sum(pos), (C_BLOCKS, R_BLOCKS, 128)),
        ],
        axis=2,
    ).reshape(C_BLOCKS * R_BLOCKS, 512)
    sums = lax.all_to_all(sums, ALL, 0, 0, tiled=True).reshape(C_BLOCKS, R_BLOCKS, 512)
    total_r = jnp.sum(sums[:, :, :PER], axis=0)
    total_c = jnp.sum(sums[:, :, PER : 2 * PER], axis=1)
    positives = jnp.sum(sums[:, :, 2 * PER]) * LN2
    ur = by_core((1.0 / total_r).reshape(8, 2, PER).transpose(1, 0, 2), core).reshape(1, R)
    uc = jnp.broadcast_to((1.0 / total_c).reshape(C, 1), (C, 128))
    logs = jnp.sum(jnp.log(total_r)).reshape(1)

    terms = gradients(logs, e, z, ur, uc, partner_r, cid)
    terms = lax.all_to_all(terms.reshape(C_BLOCKS * BLOCK, D), ROW, 0, 0, tiled=True)
    terms = jnp.sum(terms.reshape(C_BLOCKS, BLOCK, D), axis=0)

    mean_objective = (terms[PER, 0] - positives) / VIEWS
    scale = lax.rsqrt(jnp.sum(projections * projections, axis=-1, keepdims=True) + 1e-06)
    z_own = projections * scale
    dz = terms[:PER] / TEMPERATURE
    grad = (dz - z_own * jnp.sum(z_own * dz, axis=-1, keepdims=True)) * scale
    return mean_objective, grad


def solution(mesh):
    fine = Mesh(mesh.devices.reshape(4, 2, 4, 2, 2), ALL)
    placed = (P(ALL, None), P(ALL))
    return jax.shard_map(
        shards, mesh=fine, in_specs=placed, out_specs=(P(), P(ALL, None)), check_vma=False
    )
```

time: 446 us -> 156 us (0.35)
  blocking collectives: 205 us -> 46.2 us
  matrix products: 120 us -> 0 us
  waiting for transfers between devices: 80.5 us -> 45.9 us
  Pallas kernels: 0 us -> 34.4 us
  other arithmetic: 20.7 us -> 7.11 us
  between operations: 16.3 us -> 3.27 us
  starting transfers between devices: 0.16 us -> 8.51 us
  local copies, waits for them, and re-layouts: 2.29 us -> 10.1 us
    psum x2 -> x0, blocking collectives: 134 us -> none  [the longest x1 66.9 us: shards(): overall_aggregate = lax.psum(resident_tile, ('row', 'col'))]
    dot_general x18 -> x0, matrix products: 120 us -> none  [the longest x6 53.8 us: derivative_list(): lax.dot_general(g, z_blk, (((0,), (0,)), ((), ())), precision=lax.Precisi...]
    unnamed x1 -> x0, blocking collectives: 71.1 us -> none
    reduce_scatter x2 -> x0, waiting for transfers between devices: 51.9 us -> none  [the longest x1 51.9 us: shards(): lax.psum_scatter(source_contributions, 'col', scatter_dimension=0, tiled=...]
    all_to_all x0 -> x2, blocking collectives: none -> 46.2 us  [the longest x1 31.4 us: shards(): own = lax.all_to_all(own, ('x', 'zh'), 0, 0, tiled=True)]
    all_to_all x0 -> x2, waiting for transfers between devices: none -> 45.9 us  [the longest x1 23.5 us: shards(): lax.all_to_all(terms.reshape(C_BLOCKS * BLOCK, D), ROW, 0, 0, tiled=True)]
    pallas_call x0 -> x2, Pallas kernels: none -> 34.4 us  [the longest x1 17.9 us: scores(): pl.pallas_call(score_kernel, grid=(STEPS,), in_specs=[pl.BlockSpec(memory...]
    all_gather x2 -> x0, waiting for transfers between devices: 27.3 us -> none  [the longest x1 27.2 us: shards(): lax.all_gather(z, 'col', axis=0, tiled=True)]
  transfers between devices with their start and end apart: 4 -> 3, of which waited for: 2 -> 2; matrix products, arithmetic and copies ran while one was open for 1% -> 3% of each run, Pallas kernels for 0% -> 0%
where the time goes in v1:
time: 156 us
  blocking collectives  46.2 us (30%)
  waiting for transfers between devices  45.9 us (29%)
  Pallas kernels  34.4 us (22%)
  local copies, waits for them, and re-layouts  10.1 us (6%)
  starting transfers between devices  8.51 us (5%)
  other arithmetic  7.11 us (5%)
  between operations  3.27 us (2%)
    all_to_all x1, blocking collectives, shards(): own = lax.all_to_all(own, ('x', 'zh'), 0, 0, tiled=True)  31.4 us
    all_to_all x1, waiting for transfers between devices, shards(): lax.all_to_all(terms.reshape(C_BLOCKS * BLOCK, D), ROW, 0, 0, tiled=True)  23.5 us
    all_to_all x1, waiting for transfers between devices, shards(): xc = lax.all_to_all(xc, ROW, 0, 0, tiled=True).reshape(C_BLOCKS, PER, D)  22.4 us
    pallas_call x1, Pallas kernels, scores(): pl.pallas_call(score_kernel, grid=(STEPS,), in_specs=[pl.BlockSpec(memory...  17.9 us
    pallas_call x1, Pallas kernels, gradients(): pl.pallas_call(gradient_kernel, grid=(STEPS,), in_specs=[pl.BlockSpec(mem...  16.5 us
    all_to_all x1, blocking collectives, shards(): lax.all_to_all(sums, ALL, 0, 0, tiled=True).reshape(C_BLOCKS, R_BLOCKS, 512)  14.9 us
    all_to_all x1, starting transfers between devices, shards(): xc = lax.all_to_all(xc, ROW, 0, 0, tiled=True).reshape(C_BLOCKS, PER, D)  4.93 us
    all_to_all x1, starting transfers between devices, shards(): lax.all_to_all(terms.reshape(C_BLOCKS * BLOCK, D), ROW, 0, 0, tiled=True)  3.58 us
  transfers between devices with their start and end apart: 3, of which 2 were waited for; matrix products, arithmetic and copies ran while one was open for 3% of the time, Pallas kernels for 0%

profile of v1, /device:TPU:0, one launch (start us, length us, event | category | flops | bytes accessed | tf_op | source)
XLA Modules:
  0.0 155.5 jit_solution(4173718460011264379)
XLA Ops:
  0.6 0.7 convert_element_type.10
  1.3 0.9 select_maximum_fusion
  2.4 31.4 %all_to_all.30.own_ref = f32[8,200,256]{2,1,0:T(8,128)S(1)} all-to-all(f32[8,200,256]{2,1,0:T(8,128)S(1)} %broadcast_in_dim.20), channel_id=1, replica_groups=mesh['y'=4,'zl'=2,'x'=4,'zh'=2,'core'=2] {'x','zh'}, dimensions={0} | all-to-all | bytes 3276800 | tf_op jit(solution)/shard_map/all_to_all | solution.py:217
  33.8 1.4 broadcast_in_dim.18
  35.1 4.9 %all-to-all-start = ((f32[8,192,256]{2,1,0:T(8,128)}), f32[8,192,256]{2,1,0:T(8,128)S(1)}, u32[]{:S(2)}, u32[]{:S(2)}) async-start(f32[8,192,256]{2,1,0:T(8,128)} %broadcast_in_dim.18), calls=%async_computation | async-start | bytes 3145728 | tf_op jit(solution)/shard_map/all_to_all | solution.py:213
  40.2 0.7 add.93.ids_ref
  40.9 0.8 slice_bitcast_fusion
  41.8 0.7 convert_element_type.12.partner_ref
  42.4 22.4 %all-to-all-done.xc_ref = f32[8,192,256]{2,1,0:T(8,128)S(1)} async-done(((f32[8,192,256]{2,1,0:T(8,128)}), f32[8,192,256]{2,1,0:T(8,128)S(1)}, u32[]{:S(2)}, u32[]{:S(2)}) %all-to-all-start) | async-done | bytes 1572896 | tf_op jit(solution)/shard_map/all_to_all | solution.py:213
  64.8 1.2 copy-done.1
  66.0 17.9 %shard_map.41 = (f32[1536,3072]{1,0:T(8,128)}, bf16[3072,512]{1,0:T(8,128)(2,1)}, f32[1,3072]{1,0:T(1,128)}, f32[8,1536]{1,0:T(8,128)}, f32[8,128]{1,0:T(8,128)}, /*index=5*/s32[1536,128]{1,0:T(8,128)}) custom-call(s32[1]{0:T(128)} %bitcast.first_ref, f32[8,192,256]{2,1,0:T(8,128)} %copy-done.1, f32[8,200,256]{2,1,0:T(8,128)} %copy-done, ...), custom_call_target="tpu_custom_call" | custom-call | tf_op jit(solution)/shard_map/pallas_call | solution.py:110
  84.5 1.4 reduce.7
  86.1 0.8 slice_reduce_fusion.3
  87.0 1.3 reduce_sum.72
  88.3 0.6 broadcast_in_dim.48
  89.4 14.9 %all_to_all.31 = f32[128,1,512]{2,1,0:T(1,128)S(1)} all-to-all(f32[128,1,512]{2,1,0:T(1,128)S(1)} %all_to_all.23), channel_id=1, replica_groups=mesh['y'=4,'zl'=2,'x'=4,'zh'=2,'core'=2] {'y','zl','x','zh','core'}, dimensions={0} | all-to-all | bytes 524288 | tf_op jit(solution)/shard_map/all_to_all | solution.py:238
  104.5 0.6 broadcast_divide_fusion
  105.3 0.7 reshape.143.ur_ref
  106.0 1.1 broadcast_in_dim.49.uc_ref
  107.1 16.5 %shard_map.42 = f32[8,200,256]{2,1,0:T(8,128)} custom-call(f32[1]{0:T(128)} %bitcast.7.logs_ref, f32[1536,3072]{1,0:T(8,128)} %get-tuple-element.11.e_ref, bf16[3072,512]{1,0:T(8,128)(2,1)} %get-tuple-element.12.z_ref, f32[1,3072]{1,0:T(1,128)} %reshape.143.ur_ref, f32[1536,128]{1,0:T(8,128)} %broadcast_in_dim.49.uc_ref, ...), custom_call_target="tpu_custom_call" | custom-call | tf_op jit(solution)/shard_map/pallas_call | solution.py:180
  123.6 3.6 %all-to-all-start.3 = ((f32[8,200,256]{2,1,0:T(8,128)}), f32[8,200,256]{2,1,0:T(8,128)S(1)}, u32[]{:S(2)}, u32[]{:S(2)}) async-start(f32[8,200,256]{2,1,0:T(8,128)} %shard_map.42), calls=%async_computation.3 | async-start | bytes 3276800 | tf_op jit(solution)/shard_map/all_to_all | solution.py:247
  127.3 0.6 slice_reduce_fusion.2
  128.6 23.5 %all-to-all-done.3 = f32[8,200,256]{2,1,0:T(8,128)S(1)} async-done(((f32[8,200,256]{2,1,0:T(8,128)}), f32[8,200,256]{2,1,0:T(8,128)S(1)}, u32[]{:S(2)}, u32[]{:S(2)}) %all-to-all-start.3) | async-done | bytes 1638432 | tf_op jit(solution)/shard_map/all_to_all | solution.py:247
  152.9 0.8 subtract_multiply_fusion
  (39 shorter events, 2.8 us)
Async XLA Ops:
  2.4 31.4 %copy-start.2 = (f32[192,256]{1,0:T(8,128)S(1)}, f32[192,256]{1,0:T(8,128)}, u32[]{:S(2)}) copy-start(f32[192,256]{1,0:T(8,128)} %param.2) | copy-start | bytes 589828
  33.7 7.1 %copy-start = (f32[8,200,256]{2,1,0:T(8,128)}, f32[8,200,256]{2,1,0:T(8,128)S(1)}, u32[]{:S(2)}) copy-start(f32[8,200,256]{2,1,0:T(8,128)S(1)} %all_to_all.30.own_ref) | copy-start | bytes 4915204
  33.7 7.1 %collective-permute-start = (f32[1600,256]{1,0:T(8,128)S(1)}, f32[1600,256]{1,0:T(8,128)}, u32[]{:S(2)}, u32[]{:S(2)}) collective-permute-start(f32[1600,256]{1,0:T(8,128)S(1)} %bitcast.15), channel_id=1, source_target_pairs={{0,1},{1,0},{2,3},{3,2},{4,5},{5,4},{6,7},{7,6},{8,9},{9,8},{10,11... | collective-permute-start | bytes 4915208 | tf_op jit(solution)/shard_map/ppermute | solution.py:218
  35.1 29.7 %all-to-all-start = ((f32[8,192,256]{2,1,0:T(8,128)}), f32[8,192,256]{2,1,0:T(8,128)S(1)}, u32[]{:S(2)}, u32[]{:S(2)}) async-start(f32[8,192,256]{2,1,0:T(8,128)} %broadcast_in_dim.18), calls=%async_computation | async-start | bytes 3145728 | tf_op jit(solution)/shard_map/all_to_all | solution.py:213
  64.8 1.2 copy-start.1
  123.6 28.5 %all-to-all-start.3 = ((f32[8,200,256]{2,1,0:T(8,128)}), f32[8,200,256]{2,1,0:T(8,128)S(1)}, u32[]{:S(2)}, u32[]{:S(2)}) async-start(f32[8,200,256]{2,1,0:T(8,128)} %shard_map.42), calls=%async_computation.3 | async-start | bytes 3276800 | tf_op jit(solution)/shard_map/all_to_all | solution.py:247

commit v2 on v1

v2 whole, which is shorter than its diff:
```python
import functools

import jax
import jax.numpy as jnp
from jax import lax
from jax.experimental import pallas as pl
from jax.experimental.pallas import tpu as pltpu
from jax.sharding import Mesh, PartitionSpec as P

f32, bf16 = jnp.float32, jnp.bfloat16
PER = 192
D = 256
VIEWS = 24576
C_BLOCKS = 8
R_BLOCKS = 16
C = C_BLOCKS * PER
R = R_BLOCKS * PER
SPAN = 768
STEPS = R // SPAN
LANES = 256
BLOCK = 200
PAIR = PER + BLOCK
TEMPERATURE = 0.1
LOG2E = 1.4426950408889634
LN2 = 0.6931471805599453
NT = (((1,), (1,)), ((), ()))
ROW = ("y", "zl")
COL = ("x", "zh", "core")
ALL = ROW + COL


def unit(rows):
    return rows * lax.rsqrt(jnp.sum(rows * rows, axis=-1, keepdims=True) + 1e-06)


def halves(a):
    hi = a.astype(bf16)
    return hi, (a - hi.astype(f32)).astype(bf16)


def places():
    y, zl, x, zh, core = (lax.axis_index(a) for a in ALL)
    found = []
    for dz in (0, 1):
        for dy in (0, -1, 1, 2):
            found.append((y + 4 + dy) % 4 * 2 + (zl + dz) % 2)
    for dx in (0, -1, 1, 2):
        for dcore in (0, 1):
            for dz in (0, 1):
                found.append(((x + 4 + dx) % 4 * 2 + (zh + dz) % 2) * 2 + (core + dcore) % 2)
    return found + [(x * 2 + zh) * 2 + core]


def score_kernel(
    c0_ref, c1_ref, c2_ref, c3z_ref, c3a_ref,
    r0_ref, r1_ref, r2_ref, r3z_ref, r3b_ref,
    s0_ref, s1_ref, s2_ref, s3z_ref, s3b_ref,
    e_ref, zr_ref, partner_ref, send_ref,
    a_ref, b_ref, cid_ref, cacc_ref, pacc_ref, rsum_ref, rows_ref,
):
    place = places()
    k = pl.program_id(0)

    @pl.when(k == 0)
    def _():
        cacc_ref[...] = jnp.zeros_like(cacc_ref)
        pacc_ref[...] = jnp.zeros_like(pacc_ref)
        parts = [ref[PER : 2 * PER, :] for ref in (c0_ref, c1_ref, c2_ref)] + [c3z_ref[...]]
        parts += [ref[0:PER, :] for ref in (c0_ref, c1_ref, c2_ref)] + [c3a_ref[...]]
        for s, part in enumerate(parts):
            rows = pl.ds(s * PER, PER)
            hi, lo = halves(unit(part) * (LOG2E / TEMPERATURE))
            a_ref[rows, 0:D] = hi
            a_ref[rows, D : 2 * D] = lo
            a_ref[rows, 2 * D : 3 * D] = hi
            first = (place[s] * R_BLOCKS + place[24]) * PER
            cid_ref[rows, :] = (first + lax.broadcasted_iota(jnp.int32, (PER, 128), 0)).astype(f32)

    def prepare(parts, indices):
        for b in range(4):
            hi, lo = halves(unit(parts[b]))
            rows = pl.ds(b * PER, PER)
            b_ref[rows, 0:D] = hi
            b_ref[rows, D : 2 * D] = hi
            b_ref[rows, 2 * D : 3 * D] = lo
            zr_ref[rows, 0:D] = hi
            zr_ref[rows, D : 2 * D] = lo
            partner_ref[:, b * PER : (b + 1) * PER] = indices[b]

    for step, refs in enumerate(((r0_ref, s0_ref), (r1_ref, s1_ref), (r2_ref, s2_ref))):

        @pl.when(k == step)
        def _():
            parts, indices = [], []
            for ref in refs:
                parts += [ref[BLOCK : BLOCK + PER, :], ref[0:PER, :]]
                indices += [ref[PER : PER + 1, 0:PER], ref[PER + 1 : PER + 2, 0:PER]]
            prepare(parts, indices)

    @pl.when(k == STEPS - 1)
    def _():
        parts, indices = [], []
        for z, b in ((r3z_ref, r3b_ref), (s3z_ref, s3b_ref)):
            parts += [z[BLOCK - PER : BLOCK, :], b[0:PER, :]]
            indices += [z[0:1, 0:PER], b[PER + 1 : PER + 2, 0:PER]]
        prepare(parts, indices)

    cid = cid_ref[...]
    for n in range(SPAN // LANES):
        cols = pl.ds(n * LANES, LANES)
        s = lax.dot_general(a_ref[...], b_ref[cols, :], NT, preferred_element_type=f32)
        row_total = None
        for h in range(LANES // 128):
            lane0 = n * LANES + h * 128
            lanes = pl.ds(lane0, 128)
            part = s[:, h * 128 : (h + 1) * 128]
            e = jnp.exp2(part)
            if lane0 < PER:
                i = lax.broadcasted_iota(jnp.int32, (PER, 128), 0)
                j = lax.broadcasted_iota(jnp.int32, (PER, 128), 1) + lane0
                e = jnp.concatenate([jnp.where((i == j) & (k == 0), 0.0, e[:PER]), e[PER:]])
            hit = jnp.where(cid == partner_ref[:, lanes], part, 0.0)
            e_ref[:, lanes] = e
            rsum_ref[k, 0:1, lanes] = jnp.sum(e, axis=0, keepdims=True)
            pacc_ref[...] += jnp.sum(hit.reshape(C // 8, 8, 128), axis=0)
            row_total = e if row_total is None else row_total + e
        cacc_ref[...] += row_total

    @pl.when(k == STEPS - 1)
    def _():
        csum = lax.dot_general(
            jnp.ones((8, 128), f32), cacc_ref[...], NT, precision=lax.Precision.HIGHEST, preferred_element_type=f32
        )
        positives = jnp.full((R_BLOCKS, 256 - PER), jnp.sum(pacc_ref[...]), f32)
        for s in range(R_BLOCKS):
            step, b = divmod(s, 4)
            rows_ref[place[C_BLOCKS + s], 0:1, 0:PER] = rsum_ref[step, 0:1, b * PER : (b + 1) * PER]
        of_rows = jnp.concatenate([rows_ref[c, 0:1, 0:PER] for c in range(R_BLOCKS)])
        for s in range(C_BLOCKS):
            rows = pl.ds(place[s] * R_BLOCKS, R_BLOCKS)
            mine = jnp.broadcast_to(csum[0:1, s * PER : (s + 1) * PER], (R_BLOCKS, PER))
            send_ref[rows, 0, :] = jnp.concatenate([mine, positives, of_rows, positives], axis=1)


def scores(columns, rows, swapped):
    whole = lambda k: (0, 0)
    arrays = (*columns, *rows, *swapped)
    return pl.pallas_call(
        score_kernel,
        grid=(STEPS,),
        in_specs=[pl.BlockSpec(a.shape, whole) for a in arrays],
        out_specs=[
            pl.BlockSpec((C, SPAN), lambda k: (0, k)),
            pl.BlockSpec((SPAN, 2 * D), lambda k: (k, 0)),
            pl.BlockSpec((1, SPAN), lambda k: (0, k)),
            pl.BlockSpec((C_BLOCKS * R_BLOCKS, 1, 512), lambda k: (0, 0, 0)),
        ],
        out_shape=[
            jax.ShapeDtypeStruct((C, R), f32),
            jax.ShapeDtypeStruct((R, 2 * D), bf16),
            jax.ShapeDtypeStruct((1, R), f32),
            jax.ShapeDtypeStruct((C_BLOCKS * R_BLOCKS, 1, 512), f32),
        ],
        scratch_shapes=[
            pltpu.VMEM((C, 3 * D), bf16),
            pltpu.VMEM((SPAN, 3 * D), bf16),
            pltpu.VMEM((C, 128), f32),
            pltpu.VMEM((C, 128), f32),
            pltpu.VMEM((8, 128), f32),
            pltpu.VMEM((STEPS, 8, SPAN), f32),
            pltpu.VMEM((R_BLOCKS, 8, 256), f32),
        ],
        compiler_params=pltpu.CompilerParams(vmem_limit_bytes=58 << 20),
    )(*arrays)


def gradient_kernel(group, sums_ref, e_ref, z_ref, partner_ref, uc_in_ref, ur_in_ref, *refs):
    first = uc_in_ref is None
    out_refs, refs = refs[:4], refs[4:]
    if first:
        uc_ref, ur_ref, logs_ref, acc_ref, total_ref = refs
    else:
        (acc_ref,) = refs
        uc_ref, ur_ref, logs_ref = uc_in_ref, ur_in_ref, sums_ref
    place = places()
    k = pl.program_id(0)
    half = 4 * PER

    @pl.when(k == 0)
    def _():
        acc_ref[...] = jnp.zeros_like(acc_ref)
        if first:
            total = sums_ref[0:R_BLOCKS, 0, :]
            for r in range(1, C_BLOCKS):
                total = total + sums_ref[r * R_BLOCKS : (r + 1) * R_BLOCKS, 0, :]
            for c in range(R_BLOCKS):
                total_ref[c, 0:1, :] = total[c : c + 1, 0:256]
            logs = jnp.sum(jnp.log(total[:, 0:PER]))
            positives = jnp.sum(total[:, PER : PER + 1]) * LN2
            logs_ref[...] = jnp.full(logs_ref.shape, logs - positives / C_BLOCKS, f32)
            for s in range(R_BLOCKS):
                step, b = divmod(s, 4)
                found = total_ref[place[C_BLOCKS + s], 0:1, 0:PER]
                ur_ref[step, :, b * PER : (b + 1) * PER] = 1.0 / found
            for s in range(C_BLOCKS):
                mine = sums_ref[pl.ds(place[s] * R_BLOCKS, R_BLOCKS), 0, 256 : 256 + PER]
                found = 1.0 / jnp.sum(mine, axis=0, keepdims=True)
                uc_ref[s * PER : (s + 1) * PER, :] = jnp.broadcast_to(found, (128, PER)).T

    uc = uc_ref[group * half : (group + 1) * half, :]
    ids = lax.broadcasted_iota(jnp.int32, (half, 128), 0)
    firsts = [(place[4 * group + i] * R_BLOCKS + place[24]) * PER - i * PER for i in range(4)]
    ids = jnp.concatenate([ids[i * PER : (i + 1) * PER] + firsts[i] for i in range(4)]).astype(f32)
    total = None
    for c in range(0, SPAN, 256):
        his, los = [], []
        for h in range(c, c + 256, 128):
            lanes = pl.ds(h, 128)
            g = e_ref[:, lanes] * (uc + ur_ref[k, :, lanes])
            g = g - jnp.where(ids == partner_ref[:, lanes], 2.0, 0.0)
            hi, lo = halves(g)
            his.append(hi)
            los.append(lo)
        hi, lo = jnp.concatenate(his, axis=1), jnp.concatenate(los, axis=1)
        rows = pl.ds(c, 256)
        both = jnp.dot(jnp.concatenate([hi, lo]), z_ref[rows, 0:D], preferred_element_type=f32)
        rest = jnp.dot(hi, z_ref[rows, D : 2 * D], preferred_element_type=f32)
        part = both[:half] + (both[half:] + rest)
        total = part if total is None else total + part
    acc_ref[...] += total

    @pl.when(k == STEPS - 1)
    def _():
        for i, out_ref in enumerate(out_refs):
            out_ref[0:PER, :] = acc_ref[i * PER : (i + 1) * PER, :]
            out_ref[PER:BLOCK, :] = jnp.broadcast_to(logs_ref[...], (BLOCK - PER, D))


def gradients(group, sums, e, z, partner, weights=None):
    half = 4 * PER
    first = weights is None
    vmem = pl.BlockSpec(memory_space=pltpu.VMEM)
    blocks = [jax.ShapeDtypeStruct((BLOCK, D), f32)] * 4
    if first:
        kernel = lambda s, e, z, i, *refs: gradient_kernel(group, s, e, z, i, None, None, *refs)
        given = ()
        made = [
            jax.ShapeDtypeStruct((C, 128), f32),
            jax.ShapeDtypeStruct((STEPS, 1, SPAN), f32),
            jax.ShapeDtypeStruct((1, D), f32),
        ]
        scratch = [pltpu.VMEM((R_BLOCKS, 8, 256), f32)]
    else:
        kernel = functools.partial(gradient_kernel, group)
        given, made, scratch = weights, [], []
    return pl.pallas_call(
        kernel,
        grid=(STEPS,),
        in_specs=[
            vmem,
            pl.BlockSpec((half, SPAN), lambda k: (group, k)),
            pl.BlockSpec((SPAN, 2 * D), lambda k: (k, 0)),
            pl.BlockSpec((1, SPAN), lambda k: (0, k)),
        ]
        + [vmem] * len(given),
        out_specs=[vmem] * (4 + len(made)),
        out_shape=blocks + made,
        scratch_shapes=[pltpu.VMEM((half, D), f32)] + scratch,
        compiler_params=pltpu.CompilerParams(vmem_limit_bytes=40 << 20),
        cost_estimate=pl.CostEstimate(flops=2 * 3 * half * R * D, bytes_accessed=4 * half * R, transcendentals=0),
    )(sums, e, z, partner, *given)


SWAP = [(0, 1), (1, 0)]
UP = [(i, (i + 1) % 4) for i in range(4)]
DOWN = [(i, (i + 3) % 4) for i in range(4)]


def over_y(terms):
    here, down, up, across = terms
    across = lax.ppermute(across, "y", [(i, (i + 2) % 4) for i in range(4)])
    down = lax.ppermute(down, "y", DOWN)
    up = lax.ppermute(up, "y", UP)
    return here + down + up + across


def shards(projections, partner):
    index = jnp.pad(partner.astype(f32)[None], ((0, 7), (0, D - PER)))
    index, z = lax.optimization_barrier((index, projections))
    index_b = lax.ppermute(index, "zh", SWAP)
    b = lax.ppermute(z, "zh", SWAP)
    a = lax.ppermute(z, "zl", SWAP)
    r0 = jnp.concatenate([b, index[0:1], index_b[0:1], jnp.zeros((6, D), f32), z])
    c0 = jnp.concatenate([a, z])
    c1, c2 = lax.ppermute(c0, "y", UP), lax.ppermute(c0, "y", DOWN)
    r1, r2 = lax.ppermute(r0, "x", UP), lax.ppermute(r0, "x", DOWN)
    c3z, c3a = lax.ppermute(c1[PER:], "y", UP), lax.ppermute(c2[:PER], "y", DOWN)
    r3z, r3b = lax.ppermute(r1[PER:], "x", UP), lax.ppermute(r2[:BLOCK], "x", DOWN)
    s0 = lax.ppermute(r0, "core", SWAP)
    r1, r2, r3z, r3b, c3z, c3a = lax.optimization_barrier((r1, r2, r3z, r3b, c3z, c3a))
    rows = (r0, r1, r2, r3z, r3b)
    swapped = [s0] + [lax.ppermute(r, "core", SWAP) for r in rows[1:]]

    e, zr, partners, sums = scores((c0, c1, c2, c3z, c3a), rows, swapped)
    sums = lax.all_to_all(sums, ALL, 0, 0, tiled=True)
    e, zr, partners = (pltpu.with_memory_space_constraint(v, pltpu.HBM) for v in (e, zr, partners))
    *other, uc, ur, logs = gradients(1, sums, e, zr, partners)
    other = over_y(other)
    same = over_y(gradients(0, logs, e, zr, partners, (uc, ur)))
    terms = same + lax.ppermute(other, "zl", SWAP)

    mean_objective = terms[PER, 0] / VIEWS
    scale = lax.rsqrt(jnp.sum(z * z, axis=-1, keepdims=True) + 1e-06)
    z = z * scale
    dz = terms[:PER] / TEMPERATURE
    grad = (dz - z * jnp.sum(z * dz, axis=-1, keepdims=True)) * scale
    return mean_objective, grad


def solution(mesh):
    fine = Mesh(mesh.devices.reshape(4, 2, 4, 2, 2), ALL)
    placed = (P(ALL, None), P(ALL))
    return jax.shard_map(
        shards, mesh=fine, in_specs=placed, out_specs=(P(), P(ALL, None)), check_vma=False
    )
```

time: 156 us -> 117 us (0.75)
  blocking collectives: 46.2 us -> 18.3 us
  starting transfers between devices: 8.51 us -> 29.3 us
  waiting for transfers between devices: 45.9 us -> 27.6 us
  local copies, waits for them, and re-layouts: 10.1 us -> 3.08 us
  other arithmetic: 7.11 us -> 2.87 us
  Pallas kernels: 34.4 us -> 32.8 us
    all_to_all x2 -> x0, waiting for transfers between devices: 45.9 us -> none  [the longest x1 23.5 us: shards(): lax.all_to_all(terms.reshape(C_BLOCKS * BLOCK, D), ROW, 0, 0, tiled=True)]
    ppermute x1 -> x23, starting transfers between devices: 0.01 us -> 29.3 us  [the longest x1 3.96 us: shards(): b = lax.ppermute(z, 'zh', SWAP)]
    all_to_all x2 -> x1, blocking collectives: 46.2 us -> 18.3 us  [shards(): sums = lax.all_to_all(sums, ALL, 0, 0, tiled=True)]
    ppermute x1 -> x23, waiting for transfers between devices: 0.01 us -> 27.6 us  [the longest x1 7.32 us: shards(): index_b = lax.ppermute(index, 'zh', SWAP)]
    all_to_all x2 -> x0, starting transfers between devices: 8.51 us -> none  [the longest x1 4.93 us: shards(): xc = lax.all_to_all(xc, ROW, 0, 0, tiled=True).reshape(C_BLOCKS, PER, D)]
    broadcast_in_dim x8 -> x1, local copies, waits for them, and re-layouts: 3.4 us -> 0.01 us  [shards(): jnp.zeros((6, D), f32)]
    pallas_call x2 -> x3, Pallas kernels: 34.4 us -> 32.8 us  [the longest x1 17 us: scores(): pl.pallas_call(score_kernel, grid=(STEPS,), in_specs=[pl.BlockSpec(a.shap...]
  transfers between devices with their start and end apart: 3 -> 23, of which waited for: 2 -> 8; matrix products, arithmetic and copies ran while one was open for 3% -> 2% of each run, Pallas kernels for 0% -> 7%
where the time goes in v2:
time: 117 us
  Pallas kernels  32.8 us (28%)
  starting transfers between devices  29.3 us (25%)
  waiting for transfers between devices  27.6 us (24%)
  blocking collectives  18.3 us (16%)
  local copies, waits for them, and re-layouts  3.08 us (3%)
  other arithmetic  2.87 us (2%)
  between operations  2.67 us (2%)
    all_to_all x1, blocking collectives, shards(): sums = lax.all_to_all(sums, ALL, 0, 0, tiled=True)  18.3 us
    pallas_call x1, Pallas kernels, scores(): pl.pallas_call(score_kernel, grid=(STEPS,), in_specs=[pl.BlockSpec(a.shap...  17 us
    pallas_call x2, Pallas kernels, gradients(): pl.pallas_call(kernel, grid=(STEPS,), in_specs=[vmem, pl.BlockSpec((half,...  15.8 us
    ppermute x1, waiting for transfers between devices, shards(): index_b = lax.ppermute(index, 'zh', SWAP)  7.32 us
    ppermute x2, waiting for transfers between devices, over_y(): down = lax.ppermute(down, 'y', DOWN)  4.67 us
    ppermute x1, starting transfers between devices, shards(): b = lax.ppermute(z, 'zh', SWAP)  3.96 us
    ppermute x2, starting transfers between devices, over_y(): down = lax.ppermute(down, 'y', DOWN)  3.87 us
    ppermute x1, waiting for transfers between devices, shards(): lax.ppermute(c1[PER:], 'y', UP)  3.78 us
  transfers between devices with their start and end apart: 23, of which 8 were waited for; matrix products, arithmetic and copies ran while one was open for 2% of the time, Pallas kernels for 7%

profile of v2, /device:TPU:0, one launch (start us, length us, event | category | flops | bytes accessed | tf_op | source)
XLA Modules:
  0.0 116.6 jit_solution(10502953268656039231)
XLA Ops:
  1.3 4.0 %collective-permute-start.3 = (f32[192,256]{1,0:T(8,128)}, f32[192,256]{1,0:T(8,128)S(1)}, u32[]{:S(2)}, u32[]{:S(2)}) collective-permute-start(f32[192,256]{1,0:T(8,128)} %param.2), channel_id=1, source_target_pairs={{0,2},{2,0},{1,3},{3,1},{4,6},{6,4},{5,7},{7,5},{8,10},{10,8},{9,1... | collective-permute-start | bytes 589832 | tf_op jit(solution)/shard_map/ppermute | solution.py:291
  5.3 1.0 collective-permute-start
  6.3 1.2 collective-permute-start.4
  7.5 7.3 %collective-permute-done.4 = f32[8,256]{1,0:T(8,128)S(1)} collective-permute-done((f32[8,256]{1,0:T(8,128)S(1)}, f32[8,256]{1,0:T(8,128)S(1)}, u32[]{:S(2)}, u32[]{:S(2)}) %collective-permute-start.4) | collective-permute-done | bytes 8224 | tf_op jit(solution)/shard_map/ppermute | solution.py:290
  14.8 1.0 concatenate.7.r0_ref
  15.8 2.8 %collective-permute-start.6 = (f32[392,256]{1,0:T(8,128)S(1)}, f32[392,256]{1,0:T(8,128)S(1)}, u32[]{:S(2)}, u32[]{:S(2)}) collective-permute-start(f32[392,256]{1,0:T(8,128)S(1)} %concatenate.7.r0_ref), channel_id=1, source_target_pairs={{0,12},{4,0},{8,4},{12,8},{1,13},{5,1},{9,5},{13,9},{2,14},{6,2},{... | collective-permute-start | bytes 1204232 | tf_op jit(solution)/shard_map/ppermute | solution.py:296
  18.6 1.0 multiply_reduce_fusion.1
  19.7 3.1 %collective-permute-start.2 = (f32[384,256]{1,0:T(8,128)S(1)}, f32[384,256]{1,0:T(8,128)S(1)}, u32[]{:S(2)}, u32[]{:S(2)}) collective-permute-start(f32[384,256]{1,0:T(8,128)S(1)} %get-tuple-element.49.c0_ref), channel_id=1, source_target_pairs={{0,96},{32,0},{64,32},{96,64},{1,97},{33,1},{65,33},{97,65},{2,98}... | collective-permute-start | bytes 1179656 | tf_op jit(solution)/shard_map/ppermute | solution.py:295
  22.8 3.5 %collective-permute-done.6.r2_ref = f32[392,256]{1,0:T(8,128)S(1)} collective-permute-done((f32[392,256]{1,0:T(8,128)S(1)}, f32[392,256]{1,0:T(8,128)S(1)}, u32[]{:S(2)}, u32[]{:S(2)}) %collective-permute-start.6) | collective-permute-done | bytes 401440 | tf_op jit(solution)/shard_map/ppermute | solution.py:296
  26.3 3.8 %collective-permute-start.8 = (f32[200,256]{1,0:T(8,128)S(1)}, f32[200,256]{1,0:T(8,128)S(1)}, u32[]{:S(2)}, u32[]{:S(2)}) collective-permute-start(f32[200,256]{1,0:T(8,128)S(1)} %slice.34), channel_id=1, source_target_pairs={{0,12},{4,0},{8,4},{12,8},{1,13},{5,1},{9,5},{13,9},{2,14},{6,2},{... | collective-permute-start | bytes 614408 | tf_op jit(solution)/shard_map/ppermute | solution.py:298
  30.2 3.6 %collective-permute-start.10 = (f32[192,256]{1,0:T(8,128)S(1)}, f32[192,256]{1,0:T(8,128)S(1)}, u32[]{:S(2)}, u32[]{:S(2)}) collective-permute-start(f32[192,256]{1,0:T(8,128)S(1)} %slice.36), channel_id=1, source_target_pairs={{0,96},{32,0},{64,32},{96,64},{1,97},{33,1},{65,33},{97,65},{2,98}... | collective-permute-start | bytes 589832 | tf_op jit(solution)/shard_map/ppermute | solution.py:297
  34.0 3.0 %collective-permute-done.10.c3a_ref = f32[192,256]{1,0:T(8,128)S(1)} collective-permute-done((f32[192,256]{1,0:T(8,128)S(1)}, f32[192,256]{1,0:T(8,128)S(1)}, u32[]{:S(2)}, u32[]{:S(2)}) %collective-permute-start.10) | collective-permute-done | bytes 196640 | tf_op jit(solution)/shard_map/ppermute | solution.py:297
  37.0 3.8 %collective-permute-done.9.c3z_ref = f32[192,256]{1,0:T(8,128)S(1)} collective-permute-done((f32[192,256]{1,0:T(8,128)S(1)}, f32[192,256]{1,0:T(8,128)S(1)}, u32[]{:S(2)}, u32[]{:S(2)}) %collective-permute-start.9) | collective-permute-done | bytes 196640 | tf_op jit(solution)/shard_map/ppermute | solution.py:297
  41.9 1.6 %collective-permute-done.14.s3z_ref = f32[200,256]{1,0:T(8,128)S(1)} collective-permute-done((f32[200,256]{1,0:T(8,128)S(1)}, f32[200,256]{1,0:T(8,128)S(1)}, u32[]{:S(2)}, u32[]{:S(2)}) %collective-permute-start.14) | collective-permute-done | bytes 204832 | tf_op jit(solution)/shard_map/ppermute | solution.py:302
  45.3 17.0 %shard_map.41 = (f32[1536,3072]{1,0:T(8,128)}, bf16[3072,512]{1,0:T(8,128)(2,1)}, f32[1,3072]{1,0:T(1,128)}, f32[128,1,512]{2,1,0:T(1,128)}) custom-call(f32[384,256]{1,0:T(8,128)} %copy-done.6, f32[384,256]{1,0:T(8,128)} %copy-done.5, f32[384,256]{1,0:T(8,128)} %copy-done.4, f32[192,256]{1,0:T(8,128)} %copy-done.15, f32[192,256]{1,0:T(8,128)} %copy-done.14, ...), custom_call_target="tpu_custom_call" | custom-call | tf_op jit(solution)/shard_map/pallas_call | solution.py:148
  62.3 18.3 %all_to_all.5.s = f32[128,1,512]{2,1,0:T(1,128)S(1)} all-to-all(f32[128,1,512]{2,1,0:T(1,128)} %get-tuple-element.33), channel_id=1, replica_groups=mesh['y'=4,'zl'=2,'x'=4,'zh'=2,'core'=2] {'y','zl','x','zh','core'}, dimensions={0} | all-to-all | bytes 524288 | tf_op jit(solution)/shard_map/all_to_all | solution.py:305
  80.6 8.1 %shard_map.42 = (f32[200,256]{1,0:T(8,128)S(1)}, f32[200,256]{1,0:T(8,128)S(1)}, f32[200,256]{1,0:T(8,128)S(1)}, f32[200,256]{1,0:T(8,128)S(1)}, f32[1536,128]{1...) custom-call(f32[128,1,512]{2,1,0:T(1,128)S(1)} %all_to_all.5.s, f32[1536,3072]{1,0:T(8,128)} %get-tuple-element.34.e.e_ref, ...), custom_call_target="tpu_custom_call" | custom-call | flops 3623878656 | bytes 9437184 | tf_op jit(solution)/shard_map/pallas_call | solution.py:256
  88.8 1.2 %collective-permute-start.19 = (f32[200,256]{1,0:T(8,128)S(1)}, f32[200,256]{1,0:T(8,128)S(1)}, u32[]{:S(2)}, u32[]{:S(2)}) collective-permute-start(f32[200,256]{1,0:T(8,128)S(1)} %get-tuple-element.45), channel_id=1, source_target_pairs={{0,96},{32,0},{64,32},{96,64},{1,97},{33,1},{65,33},{97,65},{2,98}... | collective-permute-start | bytes 614408 | tf_op jit(solution)/shard_map/ppermute | solution.py:282
  89.9 0.9 collective-permute-start.20
  91.5 7.7 %shard_map.43 = (f32[200,256]{1,0:T(8,128)S(1)}, f32[200,256]{1,0:T(8,128)S(1)}, f32[200,256]{1,0:T(8,128)S(1)}, f32[200,256]{1,0:T(8,128)S(1)}) custom-call(f32[1,256]{1,0:T(1,128)S(1)} %get-tuple-element.37.sums_ref, f32[1536,3072]{1,0:T(8,128)} %get-tuple-element.34.e.e_ref, bf16[3072,512]{1,0:T(8,128)(2,1)} %get-tuple-element.35.z.z_ref, ...), custom_call_target="tpu_custom_call" | custom-call | flops 3623878656 | bytes 9437184 | tf_op jit(solution)/shard_map/pallas_call | solution.py:256
  99.2 2.7 %collective-permute-start.16 = (f32[200,256]{1,0:T(8,128)S(1)}, f32[200,256]{1,0:T(8,128)S(1)}, u32[]{:S(2)}, u32[]{:S(2)}) collective-permute-start(f32[200,256]{1,0:T(8,128)S(1)} %get-tuple-element.41), channel_id=1, source_target_pairs={{0,96},{32,0},{64,32},{96,64},{1,97},{33,1},{65,33},{97,65},{2,98}... | collective-permute-start | bytes 614408 | tf_op jit(solution)/shard_map/ppermute | solution.py:282
  101.9 2.3 %collective-permute-start.18 = (f32[200,256]{1,0:T(8,128)S(1)}, f32[200,256]{1,0:T(8,128)S(1)}, u32[]{:S(2)}, u32[]{:S(2)}) collective-permute-start(f32[200,256]{1,0:T(8,128)S(1)} %get-tuple-element.43), channel_id=1, source_target_pairs={{0,64},{32,96},{64,0},{96,32},{1,65},{33,97},{65,1},{97,33},{2,66}... | collective-permute-start | bytes 614408 | tf_op jit(solution)/shard_map/ppermute | solution.py:281
  105.1 4.7 %collective-permute-done.16 = f32[200,256]{1,0:T(8,128)S(1)} collective-permute-done((f32[200,256]{1,0:T(8,128)S(1)}, f32[200,256]{1,0:T(8,128)S(1)}, u32[]{:S(2)}, u32[]{:S(2)}) %collective-permute-start.16) | collective-permute-done | bytes 204832 | tf_op jit(solution)/shard_map/ppermute | solution.py:282
  109.8 3.4 %collective-permute-done.17 = f32[200,256]{1,0:T(8,128)S(1)} collective-permute-done((f32[200,256]{1,0:T(8,128)S(1)}, f32[200,256]{1,0:T(8,128)S(1)}, u32[]{:S(2)}, u32[]{:S(2)}) %collective-permute-start.17) | collective-permute-done | bytes 204832 | tf_op jit(solution)/shard_map/ppermute | solution.py:283
  (76 shorter events, 7.2 us)
Async XLA Ops:
  1.3 13.5 %collective-permute-start.3 = (f32[192,256]{1,0:T(8,128)}, f32[192,256]{1,0:T(8,128)S(1)}, u32[]{:S(2)}, u32[]{:S(2)}) collective-permute-start(f32[192,256]{1,0:T(8,128)} %param.2), channel_id=1, source_target_pairs={{0,2},{2,0},{1,3},{3,1},{4,6},{6,4},{5,7},{7,5},{8,10},{10,8},{9,1... | collective-permute-start | bytes 589832 | tf_op jit(solution)/shard_map/ppermute | solution.py:291
  5.3 13.3 %collective-permute-start = (f32[192,256]{1,0:T(8,128)}, f32[192,256]{1,0:T(8,128)S(1)}, u32[]{:S(2)}, u32[]{:S(2)}) collective-permute-start(f32[192,256]{1,0:T(8,128)} %param.2), channel_id=1, source_target_pairs={{0,16},{16,0},{1,17},{17,1},{2,18},{18,2},{3,19},{19,3},{4,20},{20... | collective-permute-start | bytes 589832 | tf_op jit(solution)/shard_map/ppermute | solution.py:292
  6.3 8.5 %collective-permute-start.4 = (f32[8,256]{1,0:T(8,128)S(1)}, f32[8,256]{1,0:T(8,128)S(1)}, u32[]{:S(2)}, u32[]{:S(2)}) collective-permute-start(f32[8,256]{1,0:T(8,128)S(1)} %pad.4), channel_id=1, source_target_pairs={{0,2},{2,0},{1,3},{3,1},{4,6},{6,4},{5,7},{7,5},{8,10},{10,8},{9,1... | collective-permute-start | bytes 24584 | tf_op jit(solution)/shard_map/ppermute | solution.py:290
  15.8 10.5 %collective-permute-start.6 = (f32[392,256]{1,0:T(8,128)S(1)}, f32[392,256]{1,0:T(8,128)S(1)}, u32[]{:S(2)}, u32[]{:S(2)}) collective-permute-start(f32[392,256]{1,0:T(8,128)S(1)} %concatenate.7.r0_ref), channel_id=1, source_target_pairs={{0,12},{4,0},{8,4},{12,8},{1,13},{5,1},{9,5},{13,9},{2,14},{6,2},{... | collective-permute-start | bytes 1204232 | tf_op jit(solution)/shard_map/ppermute | solution.py:296
  18.6 11.5 %collective-permute-start.5 = (f32[392,256]{1,0:T(8,128)S(1)}, f32[392,256]{1,0:T(8,128)S(1)}, u32[]{:S(2)}, u32[]{:S(2)}) collective-permute-start(f32[392,256]{1,0:T(8,128)S(1)} %concatenate.7.r0_ref), channel_id=1, source_target_pairs={{0,4},{4,8},{8,12},{12,0},{1,5},{5,9},{9,13},{13,1},{2,6},{6,10},{... | collective-permute-start | bytes 1204232 | tf_op jit(solution)/shard_map/ppermute | solution.py:296
  19.7 10.5 %collective-permute-start.2 = (f32[384,256]{1,0:T(8,128)S(1)}, f32[384,256]{1,0:T(8,128)S(1)}, u32[]{:S(2)}, u32[]{:S(2)}) collective-permute-start(f32[384,256]{1,0:T(8,128)S(1)} %get-tuple-element.49.c0_ref), channel_id=1, source_target_pairs={{0,96},{32,0},{64,32},{96,64},{1,97},{33,1},{65,33},{97,65},{2,98}... | collective-permute-start | bytes 1179656 | tf_op jit(solution)/shard_map/ppermute | solution.py:295
  22.8 11.0 %collective-permute-start.1 = (f32[384,256]{1,0:T(8,128)S(1)}, f32[384,256]{1,0:T(8,128)S(1)}, u32[]{:S(2)}, u32[]{:S(2)}) collective-permute-start(f32[384,256]{1,0:T(8,128)S(1)} %get-tuple-element.49.c0_ref), channel_id=1, source_target_pairs={{0,32},{32,64},{64,96},{96,0},{1,33},{33,65},{65,97},{97,1},{2,34}... | collective-permute-start | bytes 1179656 | tf_op jit(solution)/shard_map/ppermute | solution.py:295
  26.3 14.4 %collective-permute-start.8 = (f32[200,256]{1,0:T(8,128)S(1)}, f32[200,256]{1,0:T(8,128)S(1)}, u32[]{:S(2)}, u32[]{:S(2)}) collective-permute-start(f32[200,256]{1,0:T(8,128)S(1)} %slice.34), channel_id=1, source_target_pairs={{0,12},{4,0},{8,4},{12,8},{1,13},{5,1},{9,5},{13,9},{2,14},{6,2},{... | collective-permute-start | bytes 614408 | tf_op jit(solution)/shard_map/ppermute | solution.py:298
  30.1 10.7 %collective-permute-start.7 = (f32[200,256]{1,0:T(8,128)S(1)}, f32[200,256]{1,0:T(8,128)S(1)}, u32[]{:S(2)}, u32[]{:S(2)}) collective-permute-start(f32[200,256]{1,0:T(8,128)S(1)} %slice.33), channel_id=1, source_target_pairs={{0,4},{4,8},{8,12},{12,0},{1,5},{5,9},{9,13},{13,1},{2,6},{6,10},{... | collective-permute-start | bytes 614408 | tf_op jit(solution)/shard_map/ppermute | solution.py:298
  30.2 6.7 %collective-permute-start.10 = (f32[192,256]{1,0:T(8,128)S(1)}, f32[192,256]{1,0:T(8,128)S(1)}, u32[]{:S(2)}, u32[]{:S(2)}) collective-permute-start(f32[192,256]{1,0:T(8,128)S(1)} %slice.36), channel_id=1, source_target_pairs={{0,96},{32,0},{64,32},{96,64},{1,97},{33,1},{65,33},{97,65},{2,98}... | collective-permute-start | bytes 589832 | tf_op jit(solution)/shard_map/ppermute | solution.py:297
  33.8 6.9 %collective-permute-start.9 = (f32[192,256]{1,0:T(8,128)S(1)}, f32[192,256]{1,0:T(8,128)S(1)}, u32[]{:S(2)}, u32[]{:S(2)}) collective-permute-start(f32[192,256]{1,0:T(8,128)S(1)} %slice.35), channel_id=1, source_target_pairs={{0,32},{32,64},{64,96},{96,0},{1,33},{33,65},{65,97},{97,1},{2,34}... | collective-permute-start | bytes 589832 | tf_op jit(solution)/shard_map/ppermute | solution.py:297
  33.9 8.0 %collective-permute-start.11 = (f32[392,256]{1,0:T(8,128)S(1)}, f32[392,256]{1,0:T(8,128)S(1)}, u32[]{:S(2)}, u32[]{:S(2)}) collective-permute-start(f32[392,256]{1,0:T(8,128)S(1)} %concatenate.7.r0_ref), channel_id=1, source_target_pairs={{0,1},{1,0},{2,3},{3,2},{4,5},{5,4},{6,7},{7,6},{8,9},{9,8},{10,11... | collective-permute-start | bytes 1204232 | tf_op jit(solution)/shard_map/ppermute | solution.py:299
  40.8 3.0 %collective-permute-start.12 = (f32[392,256]{1,0:T(8,128)S(1)}, f32[392,256]{1,0:T(8,128)S(1)}, u32[]{:S(2)}, u32[]{:S(2)}) collective-permute-start(f32[392,256]{1,0:T(8,128)S(1)} %collective-permute-done.5.r1_ref), channel_id=1, source_target_pairs={{0,1},{1,0},{2,3},{3,2},{4,5},{5,4},{6,7},{7,6},{8,9},{9,8},{10,11... | collective-permute-start | bytes 1204232 | tf_op jit(solution)/shard_map/ppermute | solution.py:302
  40.9 2.9 %collective-permute-start.13 = (f32[392,256]{1,0:T(8,128)S(1)}, f32[392,256]{1,0:T(8,128)S(1)}, u32[]{:S(2)}, u32[]{:S(2)}) collective-permute-start(f32[392,256]{1,0:T(8,128)S(1)} %collective-permute-done.6.r2_ref), channel_id=1, source_target_pairs={{0,1},{1,0},{2,3},{3,2},{4,5},{5,4},{6,7},{7,6},{8,9},{9,8},{10,11... | collective-permute-start | bytes 1204232 | tf_op jit(solution)/shard_map/ppermute | solution.py:302
  41.4 2.1 %collective-permute-start.14 = (f32[200,256]{1,0:T(8,128)S(1)}, f32[200,256]{1,0:T(8,128)S(1)}, u32[]{:S(2)}, u32[]{:S(2)}) collective-permute-start(f32[200,256]{1,0:T(8,128)S(1)} %collective-permute-done.7.r3z_ref), channel_id=1, source_target_pairs={{0,1},{1,0},{2,3},{3,2},{4,5},{5,4},{6,7},{7,6},{8,9},{9,8},{10,11... | collective-permute-start | bytes 614408 | tf_op jit(solution)/shard_map/ppermute | solution.py:302
  41.5 2.3 %collective-permute-start.15 = (f32[200,256]{1,0:T(8,128)S(1)}, f32[200,256]{1,0:T(8,128)S(1)}, u32[]{:S(2)}, u32[]{:S(2)}) collective-permute-start(f32[200,256]{1,0:T(8,128)S(1)} %collective-permute-done.8.r3b_ref), channel_id=1, source_target_pairs={{0,1},{1,0},{2,3},{3,2},{4,5},{5,4},{6,7},{7,6},{8,9},{9,8},{10,11... | collective-permute-start | bytes 614408 | tf_op jit(solution)/shard_map/ppermute | solution.py:302
  80.6 33.2 %copy-start = (f32[192,256]{1,0:T(8,128)S(1)}, f32[192,256]{1,0:T(8,128)}, u32[]{:S(2)}) copy-start(f32[192,256]{1,0:T(8,128)} %param.2) | copy-start | bytes 589828
  88.8 13.1 %collective-permute-start.19 = (f32[200,256]{1,0:T(8,128)S(1)}, f32[200,256]{1,0:T(8,128)S(1)}, u32[]{:S(2)}, u32[]{:S(2)}) collective-permute-start(f32[200,256]{1,0:T(8,128)S(1)} %get-tuple-element.45), channel_id=1, source_target_pairs={{0,96},{32,0},{64,32},{96,64},{1,97},{33,1},{65,33},{97,65},{2,98}... | collective-permute-start | bytes 614408 | tf_op jit(solution)/shard_map/ppermute | solution.py:282
  89.9 14.2 %collective-permute-start.20 = (f32[200,256]{1,0:T(8,128)S(1)}, f32[200,256]{1,0:T(8,128)S(1)}, u32[]{:S(2)}, u32[]{:S(2)}) collective-permute-start(f32[200,256]{1,0:T(8,128)S(1)} %get-tuple-element.46), channel_id=1, source_target_pairs={{0,32},{32,64},{64,96},{96,0},{1,33},{33,65},{65,97},{97,1},{2,34}... | collective-permute-start | bytes 614408 | tf_op jit(solution)/shard_map/ppermute | solution.py:283
  90.9 13.3 %collective-permute-start.21 = (f32[200,256]{1,0:T(8,128)S(1)}, f32[200,256]{1,0:T(8,128)S(1)}, u32[]{:S(2)}, u32[]{:S(2)}) collective-permute-start(f32[200,256]{1,0:T(8,128)S(1)} %get-tuple-element.47), channel_id=1, source_target_pairs={{0,64},{32,96},{64,0},{96,32},{1,65},{33,97},{65,1},{97,33},{2,66}... | collective-permute-start | bytes 614408 | tf_op jit(solution)/shard_map/ppermute | solution.py:281
  99.2 10.6 %collective-permute-start.16 = (f32[200,256]{1,0:T(8,128)S(1)}, f32[200,256]{1,0:T(8,128)S(1)}, u32[]{:S(2)}, u32[]{:S(2)}) collective-permute-start(f32[200,256]{1,0:T(8,128)S(1)} %get-tuple-element.41), channel_id=1, source_target_pairs={{0,96},{32,0},{64,32},{96,64},{1,97},{33,1},{65,33},{97,65},{2,98}... | collective-permute-start | bytes 614408 | tf_op jit(solution)/shard_map/ppermute | solution.py:282
  101.9 11.3 %collective-permute-start.17 = (f32[200,256]{1,0:T(8,128)S(1)}, f32[200,256]{1,0:T(8,128)S(1)}, u32[]{:S(2)}, u32[]{:S(2)}) collective-permute-start(f32[200,256]{1,0:T(8,128)S(1)} %get-tuple-element.42), channel_id=1, source_target_pairs={{0,32},{32,64},{64,96},{96,0},{1,33},{33,65},{65,97},{97,1},{2,34}... | collective-permute-start | bytes 614408 | tf_op jit(solution)/shard_map/ppermute | solution.py:283
  101.9 11.3 %collective-permute-start.18 = (f32[200,256]{1,0:T(8,128)S(1)}, f32[200,256]{1,0:T(8,128)S(1)}, u32[]{:S(2)}, u32[]{:S(2)}) collective-permute-start(f32[200,256]{1,0:T(8,128)S(1)} %get-tuple-element.43), channel_id=1, source_target_pairs={{0,64},{32,96},{64,0},{96,32},{1,65},{33,97},{65,1},{97,33},{2,66}... | collective-permute-start | bytes 614408 | tf_op jit(solution)/shard_map/ppermute | solution.py:281
  104.2 9.0 %collective-permute-start.22 = (f32[200,256]{1,0:T(8,128)S(1)}, f32[200,256]{1,0:T(8,128)S(1)}, u32[]{:S(2)}, u32[]{:S(2)}) collective-permute-start(f32[200,256]{1,0:T(8,128)S(1)} %add_add_fusion), channel_id=1, source_target_pairs={{0,16},{16,0},{1,17},{17,1},{2,18},{18,2},{3,19},{19,3},{4,20},{20... | collective-permute-start | bytes 614408 | tf_op jit(solution)/shard_map/ppermute | solution.py:310
  (15 other events, 128.0 us)

commit v3 on v2

v3 whole, which is shorter than its diff:
```python
import functools

import jax
import jax.numpy as jnp
from jax import lax
from jax.experimental import pallas as pl
from jax.experimental.pallas import tpu as pltpu
from jax.sharding import Mesh, PartitionSpec as P

f32, bf16 = jnp.float32, jnp.bfloat16
PER = 192
D = 256
VIEWS = 24576
C_BLOCKS = 8
R_BLOCKS = 16
C = C_BLOCKS * PER
R = R_BLOCKS * PER
SPAN = 768
STEPS = R // SPAN
LANES = 256
TILES = SPAN // LANES
BLOCK = 200
PAIR = PER + BLOCK
TEMPERATURE = 0.1
LOG2E = 1.4426950408889634
LN2 = 0.6931471805599453
NT = (((1,), (1,)), ((), ()))
ROW = ("y", "zl")
COL = ("x", "zh", "core")
ALL = ROW + COL


def unit(rows):
    return rows * lax.rsqrt(jnp.sum(rows * rows, axis=-1, keepdims=True) + 1e-06)


def halves(a):
    hi = a.astype(bf16)
    return hi, (a - hi.astype(f32)).astype(bf16)


def places():
    y, zl, x, zh, core = (lax.axis_index(a) for a in ALL)
    found = []
    for dz in (0, 1):
        for dy in (0, -1, 1, 2):
            found.append((y + 4 + dy) % 4 * 2 + (zl + dz) % 2)
    for dx in (0, -1, 1, 2):
        for dcore in (0, 1):
            for dz in (0, 1):
                found.append(((x + 4 + dx) % 4 * 2 + (zh + dz) % 2) * 2 + (core + dcore) % 2)
    return found + [(x * 2 + zh) * 2 + core]


def score_kernel(start, steps, *refs):
    place = places()
    first, last = start == 0, start + steps == STEPS
    if first:
        columns, blocks, refs = refs[:C_BLOCKS], refs[C_BLOCKS : C_BLOCKS + 4], refs[C_BLOCKS + 4 :]
        e_ref, zr_ref, partner_ref, rsum_ref, pos_ref, cacc_ref, a_ref, cid_ref, b_ref = refs
    else:
        blocks, refs = refs[: 4 * steps], refs[4 * steps :]
        a_ref, cid_ref, pos_in_ref, cacc_in_ref = refs[:4]
        refs = refs[7:]
        if last:
            earlier, refs = refs[:start], refs[start:]
            e_ref, zr_ref, partner_ref, send_ref, b_ref, rsum_ref, pos_ref, cacc_ref, rows_ref = refs
        else:
            e_ref, zr_ref, partner_ref, rsum_ref, pos_ref, cacc_ref, b_ref = refs
    j = pl.program_id(0)

    @pl.when(j == 0)
    def _():
        if first:
            cacc_ref[...] = jnp.zeros_like(cacc_ref)
            pos_ref[...] = jnp.zeros_like(pos_ref)
            for s, ref in enumerate(columns):
                rows = pl.ds(s * PER, PER)
                hi, lo = halves(unit(ref[...]) * (LOG2E / TEMPERATURE))
                a_ref[rows, 0:D] = hi
                a_ref[rows, D : 2 * D] = lo
                a_ref[rows, 2 * D : 3 * D] = hi
                start = (place[s] * R_BLOCKS + place[24]) * PER
                cid_ref[rows, :] = (start + lax.broadcasted_iota(jnp.int32, (PER, 128), 0)).astype(f32)
        else:
            cacc_ref[...] = cacc_in_ref[...]
            pos_ref[...] = pos_in_ref[...]

    for step in range(len(blocks) // 4):

        @pl.when(j == step * TILES)
        def _():
            for b, ref in enumerate(blocks[4 * step : 4 * step + 4]):
                hi, lo = halves(unit(ref[0:PER, :]))
                rows = pl.ds(b * PER, PER)
                b_ref[rows, 0:D] = hi
                b_ref[rows, D : 2 * D] = hi
                b_ref[rows, 2 * D : 3 * D] = lo
                zr_ref[rows, 0:D] = hi
                zr_ref[rows, D : 2 * D] = lo
                partner_ref[0, :, b * PER : (b + 1) * PER] = ref[PER : PER + 1, 0:PER]

    cid = cid_ref[...]
    tile = lax.rem(j, TILES) * LANES
    s = lax.dot_general(
        a_ref[...], b_ref[pl.ds(pl.multiple_of(tile, LANES), LANES), :], NT, preferred_element_type=f32
    )
    row_total = None
    for h in range(LANES // 128):
        lanes = pl.ds(pl.multiple_of(tile + h * 128, 128), 128)
        part = s[:, h * 128 : (h + 1) * 128]
        e = jnp.exp2(part)
        if first:
            i = lax.broadcasted_iota(jnp.int32, (PER, 128), 0)
            i2 = lax.broadcasted_iota(jnp.int32, (PER, 128), 1) + h * 128
            e = jnp.concatenate([jnp.where((i == i2) & (j == 0), 0.0, e[:PER]), e[PER:]])
        hit = jnp.where(cid == partner_ref[0, :, lanes], part, 0.0)
        e_ref[0, :, h * 128 : (h + 1) * 128] = e
        rsum_ref[j // TILES, :, lanes] = jnp.sum(e, axis=0, keepdims=True)
        pos_ref[...] += jnp.sum(hit.reshape(C // 8, 8, 128), axis=0)
        row_total = e if row_total is None else row_total + e
    cacc_ref[...] += row_total

    if last:

        @pl.when(j == pl.num_programs(0) - 1)
        def _():
            csum = lax.dot_general(
                jnp.ones((8, 128), f32), cacc_ref[...], NT, precision=lax.Precision.HIGHEST, preferred_element_type=f32
            )
            positives = jnp.full((R_BLOCKS, 256 - PER), jnp.sum(pos_ref[...]), f32)
            for s in range(R_BLOCKS):
                step, b = divmod(s, 4)
                sums = earlier[step][0] if step < start else rsum_ref[step - start]
                rows_ref[place[C_BLOCKS + s], 0:1, 0:PER] = sums[:, b * PER : (b + 1) * PER]
            of_rows = jnp.concatenate([rows_ref[c, 0:1, 0:PER] for c in range(R_BLOCKS)])
            for s in range(C_BLOCKS):
                rows = pl.ds(place[s] * R_BLOCKS, R_BLOCKS)
                mine = jnp.broadcast_to(csum[0:1, s * PER : (s + 1) * PER], (R_BLOCKS, PER))
                send_ref[rows, 0, :] = jnp.concatenate([mine, positives, of_rows, positives], axis=1)


def scores(start, blocks, columns=None, carried=None):
    vmem = pl.BlockSpec(memory_space=pltpu.VMEM)
    steps = len(blocks) // 4
    first, last = start == 0, start + steps == STEPS
    shared = [
        pltpu.HBM((R // LANES, C, LANES), f32),
        pltpu.HBM((R, 2 * D), bf16),
        pltpu.HBM((STEPS, 1, SPAN), f32),
    ]
    shared_specs = [
        pl.BlockSpec((1, C, LANES), lambda j: (start * TILES + j, 0, 0)),
        pl.BlockSpec((SPAN, 2 * D), lambda j: (start + j // TILES, 0)),
        pl.BlockSpec((1, 1, SPAN), lambda j: (start + j // TILES, 0, 0)),
    ]
    sums = [pltpu.VMEM((steps, 1, SPAN), f32), pltpu.VMEM((8, 128), f32), pltpu.VMEM((C, 128), f32)]
    scratch = [pltpu.VMEM((SPAN, 3 * D), bf16)]
    if first:
        given, in_specs, aliases = (*columns, *blocks), [vmem] * (C_BLOCKS + 4), {}
        made = sums + [pltpu.VMEM((C, 3 * D), bf16), pltpu.VMEM((C, 128), f32)]
    else:
        e, zr, partners, rsums, pos, cacc, a, cid = carried
        keep = lambda v: pltpu.with_memory_space_constraint(v, pltpu.VMEM)
        given = (*blocks, *(keep(v) for v in (a, cid, pos, cacc)), e, zr, partners)
        n = len(given) - 3
        in_specs = [vmem] * n + [pl.BlockSpec(memory_space=pl.ANY)] * 3
        aliases = {n: 0, n + 1: 1, n + 2: 2}
        made = sums
        if last:
            given, in_specs = (*given, *(keep(v) for v in rsums)), in_specs + [vmem] * len(rsums)
            made = [jax.ShapeDtypeStruct((C_BLOCKS * R_BLOCKS, 1, 512), f32)]
            scratch += sums + [pltpu.VMEM((R_BLOCKS, 8, 256), f32)]
    size = C * SPAN * steps
    out = pl.pallas_call(
        functools.partial(score_kernel, start, steps),
        grid=(steps * TILES,),
        in_specs=in_specs,
        out_specs=shared_specs + [vmem] * len(made),
        out_shape=shared + made,
        scratch_shapes=scratch,
        input_output_aliases=aliases,
        compiler_params=pltpu.CompilerParams(vmem_limit_bytes=40 << 20),
        cost_estimate=pl.CostEstimate(flops=6 * size * D, bytes_accessed=4 * size, transcendentals=size),
    )(*given)
    if last:
        return out
    e, zr, partners, rsum, pos, cacc = out[:6]
    if first:
        return e, zr, partners, [rsum], pos, cacc, *out[6:]
    return e, zr, partners, [*rsums, rsum], pos, cacc, a, cid


def gradient_kernel(slots, first, sums_ref, *refs):
    count = len(slots)
    e_refs, (z_ref, partner_ref), refs = refs[:count], refs[count : count + 2], refs[count + 2 :]
    if not first:
        (uc_ref, ur_ref), logs_ref, refs = refs[:2], sums_ref, refs[2:]
    out_refs, refs = refs[:count], refs[count:]
    if first:
        uc_ref, ur_ref, logs_ref, acc_ref, total_ref = refs
    else:
        (acc_ref,) = refs
    place = places()
    k = pl.program_id(0)
    rows_here = count * PER

    @pl.when(k == 0)
    def _():
        acc_ref[...] = jnp.zeros_like(acc_ref)
        if first:
            total = sums_ref[0:R_BLOCKS, 0, :]
            for r in range(1, C_BLOCKS):
                total = total + sums_ref[r * R_BLOCKS : (r + 1) * R_BLOCKS, 0, :]
            for c in range(R_BLOCKS):
                total_ref[c, 0:1, :] = total[c : c + 1, 0:256]
            logs = jnp.sum(jnp.log(total[:, 0:PER]))
            positives = jnp.sum(total[:, PER : PER + 1]) * LN2
            logs_ref[...] = jnp.full(logs_ref.shape, logs - positives / C_BLOCKS, f32)
            for s in range(R_BLOCKS):
                step, b = divmod(s, 4)
                found = total_ref[place[C_BLOCKS + s], 0:1, 0:PER]
                ur_ref[step, :, b * PER : (b + 1) * PER] = 1.0 / found
            for s in range(C_BLOCKS):
                mine = sums_ref[pl.ds(place[s] * R_BLOCKS, R_BLOCKS), 0, 256 : 256 + PER]
                found = 1.0 / jnp.sum(mine, axis=0, keepdims=True)
                uc_ref[s * PER : (s + 1) * PER, :] = jnp.broadcast_to(found, (128, PER)).T

    uc = jnp.concatenate([uc_ref[i * PER : (i + 1) * PER, :] for i in slots])
    ids = lax.broadcasted_iota(jnp.int32, (PER, 128), 0)
    ids = jnp.concatenate([ids + (place[i] * R_BLOCKS + place[24]) * PER for i in slots]).astype(f32)
    total = None
    for c in range(0, SPAN, 256):
        his, los = [], []
        for h in range(c, c + 256, 128):
            lanes = pl.ds(h, 128)
            e = jnp.concatenate([e_ref[c // 256, :, h - c : h - c + 128] for e_ref in e_refs])
            g = e * (uc + ur_ref[k, :, lanes])
            g = g - jnp.where(ids == partner_ref[0, :, lanes], 2.0, 0.0)
            hi, lo = halves(g)
            his.append(hi)
            los.append(lo)
        hi, lo = jnp.concatenate(his, axis=1), jnp.concatenate(los, axis=1)
        rows = pl.ds(c, 256)
        both = jnp.dot(jnp.concatenate([hi, lo]), z_ref[rows, 0:D], preferred_element_type=f32)
        rest = jnp.dot(hi, z_ref[rows, D : 2 * D], preferred_element_type=f32)
        part = both[:rows_here] + (both[rows_here:] + rest)
        total = part if total is None else total + part
    acc_ref[...] += total

    @pl.when(k == STEPS - 1)
    def _():
        for i, out_ref in enumerate(out_refs):
            out_ref[0:PER, :] = acc_ref[i * PER : (i + 1) * PER, :]
            out_ref[PER:BLOCK, :] = jnp.broadcast_to(logs_ref[...], (BLOCK - PER, D))


def gradients(slots, sums, e, z, partner, weights=None):
    count = len(slots)
    first = weights is None
    vmem = pl.BlockSpec(memory_space=pltpu.VMEM)
    blocks = [jax.ShapeDtypeStruct((BLOCK, D), f32)] * count
    given, made, scratch = (), [], []
    if first:
        made = [
            jax.ShapeDtypeStruct((C, 128), f32),
            jax.ShapeDtypeStruct((STEPS, 1, SPAN), f32),
            jax.ShapeDtypeStruct((1, D), f32),
        ]
        scratch = [pltpu.VMEM((R_BLOCKS, 8, 256), f32)]
    else:
        given = weights
    size = count * PER * R
    return pl.pallas_call(
        functools.partial(gradient_kernel, slots, first),
        grid=(STEPS,),
        in_specs=[vmem]
        + [pl.BlockSpec((TILES, PER, LANES), lambda k, i=i: (k, i, 0)) for i in slots]
        + [pl.BlockSpec((SPAN, 2 * D), lambda k: (k, 0)), pl.BlockSpec((1, 1, SPAN), lambda k: (k, 0, 0))]
        + [vmem] * len(given),
        out_specs=[vmem] * (count + len(made)),
        out_shape=blocks + made,
        scratch_shapes=[pltpu.VMEM((count * PER, D), f32)] + scratch,
        compiler_params=pltpu.CompilerParams(vmem_limit_bytes=40 << 20),
        cost_estimate=pl.CostEstimate(flops=6 * size * D, bytes_accessed=4 * size, transcendentals=0),
    )(sums, *[e] * count, z, partner, *given)


SWAP = [(0, 1), (1, 0)]
UP = [(i, (i + 1) % 4) for i in range(4)]
DOWN = [(i, (i + 3) % 4) for i in range(4)]


def over_y(down, up, across):
    across = lax.ppermute(across, "y", [(i, (i + 2) % 4) for i in range(4)])
    return lax.ppermute(down, "y", DOWN), lax.ppermute(up, "y", UP), across


def shards(projections, partner):
    index = jnp.pad(partner.astype(f32)[None], ((0, BLOCK - PER - 1), (0, D - PER)))
    z, block = lax.optimization_barrier((projections, jnp.concatenate([projections, index])))
    a = lax.ppermute(z, "zl", SWAP)
    b = lax.ppermute(block, "zh", SWAP)
    c0 = jnp.concatenate([a, z])
    c1, c2 = lax.ppermute(c0, "y", UP), lax.ppermute(c0, "y", DOWN)
    c3z, c3a = lax.ppermute(c1[PER:], "y", UP), lax.ppermute(c2[:PER], "y", DOWN)
    r0 = jnp.concatenate([b, block])
    r1, r2 = lax.ppermute(r0, "x", UP), lax.ppermute(r0, "x", DOWN)
    r3z, r3b = lax.ppermute(r1[BLOCK:], "x", UP), lax.ppermute(r2[:BLOCK], "x", DOWN)
    swap = lambda r: lax.ppermute(r, "core", SWAP)
    columns = (z, c1[PER:], c2[PER:], c3z, a, c1[:PER], c2[:PER], c3a)
    rows = [(r[BLOCK:], r[:BLOCK], q[BLOCK:], q[:BLOCK]) for r, q in ((r, swap(r)) for r in (r0, r1, r2))]
    carried = scores(0, rows[0], columns)
    carried = scores(1, rows[1], carried=carried)
    e, zr, partners, sums = scores(2, (*rows[2], r3z, r3b, swap(r3z), swap(r3b)), carried=carried)
    sums = lax.all_to_all(sums, ALL, 0, 0, tiled=True)
    e, zr, partners = (pltpu.with_memory_space_constraint(v, pltpu.HBM) for v in (e, zr, partners))
    here, *away, uc, ur, logs = gradients((4, 5, 6, 7), sums, e, zr, partners)
    other = sum(over_y(*away), here)
    away = gradients((1, 2, 3), logs, e, zr, partners, (uc, ur))
    logs, other = lax.optimization_barrier((logs, other))
    (here,) = gradients((0,), logs, e, zr, partners, (uc, ur))
    terms = sum(over_y(*away), here) + lax.ppermute(other, "zl", SWAP)
    z, _ = lax.optimization_barrier((z, other))

    mean_objective = terms[PER, 0] / VIEWS
    scale = lax.rsqrt(jnp.sum(z * z, axis=-1, keepdims=True) + 1e-06)
    z = z * scale
    dz = terms[:PER] / TEMPERATURE
    grad = (dz - z * jnp.sum(z * dz, axis=-1, keepdims=True)) * scale
    return mean_objective, grad


def solution(mesh):
    fine = Mesh(mesh.devices.reshape(4, 2, 4, 2, 2), ALL)
    placed = (P(ALL, None), P(ALL))
    return jax.shard_map(
        shards, mesh=fine, in_specs=placed, out_specs=(P(), P(ALL, None)), check_vma=False
    )
```

time: 117 us -> 105 us (0.90)
  waiting for transfers between devices: 27.6 us -> 15.2 us
  Pallas kernels: 32.8 us -> 37 us
  blocking collectives: 18.3 us -> 16.8 us
  local copies, waits for them, and re-layouts: 3.08 us -> 1.7 us
    ppermute x13 -> x12, waiting for transfers between devices: 17.2 us -> 6.42 us  [the longest x4 3.84 us: over_y(): return (lax.ppermute(down, 'y', DOWN), lax.ppermute(up, 'y', UP), across)]
    pallas_call x3 -> x6, Pallas kernels: 32.8 us -> 37 us  [the longest x3 18.5 us: gradients(): pl.pallas_call(functools.partial(gradient_kernel, slots, first), grid=(ST...]
    ppermute x1, waiting for transfers between devices: 3.78 us -> 0.01 us  [shards(): lax.ppermute(c1[PER:], 'y', UP)]
    ppermute x1, waiting for transfers between devices: 2.99 us -> 0.01 us  [shards(): lax.ppermute(c2[:PER], 'y', DOWN)]
    ppermute x1, waiting for transfers between devices: 0.01 us -> 2.38 us  [shards(): a = lax.ppermute(z, 'zl', SWAP)]
    all_to_all x1, blocking collectives: 18.3 us -> 16.8 us  [shards(): sums = lax.all_to_all(sums, ALL, 0, 0, tiled=True)]
    unnamed x33 -> x4, local copies, waits for them, and re-layouts: 1.52 us -> 0.03 us
    ppermute x2, waiting for transfers between devices: 3.54 us -> 4.95 us  [shards(): r1, r2 = (lax.ppermute(r0, 'x', UP), lax.ppermute(r0, 'x', DOWN))]
  transfers between devices with their start and end apart: 23 -> 22, of which waited for: 8 -> 6; matrix products, arithmetic and copies ran while one was open for 2% -> 1% of each run, Pallas kernels for 7% -> 19%
where the time goes in v3:
time: 105 us
  Pallas kernels  37 us (35%)
  starting transfers between devices  28.8 us (27%)
  blocking collectives  16.8 us (16%)
  waiting for transfers between devices  15.2 us (14%)
  other arithmetic  2.93 us (3%)
  between operations  2.56 us (2%)
  local copies, waits for them, and re-layouts  1.7 us (2%)
    pallas_call x3, Pallas kernels, gradients(): pl.pallas_call(functools.partial(gradient_kernel, slots, first), grid=(ST...  18.5 us
    pallas_call x3, Pallas kernels, scores(): pl.pallas_call(functools.partial(score_kernel, start, steps), grid=(steps...  18.5 us
    all_to_all x1, blocking collectives, shards(): sums = lax.all_to_all(sums, ALL, 0, 0, tiled=True)  16.8 us
    ppermute x2, waiting for transfers between devices, shards(): r1, r2 = (lax.ppermute(r0, 'x', UP), lax.ppermute(r0, 'x', DOWN))  4.95 us
    ppermute x4, starting transfers between devices, over_y(): return (lax.ppermute(down, 'y', DOWN), lax.ppermute(up, 'y', UP), across)  4.75 us
    ppermute x4, waiting for transfers between devices, over_y(): return (lax.ppermute(down, 'y', DOWN), lax.ppermute(up, 'y', UP), across)  3.84 us
    ppermute x1, starting transfers between devices, shards(): b = lax.ppermute(block, 'zh', SWAP)  3.58 us
    ppermute x2, starting transfers between devices, shards(): r1, r2 = (lax.ppermute(r0, 'x', UP), lax.ppermute(r0, 'x', DOWN))  3.31 us
  transfers between devices with their start and end apart: 22, of which 6 were waited for; matrix products, arithmetic and copies ran while one was open for 1% of the time, Pallas kernels for 19%

profile of v3, /device:TPU:0, one launch (start us, length us, event | category | flops | bytes accessed | tf_op | source)
XLA Modules:
  0.0 105.0 jit_solution(18153517803084062668)
XLA Ops:
  2.3 2.1 %collective-permute-start.8 = (f32[192,256]{1,0:T(8,128)}, f32[192,256]{1,0:T(8,128)S(1)}, u32[]{:S(2)}, u32[]{:S(2)}) collective-permute-start(f32[192,256]{1,0:T(8,128)} %refs_0_), channel_id=1, source_target_pairs={{0,16},{16,0},{1,17},{17,1},{2,18},{18,2},{3,19},{19,3},{4,20},{20... | collective-permute-start | bytes 589832 | tf_op jit(solution)/shard_map/ppermute | solution.py:302
  4.4 3.6 %collective-permute-start = (f32[200,256]{1,0:T(8,128)S(1)}, f32[200,256]{1,0:T(8,128)S(1)}, u32[]{:S(2)}, u32[]{:S(2)}) collective-permute-start(f32[200,256]{1,0:T(8,128)S(1)} %select_maximum_fusion.refs_8_), channel_id=1, source_target_pairs={{0,2},{2,0},{1,3},{3,1},{4,6},{6,4},{5,7},{7,5},{8,10},{10,8},{9,1... | collective-permute-start | bytes 614408 | tf_op jit(solution)/shard_map/ppermute | solution.py:303
  8.0 2.4 %collective-permute-done.8.refs_4_ = f32[192,256]{1,0:T(8,128)S(1)} collective-permute-done((f32[192,256]{1,0:T(8,128)}, f32[192,256]{1,0:T(8,128)S(1)}, u32[]{:S(2)}, u32[]{:S(2)}) %collective-permute-start.8) | collective-permute-done | bytes 196640 | tf_op jit(solution)/shard_map/ppermute | solution.py:302
  10.4 0.9 constant_dynamic-update-slice_fusion.2
  11.3 1.7 %collective-permute-start.9 = (f32[384,256]{1,0:T(8,128)S(1)}, f32[384,256]{1,0:T(8,128)S(1)}, u32[]{:S(2)}, u32[]{:S(2)}) collective-permute-start(f32[384,256]{1,0:T(8,128)S(1)} %constant_dynamic-update-slice_fusion.2), channel_id=1, source_target_pairs={{0,32},{32,64},{64,96},{96,0},{1,33},{33,65},{65,97},{97,1},{2,34}... | collective-permute-start | bytes 1179656 | tf_op jit(solution)/shard_map/ppermute | solution.py:305
  13.1 1.6 %collective-permute-start.10 = (f32[384,256]{1,0:T(8,128)S(1)}, f32[384,256]{1,0:T(8,128)S(1)}, u32[]{:S(2)}, u32[]{:S(2)}) collective-permute-start(f32[384,256]{1,0:T(8,128)S(1)} %constant_dynamic-update-slice_fusion.2), channel_id=1, source_target_pairs={{0,96},{32,0},{64,32},{96,64},{1,97},{33,1},{65,33},{97,65},{2,98}... | collective-permute-start | bytes 1179656 | tf_op jit(solution)/shard_map/ppermute | solution.py:305
  14.6 2.6 %collective-permute-done.refs_9_ = f32[200,256]{1,0:T(8,128)S(1)} collective-permute-done((f32[200,256]{1,0:T(8,128)S(1)}, f32[200,256]{1,0:T(8,128)S(1)}, u32[]{:S(2)}, u32[]{:S(2)}) %collective-permute-start) | collective-permute-done | bytes 204832 | tf_op jit(solution)/shard_map/ppermute | solution.py:303
  17.3 1.6 %collective-permute-start.3 = (f32[400,256]{1,0:T(8,128)S(1)}, f32[400,256]{1,0:T(8,128)S(1)}, u32[]{:S(2)}, u32[]{:S(2)}) collective-permute-start(f32[400,256]{1,0:T(8,128)S(1)} %constant_dynamic-update-slice_fusion), channel_id=1, source_target_pairs={{0,4},{4,8},{8,12},{12,0},{1,5},{5,9},{9,13},{13,1},{2,6},{6,10},{... | collective-permute-start | bytes 1228808 | tf_op jit(solution)/shard_map/ppermute | solution.py:308
  18.9 1.7 %collective-permute-start.1 = (f32[400,256]{1,0:T(8,128)S(1)}, f32[400,256]{1,0:T(8,128)S(1)}, u32[]{:S(2)}, u32[]{:S(2)}) collective-permute-start(f32[400,256]{1,0:T(8,128)S(1)} %constant_dynamic-update-slice_fusion), channel_id=1, source_target_pairs={{0,12},{4,0},{8,4},{12,8},{1,13},{5,1},{9,5},{13,9},{2,14},{6,2},{... | collective-permute-start | bytes 1228808 | tf_op jit(solution)/shard_map/ppermute | solution.py:308
  20.6 1.4 %collective-permute-done.9 = f32[384,256]{1,0:T(8,128)S(1)} collective-permute-done((f32[384,256]{1,0:T(8,128)S(1)}, f32[384,256]{1,0:T(8,128)S(1)}, u32[]{:S(2)}, u32[]{:S(2)}) %collective-permute-start.9) | collective-permute-done | bytes 393248 | tf_op jit(solution)/shard_map/ppermute | solution.py:305
  22.4 3.0 %collective-permute-start.12 = (f32[192,256]{1,0:T(8,128)S(1)}, f32[192,256]{1,0:T(8,128)S(1)}, u32[]{:S(2)}, u32[]{:S(2)}) collective-permute-start(f32[192,256]{1,0:T(8,128)S(1)} %get-tuple-element.78.refs_6_), channel_id=1, source_target_pairs={{0,96},{32,0},{64,32},{96,64},{1,97},{33,1},{65,33},{97,65},{2,98}... | collective-permute-start | bytes 589832 | tf_op jit(solution)/shard_map/ppermute | solution.py:306
  25.5 4.9 %collective-permute-done.3 = f32[400,256]{1,0:T(8,128)S(1)} collective-permute-done((f32[400,256]{1,0:T(8,128)S(1)}, f32[400,256]{1,0:T(8,128)S(1)}, u32[]{:S(2)}, u32[]{:S(2)}) %collective-permute-start.3) | collective-permute-done | bytes 409632 | tf_op jit(solution)/shard_map/ppermute | solution.py:308
  30.8 3.0 %collective-permute-start.5 = (f32[200,256]{1,0:T(8,128)S(1)}, f32[200,256]{1,0:T(8,128)S(1)}, u32[]{:S(2)}, u32[]{:S(2)}) collective-permute-start(f32[200,256]{1,0:T(8,128)S(1)} %get-tuple-element.76.refs_1_), channel_id=1, source_target_pairs={{0,12},{4,0},{8,4},{12,8},{1,13},{5,1},{9,5},{13,9},{2,14},{6,2},{... | collective-permute-start | bytes 614408 | tf_op jit(solution)/shard_map/ppermute | solution.py:309
  34.5 5.0 %shard_map.41 = (f32[12,1536,256]{2,1,0:T(8,128)}, bf16[3072,512]{1,0:T(8,128)(2,1)}, f32[4,1,768]{2,1,0:T(1,128)}, f32[1,1,768]{2,1,0:T(1,128)S(1)}, f32[8,128]...) custom-call(f32[192,256]{1,0:T(8,128)S(1)} %copy-done, ...), custom_call_target="tpu_custom_call" | custom-call | flops 1811939328 | bytes 4718592 | tf_op jit(solution)/shard_map/pallas_call | solution.py:175
  40.1 4.6 %shard_map.42 = (f32[12,1536,256]{2,1,0:T(8,128)}, bf16[3072,512]{1,0:T(8,128)(2,1)}, f32[4,1,768]{2,1,0:T(1,128)}, f32[1,1,768]{2,1,0:T(1,128)S(1)}, f32[8,128]{1,0:T(8,128)S(1)}, /*index=5*/f32[1536,128]{1,0:T(8,128)S(1)}) custom-call(f32[200,256]{1,0:T(8,128)S(1)} %get-tuple-element.71.refs_0_, ...), custom_call_target="tpu_custom_call", output_to_operand_aliasing={{0}: (8, {}), {1}: (9, {}), {2}: (10, {})} | custom-call | flops 1811939328 | bytes 4718592 | tf_op jit(solution)/shard_map/pallas_call | solution.py:175
  44.7 8.9 %shard_map.43 = (f32[12,1536,256]{2,1,0:T(8,128)}, bf16[3072,512]{1,0:T(8,128)(2,1)}, f32[4,1,768]{2,1,0:T(1,128)}, f32[128,1,512]{2,1,0:T(1,128)S(1)}) custom-call(f32[200,256]{1,0:T(8,128)S(1)} %get-tuple-element.77.refs_0_, f32[200,256]{1,0:T(8,128)S(1)} %get-tuple-element.76.refs_1_, ...), custom_call_target="tpu_custom_call", output_to_operand_aliasing={{0}: (12, {}), {1}: (13, {}), {2}: (14, {})} | custom-call | flops 3623878656 | bytes 9437184 | tf_op jit(solution)/shard_map/pallas_call | solution.py:175
  53.6 16.8 %all_to_all.5.sums_ref = f32[128,1,512]{2,1,0:T(1,128)S(1)} all-to-all(f32[128,1,512]{2,1,0:T(1,128)S(1)} %get-tuple-element.51), channel_id=1, replica_groups=mesh['y'=4,'zl'=2,'x'=4,'zh'=2,'core'=2] {'y','zl','x','zh','core'}, dimensions={0} | all-to-all | bytes 524288 | tf_op jit(solution)/shard_map/all_to_all | solution.py:316
  70.4 8.0 %shard_map.44 = (f32[200,256]{1,0:T(8,128)S(1)}, f32[200,256]{1,0:T(8,128)S(1)}, f32[200,256]{1,0:T(8,128)S(1)}, f32[200,256]{1,0:T(8,128)S(1)}, f32[1536,128]{1...) custom-call(f32[128,1,512]{2,1,0:T(1,128)S(1)} %all_to_all.5.sums_ref, ...), custom_call_target="tpu_custom_call" | custom-call | flops 3623878656 | bytes 9437184 | tf_op jit(solution)/shard_map/pallas_call | solution.py:274
  78.4 1.2 %collective-permute-start.15 = (f32[200,256]{1,0:T(8,128)S(1)}, f32[200,256]{1,0:T(8,128)S(1)}, u32[]{:S(2)}, u32[]{:S(2)}) collective-permute-start(f32[200,256]{1,0:T(8,128)S(1)} %get-tuple-element.57), channel_id=1, source_target_pairs={{0,96},{32,0},{64,32},{96,64},{1,97},{33,1},{65,33},{97,65},{2,98}... | collective-permute-start | bytes 614408 | tf_op jit(solution)/shard_map/ppermute | solution.py:296
  81.2 6.4 %shard_map.46 = (f32[200,256]{1,0:T(8,128)S(1)}, f32[200,256]{1,0:T(8,128)S(1)}, f32[200,256]{1,0:T(8,128)S(1)}) custom-call(f32[1,256]{1,0:T(1,128)S(1)} %get-tuple-element.60.sums_ref, f32[12,1536,256]{2,1,0:T(8,128)} %get-tuple-element.52.refs_0_.refs_1_.refs_2_.refs_3_, f32[12,1536,256]{2,1,0:T(8,128)} %get-tuple-element.52.refs_0_.refs_1_.refs_2_.refs_3_, ...), custom_call_target="tpu_custom_call" | custom-call | flops 2717908992 | bytes 7077888 | tf_op jit(solution)/shard_map/pallas_call | solution.py:274
  87.6 2.7 %collective-permute-start.18 = (f32[200,256]{1,0:T(8,128)S(1)}, f32[200,256]{1,0:T(8,128)S(1)}, u32[]{:S(2)}, u32[]{:S(2)}) collective-permute-start(f32[200,256]{1,0:T(8,128)S(1)} %get-tuple-element.63), channel_id=1, source_target_pairs={{0,96},{32,0},{64,32},{96,64},{1,97},{33,1},{65,33},{97,65},{2,98}... | collective-permute-start | bytes 614408 | tf_op jit(solution)/shard_map/ppermute | solution.py:296
  90.3 2.3 %collective-permute-start.20 = (f32[200,256]{1,0:T(8,128)S(1)}, f32[200,256]{1,0:T(8,128)S(1)}, u32[]{:S(2)}, u32[]{:S(2)}) collective-permute-start(f32[200,256]{1,0:T(8,128)S(1)} %get-tuple-element.65), channel_id=1, source_target_pairs={{0,64},{32,96},{64,0},{96,32},{1,65},{33,97},{65,1},{97,33},{2,66}... | collective-permute-start | bytes 614408 | tf_op jit(solution)/shard_map/ppermute | solution.py:295
  93.5 4.1 %shard_map.45 = f32[200,256]{1,0:T(8,128)S(1)} custom-call(f32[1,256]{1,0:T(1,128)S(1)} %get-tuple-element.60.sums_ref, f32[12,1536,256]{2,1,0:T(8,128)} %get-tuple-element.52.refs_0_.refs_1_.refs_2_.refs_3_, bf16[3072,512]{1,0:T(8,128)(2,1)} %get-tuple-element.53.refs_4_.refs_1_.refs_3_, f32[4,1,768]{2,1,0:T(1,128)} %get-tuple-element.54.refs_5_.refs_2_.refs_4_, ...), custom_call_target="tpu_custom_call" | custom-call | flops 905969664 | bytes 2359296 | tf_op jit(solution)/shard_map/pallas_call | solution.py:274
  98.2 3.4 %collective-permute-done.19 = f32[200,256]{1,0:T(8,128)S(1)} collective-permute-done((f32[200,256]{1,0:T(8,128)S(1)}, f32[200,256]{1,0:T(8,128)S(1)}, u32[]{:S(2)}, u32[]{:S(2)}) %collective-permute-start.19) | collective-permute-done | bytes 204832 | tf_op jit(solution)/shard_map/ppermute | solution.py:296
  (49 shorter events, 8.6 us)
Async XLA Ops:
  0.6 33.9 %copy-start = (f32[192,256]{1,0:T(8,128)S(1)}, f32[192,256]{1,0:T(8,128)}, u32[]{:S(2)}) copy-start(f32[192,256]{1,0:T(8,128)} %refs_0_) | copy-start | bytes 589828
  2.3 8.0 %collective-permute-start.8 = (f32[192,256]{1,0:T(8,128)}, f32[192,256]{1,0:T(8,128)S(1)}, u32[]{:S(2)}, u32[]{:S(2)}) collective-permute-start(f32[192,256]{1,0:T(8,128)} %refs_0_), channel_id=1, source_target_pairs={{0,16},{16,0},{1,17},{17,1},{2,18},{18,2},{3,19},{19,3},{4,20},{20... | collective-permute-start | bytes 589832 | tf_op jit(solution)/shard_map/ppermute | solution.py:302
  4.4 12.8 %collective-permute-start = (f32[200,256]{1,0:T(8,128)S(1)}, f32[200,256]{1,0:T(8,128)S(1)}, u32[]{:S(2)}, u32[]{:S(2)}) collective-permute-start(f32[200,256]{1,0:T(8,128)S(1)} %select_maximum_fusion.refs_8_), channel_id=1, source_target_pairs={{0,2},{2,0},{1,3},{3,1},{4,6},{6,4},{5,7},{7,5},{8,10},{10,8},{9,1... | collective-permute-start | bytes 614408 | tf_op jit(solution)/shard_map/ppermute | solution.py:303
  11.3 10.7 %collective-permute-start.9 = (f32[384,256]{1,0:T(8,128)S(1)}, f32[384,256]{1,0:T(8,128)S(1)}, u32[]{:S(2)}, u32[]{:S(2)}) collective-permute-start(f32[384,256]{1,0:T(8,128)S(1)} %constant_dynamic-update-slice_fusion.2), channel_id=1, source_target_pairs={{0,32},{32,64},{64,96},{96,0},{1,33},{33,65},{65,97},{97,1},{2,34}... | collective-permute-start | bytes 1179656 | tf_op jit(solution)/shard_map/ppermute | solution.py:305
  13.1 9.3 %collective-permute-start.10 = (f32[384,256]{1,0:T(8,128)S(1)}, f32[384,256]{1,0:T(8,128)S(1)}, u32[]{:S(2)}, u32[]{:S(2)}) collective-permute-start(f32[384,256]{1,0:T(8,128)S(1)} %constant_dynamic-update-slice_fusion.2), channel_id=1, source_target_pairs={{0,96},{32,0},{64,32},{96,64},{1,97},{33,1},{65,33},{97,65},{2,98}... | collective-permute-start | bytes 1179656 | tf_op jit(solution)/shard_map/ppermute | solution.py:305
  17.2 16.6 %collective-permute-start.13 = (f32[400,256]{1,0:T(8,128)S(1)}, f32[400,256]{1,0:T(8,128)S(1)}, u32[]{:S(2)}, u32[]{:S(2)}) collective-permute-start(f32[400,256]{1,0:T(8,128)S(1)} %constant_dynamic-update-slice_fusion), channel_id=1, source_target_pairs={{0,1},{1,0},{2,3},{3,2},{4,5},{5,4},{6,7},{7,6},{8,9},{9,8},{10,11... | collective-permute-start | bytes 1228808 | tf_op jit(solution)/shard_map/ppermute | solution.py:310
  17.3 13.1 %collective-permute-start.3 = (f32[400,256]{1,0:T(8,128)S(1)}, f32[400,256]{1,0:T(8,128)S(1)}, u32[]{:S(2)}, u32[]{:S(2)}) collective-permute-start(f32[400,256]{1,0:T(8,128)S(1)} %constant_dynamic-update-slice_fusion), channel_id=1, source_target_pairs={{0,4},{4,8},{8,12},{12,0},{1,5},{5,9},{9,13},{13,1},{2,6},{6,10},{... | collective-permute-start | bytes 1228808 | tf_op jit(solution)/shard_map/ppermute | solution.py:308
  18.9 11.9 %collective-permute-start.1 = (f32[400,256]{1,0:T(8,128)S(1)}, f32[400,256]{1,0:T(8,128)S(1)}, u32[]{:S(2)}, u32[]{:S(2)}) collective-permute-start(f32[400,256]{1,0:T(8,128)S(1)} %constant_dynamic-update-slice_fusion), channel_id=1, source_target_pairs={{0,12},{4,0},{8,4},{12,8},{1,13},{5,1},{9,5},{13,9},{2,14},{6,2},{... | collective-permute-start | bytes 1228808 | tf_op jit(solution)/shard_map/ppermute | solution.py:308
  22.1 11.8 %collective-permute-start.11 = (f32[192,256]{1,0:T(8,128)S(1)}, f32[192,256]{1,0:T(8,128)S(1)}, u32[]{:S(2)}, u32[]{:S(2)}) collective-permute-start(f32[192,256]{1,0:T(8,128)S(1)} %get-tuple-element.81.refs_1_), channel_id=1, source_target_pairs={{0,32},{32,64},{64,96},{96,0},{1,33},{33,65},{65,97},{97,1},{2,34}... | collective-permute-start | bytes 589832 | tf_op jit(solution)/shard_map/ppermute | solution.py:306
  22.4 12.1 %collective-permute-start.12 = (f32[192,256]{1,0:T(8,128)S(1)}, f32[192,256]{1,0:T(8,128)S(1)}, u32[]{:S(2)}, u32[]{:S(2)}) collective-permute-start(f32[192,256]{1,0:T(8,128)S(1)} %get-tuple-element.78.refs_6_), channel_id=1, source_target_pairs={{0,96},{32,0},{64,32},{96,64},{1,97},{33,1},{65,33},{97,65},{2,98}... | collective-permute-start | bytes 589832 | tf_op jit(solution)/shard_map/ppermute | solution.py:306
  30.4 9.0 %collective-permute-start.4 = (f32[200,256]{1,0:T(8,128)S(1)}, f32[200,256]{1,0:T(8,128)S(1)}, u32[]{:S(2)}, u32[]{:S(2)}) collective-permute-start(f32[200,256]{1,0:T(8,128)S(1)} %get-tuple-element.71.refs_0_), channel_id=1, source_target_pairs={{0,4},{4,8},{8,12},{12,0},{1,5},{5,9},{9,13},{13,1},{2,6},{6,10},{... | collective-permute-start | bytes 614408 | tf_op jit(solution)/shard_map/ppermute | solution.py:309
  30.8 8.7 %collective-permute-start.5 = (f32[200,256]{1,0:T(8,128)S(1)}, f32[200,256]{1,0:T(8,128)S(1)}, u32[]{:S(2)}, u32[]{:S(2)}) collective-permute-start(f32[200,256]{1,0:T(8,128)S(1)} %get-tuple-element.76.refs_1_), channel_id=1, source_target_pairs={{0,12},{4,0},{8,4},{12,8},{1,13},{5,1},{9,5},{13,9},{2,14},{6,2},{... | collective-permute-start | bytes 614408 | tf_op jit(solution)/shard_map/ppermute | solution.py:309
  33.9 6.1 %collective-permute-start.14 = (f32[400,256]{1,0:T(8,128)S(1)}, f32[400,256]{1,0:T(8,128)S(1)}, u32[]{:S(2)}, u32[]{:S(2)}) collective-permute-start(f32[400,256]{1,0:T(8,128)S(1)} %collective-permute-done.3), channel_id=1, source_target_pairs={{0,1},{1,0},{2,3},{3,2},{4,5},{5,4},{6,7},{7,6},{8,9},{9,8},{10,11... | collective-permute-start | bytes 1228808 | tf_op jit(solution)/shard_map/ppermute | solution.py:310
  33.9 6.1 %collective-permute-start.2 = (f32[400,256]{1,0:T(8,128)S(1)}, f32[400,256]{1,0:T(8,128)S(1)}, u32[]{:S(2)}, u32[]{:S(2)}) collective-permute-start(f32[400,256]{1,0:T(8,128)S(1)} %collective-permute-done.1), channel_id=1, source_target_pairs={{0,1},{1,0},{2,3},{3,2},{4,5},{5,4},{6,7},{7,6},{8,9},{9,8},{10,11... | collective-permute-start | bytes 1228808 | tf_op jit(solution)/shard_map/ppermute | solution.py:310
  39.5 5.2 %collective-permute-start.6 = (f32[200,256]{1,0:T(8,128)S(1)}, f32[200,256]{1,0:T(8,128)S(1)}, u32[]{:S(2)}, u32[]{:S(2)}) collective-permute-start(f32[200,256]{1,0:T(8,128)S(1)} %collective-permute-done.4.refs_4_), channel_id=1, source_target_pairs={{0,1},{1,0},{2,3},{3,2},{4,5},{5,4},{6,7},{7,6},{8,9},{9,8},{10,11... | collective-permute-start | bytes 614408 | tf_op jit(solution)/shard_map/ppermute | solution.py:310
  39.5 5.2 %collective-permute-start.7 = (f32[200,256]{1,0:T(8,128)S(1)}, f32[200,256]{1,0:T(8,128)S(1)}, u32[]{:S(2)}, u32[]{:S(2)}) collective-permute-start(f32[200,256]{1,0:T(8,128)S(1)} %collective-permute-done.5.refs_5_), channel_id=1, source_target_pairs={{0,1},{1,0},{2,3},{3,2},{4,5},{5,4},{6,7},{7,6},{8,9},{9,8},{10,11... | collective-permute-start | bytes 614408 | tf_op jit(solution)/shard_map/ppermute | solution.py:310
  78.4 11.9 %collective-permute-start.15 = (f32[200,256]{1,0:T(8,128)S(1)}, f32[200,256]{1,0:T(8,128)S(1)}, u32[]{:S(2)}, u32[]{:S(2)}) collective-permute-start(f32[200,256]{1,0:T(8,128)S(1)} %get-tuple-element.57), channel_id=1, source_target_pairs={{0,96},{32,0},{64,32},{96,64},{1,97},{33,1},{65,33},{97,65},{2,98}... | collective-permute-start | bytes 614408 | tf_op jit(solution)/shard_map/ppermute | solution.py:296
  79.6 13.0 %collective-permute-start.16 = (f32[200,256]{1,0:T(8,128)S(1)}, f32[200,256]{1,0:T(8,128)S(1)}, u32[]{:S(2)}, u32[]{:S(2)}) collective-permute-start(f32[200,256]{1,0:T(8,128)S(1)} %get-tuple-element.58), channel_id=1, source_target_pairs={{0,32},{32,64},{64,96},{96,0},{1,33},{33,65},{65,97},{97,1},{2,34}... | collective-permute-start | bytes 614408 | tf_op jit(solution)/shard_map/ppermute | solution.py:296
  80.5 12.0 %collective-permute-start.17 = (f32[200,256]{1,0:T(8,128)S(1)}, f32[200,256]{1,0:T(8,128)S(1)}, u32[]{:S(2)}, u32[]{:S(2)}) collective-permute-start(f32[200,256]{1,0:T(8,128)S(1)} %get-tuple-element.59), channel_id=1, source_target_pairs={{0,64},{32,96},{64,0},{96,32},{1,65},{33,97},{65,1},{97,33},{2,66}... | collective-permute-start | bytes 614408 | tf_op jit(solution)/shard_map/ppermute | solution.py:295
  87.6 10.6 %collective-permute-start.18 = (f32[200,256]{1,0:T(8,128)S(1)}, f32[200,256]{1,0:T(8,128)S(1)}, u32[]{:S(2)}, u32[]{:S(2)}) collective-permute-start(f32[200,256]{1,0:T(8,128)S(1)} %get-tuple-element.63), channel_id=1, source_target_pairs={{0,96},{32,0},{64,32},{96,64},{1,97},{33,1},{65,33},{97,65},{2,98}... | collective-permute-start | bytes 614408 | tf_op jit(solution)/shard_map/ppermute | solution.py:296
  90.3 11.3 %collective-permute-start.19 = (f32[200,256]{1,0:T(8,128)S(1)}, f32[200,256]{1,0:T(8,128)S(1)}, u32[]{:S(2)}, u32[]{:S(2)}) collective-permute-start(f32[200,256]{1,0:T(8,128)S(1)} %get-tuple-element.64), channel_id=1, source_target_pairs={{0,32},{32,64},{64,96},{96,0},{1,33},{33,65},{65,97},{97,1},{2,34}... | collective-permute-start | bytes 614408 | tf_op jit(solution)/shard_map/ppermute | solution.py:296
  90.3 11.3 %collective-permute-start.20 = (f32[200,256]{1,0:T(8,128)S(1)}, f32[200,256]{1,0:T(8,128)S(1)}, u32[]{:S(2)}, u32[]{:S(2)}) collective-permute-start(f32[200,256]{1,0:T(8,128)S(1)} %get-tuple-element.65), channel_id=1, source_target_pairs={{0,64},{32,96},{64,0},{96,32},{1,65},{33,97},{65,1},{97,33},{2,66}... | collective-permute-start | bytes 614408 | tf_op jit(solution)/shard_map/ppermute | solution.py:295
  92.6 9.0 %collective-permute-start.21 = (f32[200,256]{1,0:T(8,128)S(1)}, f32[200,256]{1,0:T(8,128)S(1)}, u32[]{:S(2)}, u32[]{:S(2)}) collective-permute-start(f32[200,256]{1,0:T(8,128)S(1)} %add_add_fusion.1), channel_id=1, source_target_pairs={{0,16},{16,0},{1,17},{17,1},{2,18},{18,2},{3,19},{19,3},{4,20},{20... | collective-permute-start | bytes 614408 | tf_op jit(solution)/shard_map/ppermute | solution.py:323

commit v4 on v3

--- a/solution.py
+++ b/solution.py
@@ -19,6 +19,7 @@
 STEPS = R // SPAN
 LANES = 256
 TILES = SPAN // LANES
+WIDE = 2
 BLOCK = 200
 PAIR = PER + BLOCK
 TEMPERATURE = 0.1
@@ -230,13 +231,13 @@
     ids = lax.broadcasted_iota(jnp.int32, (PER, 128), 0)
     ids = jnp.concatenate([ids + (place[i] * R_BLOCKS + place[24]) * PER for i in slots]).astype(f32)
     total = None
-    for c in range(0, SPAN, 256):
+    for c in range(0, WIDE * SPAN, 256):
         his, los = [], []
         for h in range(c, c + 256, 128):
-            lanes = pl.ds(h, 128)
+            part, lanes = h // SPAN, pl.ds(h % SPAN, 128)
             e = jnp.concatenate([e_ref[c // 256, :, h - c : h - c + 128] for e_ref in e_refs])
-            g = e * (uc + ur_ref[k, :, lanes])
-            g = g - jnp.where(ids == partner_ref[0, :, lanes], 2.0, 0.0)
+            g = e * (uc + ur_ref[WIDE * k + part, :, lanes])
+            g = g - jnp.where(ids == partner_ref[part, :, lanes], 2.0, 0.0)
             hi, lo = halves(g)
             his.append(hi)
             los.append(lo)
@@ -248,7 +249,7 @@
         total = part if total is None else total + part
     acc_ref[...] += total
 
-    @pl.when(k == STEPS - 1)
+    @pl.when(k == STEPS // WIDE - 1)
     def _():
         for i, out_ref in enumerate(out_refs):
             out_ref[0:PER, :] = acc_ref[i * PER : (i + 1) * PER, :]
@@ -273,10 +274,10 @@
     size = count * PER * R
     return pl.pallas_call(
         functools.partial(gradient_kernel, slots, first),
-        grid=(STEPS,),
+        grid=(STEPS // WIDE,),
         in_specs=[vmem]
-        + [pl.BlockSpec((TILES, PER, LANES), lambda k, i=i: (k, i, 0)) for i in slots]
-        + [pl.BlockSpec((SPAN, 2 * D), lambda k: (k, 0)), pl.BlockSpec((1, 1, SPAN), lambda k: (k, 0, 0))]
+        + [pl.BlockSpec((WIDE * TILES, PER, LANES), lambda k, i=i: (k, i, 0)) for i in slots]
+        + [pl.BlockSpec((WIDE * SPAN, 2 * D), lambda k: (k, 0)), pl.BlockSpec((WIDE, 1, SPAN), lambda k: (k, 0, 0))]
         + [vmem] * len(given),
         out_specs=[vmem] * (count + len(made)),
         out_shape=blocks + made,
@@ -286,6 +287,45 @@
     )(sums, *[e] * count, z, partner, *given)
 
 
+def finish_kernel(z_ref, *refs):
+    *term_refs, mean_ref, grad_ref = refs
+    total = term_refs[0][...]
+    for ref in term_refs[1:]:
+        total = total + ref[...]
+    mean_ref[0, 0] = jnp.sum(total[PER : PER + 1, 0:1]) / VIEWS
+    z = z_ref[...]
+    scale = lax.rsqrt(jnp.sum(z * z, axis=-1, keepdims=True) + 1e-06)
+    z = z * scale
+    dz = total[0:PER, :] * (1.0 / TEMPERATURE)
+    grad_ref[...] = (dz - z * jnp.sum(z * dz, axis=-1, keepdims=True)) * scale
+
+
+def finish(z, *terms):
+    return pl.pallas_call(
+        finish_kernel,
+        in_specs=[pl.BlockSpec(memory_space=pltpu.VMEM)] * (1 + len(terms)),
+        out_specs=[pl.BlockSpec(memory_space=pltpu.SMEM), pl.BlockSpec(memory_space=pltpu.VMEM)],
+        out_shape=[jax.ShapeDtypeStruct((1, 1), f32), jax.ShapeDtypeStruct((PER, D), f32)],
+        compiler_params=pltpu.CompilerParams(vmem_limit_bytes=16 << 20),
+    )(z, *terms)
+
+
+def pack_kernel(z_ref, partner_ref, out_ref):
+    out_ref[0:PER, :] = z_ref[...]
+    out_ref[PER:BLOCK, :] = jnp.zeros((BLOCK - PER, D), f32)
+    out_ref[PER : PER + 1, 0:PER] = partner_ref[...].reshape(1, PER).astype(f32)
+
+
+def pack(z, partner):
+    return pl.pallas_call(
+        pack_kernel,
+        in_specs=[pl.BlockSpec(memory_space=pltpu.VMEM)] * 2,
+        out_specs=pl.BlockSpec(memory_space=pltpu.VMEM),
+        out_shape=jax.ShapeDtypeStruct((BLOCK, D), f32),
+        compiler_params=pltpu.CompilerParams(vmem_limit_bytes=16 << 20),
+    )(z, partner)
+
+
 SWAP = [(0, 1), (1, 0)]
 UP = [(i, (i + 1) % 4) for i in range(4)]
 DOWN = [(i, (i + 3) % 4) for i in range(4)]
@@ -297,8 +337,8 @@
 
 
 def shards(projections, partner):
-    index = jnp.pad(partner.astype(f32)[None], ((0, BLOCK - PER - 1), (0, D - PER)))
-    z, block = lax.optimization_barrier((projections, jnp.concatenate([projections, index])))
+    here = (pltpu.with_memory_space_constraint(v, pltpu.HBM) for v in (projections, partner))
+    z, block = lax.optimization_barrier((projections, pack(*here)))
     a = lax.ppermute(z, "zl", SWAP)
     b = lax.ppermute(block, "zh", SWAP)
     c0 = jnp.concatenate([a, z])
@@ -320,15 +360,8 @@
     away = gradients((1, 2, 3), logs, e, zr, partners, (uc, ur))
     logs, other = lax.optimization_barrier((logs, other))
     (here,) = gradients((0,), logs, e, zr, partners, (uc, ur))
-    terms = sum(over_y(*away), here) + lax.ppermute(other, "zl", SWAP)
-    z, _ = lax.optimization_barrier((z, other))
-
-    mean_objective = terms[PER, 0] / VIEWS
-    scale = lax.rsqrt(jnp.sum(z * z, axis=-1, keepdims=True) + 1e-06)
-    z = z * scale
-    dz = terms[:PER] / TEMPERATURE
-    grad = (dz - z * jnp.sum(z * dz, axis=-1, keepdims=True)) * scale
-    return mean_objective, grad
+    mean_objective, grad = finish(z, here, *over_y(*away), lax.ppermute(other, "zl", SWAP))
+    return mean_objective[0, 0], grad
 
 
 def solution(mesh):

time: 105 us -> 101 us (0.962)
  other arithmetic: 2.93 us -> 0.06 us
  between operations: 2.56 us -> 0.94 us
    pallas_call x0 -> x2, Pallas kernels: none -> 1.89 us  [the longest x1 1.01 us: pack(): pl.pallas_call(pack_kernel, in_specs=[pl.BlockSpec(memory_space=pltpu.VME...]
    pallas_call x3, Pallas kernels: 18.5 us -> 17 us  [gradients(): pl.pallas_call(functools.partial(gradient_kernel, slots, first), grid=(ST...]
  transfers between devices with their start and end apart: 22 -> 22, of which waited for: 6 -> 5; matrix products, arithmetic and copies ran while one was open for 1% -> 1% of each run, Pallas kernels for 19% -> 18%
where the time goes in v4:
time: 101 us
  Pallas kernels  37.3 us (37%)
  starting transfers between devices  28.8 us (29%)
  blocking collectives  16.8 us (17%)
  waiting for transfers between devices  16.1 us (16%)
  local copies, waits for them, and re-layouts  1.18 us (1%)
    pallas_call x3, Pallas kernels, scores(): pl.pallas_call(functools.partial(score_kernel, start, steps), grid=(steps...  18.4 us
    pallas_call x3, Pallas kernels, gradients(): pl.pallas_call(functools.partial(gradient_kernel, slots, first), grid=(ST...  17 us
    all_to_all x1, blocking collectives, shards(): sums = lax.all_to_all(sums, ALL, 0, 0, tiled=True)  16.8 us
    ppermute x2, waiting for transfers between devices, shards(): r1, r2 = (lax.ppermute(r0, 'x', UP), lax.ppermute(r0, 'x', DOWN))  4.95 us
    ppermute x4, starting transfers between devices, over_y(): return (lax.ppermute(down, 'y', DOWN), lax.ppermute(up, 'y', UP), across)  4.75 us
    ppermute x4, waiting for transfers between devices, over_y(): return (lax.ppermute(down, 'y', DOWN), lax.ppermute(up, 'y', UP), across)  4.74 us
    ppermute x1, starting transfers between devices, shards(): b = lax.ppermute(block, 'zh', SWAP)  3.58 us
    ppermute x2, starting transfers between devices, shards(): r1, r2 = (lax.ppermute(r0, 'x', UP), lax.ppermute(r0, 'x', DOWN))  3.31 us
  transfers between devices with their start and end apart: 22, of which 5 were waited for; matrix products, arithmetic and copies ran while one was open for 1% of the time, Pallas kernels for 18%

profile of v4, /device:TPU:0, one launch (start us, length us, event | category | flops | bytes accessed | tf_op | source)
XLA Modules:
  0.0 101.3 jit_solution(5196977543518009950)
XLA Ops:
  0.6 1.0 shard_map.41.refs_8_
  1.7 2.1 %collective-permute-start.8 = (f32[192,256]{1,0:T(8,128)}, f32[192,256]{1,0:T(8,128)S(1)}, u32[]{:S(2)}, u32[]{:S(2)}) collective-permute-start(f32[192,256]{1,0:T(8,128)} %z_ref.2), channel_id=1, source_target_pairs={{0,16},{16,0},{1,17},{17,1},{2,18},{18,2},{3,19},{19,3},{4,20},{20... | collective-permute-start | bytes 589832 | tf_op jit(solution)/shard_map/ppermute | solution.py:342
  3.7 3.6 %collective-permute-start = (f32[200,256]{1,0:T(8,128)S(1)}, f32[200,256]{1,0:T(8,128)S(1)}, u32[]{:S(2)}, u32[]{:S(2)}) collective-permute-start(f32[200,256]{1,0:T(8,128)S(1)} %shard_map.41.refs_8_), channel_id=1, source_target_pairs={{0,2},{2,0},{1,3},{3,1},{4,6},{6,4},{5,7},{7,5},{8,10},{10,8},{9,1... | collective-permute-start | bytes 614408 | tf_op jit(solution)/shard_map/ppermute | solution.py:343
  7.3 2.4 %collective-permute-done.8.refs_4_ = f32[192,256]{1,0:T(8,128)S(1)} collective-permute-done((f32[192,256]{1,0:T(8,128)}, f32[192,256]{1,0:T(8,128)S(1)}, u32[]{:S(2)}, u32[]{:S(2)}) %collective-permute-start.8) | collective-permute-done | bytes 196640 | tf_op jit(solution)/shard_map/ppermute | solution.py:342
  10.7 1.7 %collective-permute-start.9 = (f32[384,256]{1,0:T(8,128)S(1)}, f32[384,256]{1,0:T(8,128)S(1)}, u32[]{:S(2)}, u32[]{:S(2)}) collective-permute-start(f32[384,256]{1,0:T(8,128)S(1)} %constant_dynamic-update-slice_fusion.2), channel_id=1, source_target_pairs={{0,32},{32,64},{64,96},{96,0},{1,33},{33,65},{65,97},{97,1},{2,34}... | collective-permute-start | bytes 1179656 | tf_op jit(solution)/shard_map/ppermute | solution.py:345
  12.4 1.6 %collective-permute-start.10 = (f32[384,256]{1,0:T(8,128)S(1)}, f32[384,256]{1,0:T(8,128)S(1)}, u32[]{:S(2)}, u32[]{:S(2)}) collective-permute-start(f32[384,256]{1,0:T(8,128)S(1)} %constant_dynamic-update-slice_fusion.2), channel_id=1, source_target_pairs={{0,96},{32,0},{64,32},{96,64},{1,97},{33,1},{65,33},{97,65},{2,98}... | collective-permute-start | bytes 1179656 | tf_op jit(solution)/shard_map/ppermute | solution.py:345
  14.0 2.6 %collective-permute-done.refs_9_ = f32[200,256]{1,0:T(8,128)S(1)} collective-permute-done((f32[200,256]{1,0:T(8,128)S(1)}, f32[200,256]{1,0:T(8,128)S(1)}, u32[]{:S(2)}, u32[]{:S(2)}) %collective-permute-start) | collective-permute-done | bytes 204832 | tf_op jit(solution)/shard_map/ppermute | solution.py:343
  16.7 1.6 %collective-permute-start.3 = (f32[400,256]{1,0:T(8,128)S(1)}, f32[400,256]{1,0:T(8,128)S(1)}, u32[]{:S(2)}, u32[]{:S(2)}) collective-permute-start(f32[400,256]{1,0:T(8,128)S(1)} %constant_dynamic-update-slice_fusion), channel_id=1, source_target_pairs={{0,4},{4,8},{8,12},{12,0},{1,5},{5,9},{9,13},{13,1},{2,6},{6,10},{... | collective-permute-start | bytes 1228808 | tf_op jit(solution)/shard_map/ppermute | solution.py:348
  18.2 1.7 %collective-permute-start.1 = (f32[400,256]{1,0:T(8,128)S(1)}, f32[400,256]{1,0:T(8,128)S(1)}, u32[]{:S(2)}, u32[]{:S(2)}) collective-permute-start(f32[400,256]{1,0:T(8,128)S(1)} %constant_dynamic-update-slice_fusion), channel_id=1, source_target_pairs={{0,12},{4,0},{8,4},{12,8},{1,13},{5,1},{9,5},{13,9},{2,14},{6,2},{... | collective-permute-start | bytes 1228808 | tf_op jit(solution)/shard_map/ppermute | solution.py:348
  20.0 1.4 %collective-permute-done.9 = f32[384,256]{1,0:T(8,128)S(1)} collective-permute-done((f32[384,256]{1,0:T(8,128)S(1)}, f32[384,256]{1,0:T(8,128)S(1)}, u32[]{:S(2)}, u32[]{:S(2)}) %collective-permute-start.9) | collective-permute-done | bytes 393248 | tf_op jit(solution)/shard_map/ppermute | solution.py:345
  21.8 3.0 %collective-permute-start.12 = (f32[192,256]{1,0:T(8,128)S(1)}, f32[192,256]{1,0:T(8,128)S(1)}, u32[]{:S(2)}, u32[]{:S(2)}) collective-permute-start(f32[192,256]{1,0:T(8,128)S(1)} %get-tuple-element.80.refs_6_), channel_id=1, source_target_pairs={{0,96},{32,0},{64,32},{96,64},{1,97},{33,1},{65,33},{97,65},{2,98}... | collective-permute-start | bytes 589832 | tf_op jit(solution)/shard_map/ppermute | solution.py:346
  24.8 4.9 %collective-permute-done.3 = f32[400,256]{1,0:T(8,128)S(1)} collective-permute-done((f32[400,256]{1,0:T(8,128)S(1)}, f32[400,256]{1,0:T(8,128)S(1)}, u32[]{:S(2)}, u32[]{:S(2)}) %collective-permute-start.3) | collective-permute-done | bytes 409632 | tf_op jit(solution)/shard_map/ppermute | solution.py:348
  30.2 3.0 %collective-permute-start.5 = (f32[200,256]{1,0:T(8,128)S(1)}, f32[200,256]{1,0:T(8,128)S(1)}, u32[]{:S(2)}, u32[]{:S(2)}) collective-permute-start(f32[200,256]{1,0:T(8,128)S(1)} %get-tuple-element.78.refs_1_), channel_id=1, source_target_pairs={{0,12},{4,0},{8,4},{12,8},{1,13},{5,1},{9,5},{13,9},{2,14},{6,2},{... | collective-permute-start | bytes 614408 | tf_op jit(solution)/shard_map/ppermute | solution.py:349
  33.8 4.9 %shard_map.42 = (f32[12,1536,256]{2,1,0:T(8,128)}, bf16[3072,512]{1,0:T(8,128)(2,1)}, f32[4,1,768]{2,1,0:T(1,128)}, f32[1,1,768]{2,1,0:T(1,128)S(1)}, f32[8,128]...) custom-call(f32[192,256]{1,0:T(8,128)S(1)} %copy-done, ...), custom_call_target="tpu_custom_call" | custom-call | flops 1811939328 | bytes 4718592 | tf_op jit(solution)/shard_map/pallas_call | solution.py:176
  39.4 4.6 %shard_map.43 = (f32[12,1536,256]{2,1,0:T(8,128)}, bf16[3072,512]{1,0:T(8,128)(2,1)}, f32[4,1,768]{2,1,0:T(1,128)}, f32[1,1,768]{2,1,0:T(1,128)S(1)}, f32[8,128]{1,0:T(8,128)S(1)}, /*index=5*/f32[1536,128]{1,0:T(8,128)S(1)}) custom-call(f32[200,256]{1,0:T(8,128)S(1)} %get-tuple-element.73.refs_0_, ...), custom_call_target="tpu_custom_call", output_to_operand_aliasing={{0}: (8, {}), {1}: (9, {}), {2}: (10, {})} | custom-call | flops 1811939328 | bytes 4718592 | tf_op jit(solution)/shard_map/pallas_call | solution.py:176
  44.0 8.9 %shard_map.44 = (f32[12,1536,256]{2,1,0:T(8,128)}, bf16[3072,512]{1,0:T(8,128)(2,1)}, f32[4,1,768]{2,1,0:T(1,128)}, f32[128,1,512]{2,1,0:T(1,128)S(1)}) custom-call(f32[200,256]{1,0:T(8,128)S(1)} %get-tuple-element.79.refs_0_, f32[200,256]{1,0:T(8,128)S(1)} %get-tuple-element.78.refs_1_, ...), custom_call_target="tpu_custom_call", output_to_operand_aliasing={{0}: (12, {}), {1}: (13, {}), {2}: (14, {})} | custom-call | flops 3623878656 | bytes 9437184 | tf_op jit(solution)/shard_map/pallas_call | solution.py:176
  52.9 16.8 %all_to_all.5.sums_ref = f32[128,1,512]{2,1,0:T(1,128)S(1)} all-to-all(f32[128,1,512]{2,1,0:T(1,128)S(1)} %get-tuple-element.52), channel_id=1, replica_groups=mesh['y'=4,'zl'=2,'x'=4,'zh'=2,'core'=2] {'y','zl','x','zh','core'}, dimensions={0} | all-to-all | bytes 524288 | tf_op jit(solution)/shard_map/all_to_all | solution.py:356
  69.7 7.8 %shard_map.45 = (f32[200,256]{1,0:T(8,128)S(1)}, f32[200,256]{1,0:T(8,128)S(1)}, f32[200,256]{1,0:T(8,128)S(1)}, f32[200,256]{1,0:T(8,128)S(1)}, f32[1536,128]{1...) custom-call(f32[128,1,512]{2,1,0:T(1,128)S(1)} %all_to_all.5.sums_ref, ...), custom_call_target="tpu_custom_call" | custom-call | flops 3623878656 | bytes 9437184 | tf_op jit(solution)/shard_map/pallas_call | solution.py:275
  77.5 1.2 %collective-permute-start.15 = (f32[200,256]{1,0:T(8,128)S(1)}, f32[200,256]{1,0:T(8,128)S(1)}, u32[]{:S(2)}, u32[]{:S(2)}) collective-permute-start(f32[200,256]{1,0:T(8,128)S(1)} %get-tuple-element.58), channel_id=1, source_target_pairs={{0,96},{32,0},{64,32},{96,64},{1,97},{33,1},{65,33},{97,65},{2,98}... | collective-permute-start | bytes 614408 | tf_op jit(solution)/shard_map/ppermute | solution.py:336
  80.3 5.9 %shard_map.47 = (f32[200,256]{1,0:T(8,128)S(1)}, f32[200,256]{1,0:T(8,128)S(1)}, f32[200,256]{1,0:T(8,128)S(1)}) custom-call(f32[1,256]{1,0:T(1,128)S(1)} %get-tuple-element.61.sums_ref, f32[12,1536,256]{2,1,0:T(8,128)} %get-tuple-element.53.refs_0_.refs_1_.refs_2_.refs_3_, f32[12,1536,256]{2,1,0:T(8,128)} %get-tuple-element.53.refs_0_.refs_1_.refs_2_.refs_3_, ...), custom_call_target="tpu_custom_call" | custom-call | flops 2717908992 | bytes 7077888 | tf_op jit(solution)/shard_map/pallas_call | solution.py:275
  86.3 2.7 %collective-permute-start.18 = (f32[200,256]{1,0:T(8,128)S(1)}, f32[200,256]{1,0:T(8,128)S(1)}, u32[]{:S(2)}, u32[]{:S(2)}) collective-permute-start(f32[200,256]{1,0:T(8,128)S(1)} %get-tuple-element.64), channel_id=1, source_target_pairs={{0,96},{32,0},{64,32},{96,64},{1,97},{33,1},{65,33},{97,65},{2,98}... | collective-permute-start | bytes 614408 | tf_op jit(solution)/shard_map/ppermute | solution.py:336
  88.9 2.2 %collective-permute-start.20 = (f32[200,256]{1,0:T(8,128)S(1)}, f32[200,256]{1,0:T(8,128)S(1)}, u32[]{:S(2)}, u32[]{:S(2)}) collective-permute-start(f32[200,256]{1,0:T(8,128)S(1)} %get-tuple-element.66), channel_id=1, source_target_pairs={{0,64},{32,96},{64,0},{96,32},{1,65},{33,97},{65,1},{97,33},{2,66}... | collective-permute-start | bytes 614408 | tf_op jit(solution)/shard_map/ppermute | solution.py:335
  92.2 3.3 %shard_map.46.refs_0_ = f32[200,256]{1,0:T(8,128)S(1)} custom-call(f32[1,256]{1,0:T(1,128)S(1)} %get-tuple-element.61.sums_ref, f32[12,1536,256]{2,1,0:T(8,128)} %get-tuple-element.53.refs_0_.refs_1_.refs_2_.refs_3_, bf16[3072,512]{1,0:T(8,128)(2,1)} %get-tuple-element.54.refs_4_.refs_1_.refs_3_, f32[4,1,768]{2,1,0:T(1,128)} %get-tuple-element.55.refs_5_.refs_2_.refs_4_, ...), custom_call_target="tpu_custom_call" | custom-call | flops 905969664 | bytes 2359296 | tf_op jit(solution)/shard_map/pallas_call | solution.py:275
  95.5 4.7 %collective-permute-done.19.refs_2_ = f32[200,256]{1,0:T(8,128)S(1)} collective-permute-done((f32[200,256]{1,0:T(8,128)S(1)}, f32[200,256]{1,0:T(8,128)S(1)}, u32[]{:S(2)}, u32[]{:S(2)}) %collective-permute-start.19) | collective-permute-done | bytes 204832 | tf_op jit(solution)/shard_map/ppermute | solution.py:336
  (43 shorter events, 6.6 us)
Async XLA Ops:
  0.6 33.2 %copy-start = (f32[192,256]{1,0:T(8,128)S(1)}, f32[192,256]{1,0:T(8,128)}, u32[]{:S(2)}) copy-start(f32[192,256]{1,0:T(8,128)} %z_ref.2) | copy-start | bytes 589828
  1.7 8.0 %collective-permute-start.8 = (f32[192,256]{1,0:T(8,128)}, f32[192,256]{1,0:T(8,128)S(1)}, u32[]{:S(2)}, u32[]{:S(2)}) collective-permute-start(f32[192,256]{1,0:T(8,128)} %z_ref.2), channel_id=1, source_target_pairs={{0,16},{16,0},{1,17},{17,1},{2,18},{18,2},{3,19},{19,3},{4,20},{20... | collective-permute-start | bytes 589832 | tf_op jit(solution)/shard_map/ppermute | solution.py:342
  3.7 12.8 %collective-permute-start = (f32[200,256]{1,0:T(8,128)S(1)}, f32[200,256]{1,0:T(8,128)S(1)}, u32[]{:S(2)}, u32[]{:S(2)}) collective-permute-start(f32[200,256]{1,0:T(8,128)S(1)} %shard_map.41.refs_8_), channel_id=1, source_target_pairs={{0,2},{2,0},{1,3},{3,1},{4,6},{6,4},{5,7},{7,5},{8,10},{10,8},{9,1... | collective-permute-start | bytes 614408 | tf_op jit(solution)/shard_map/ppermute | solution.py:343
  10.7 10.7 %collective-permute-start.9 = (f32[384,256]{1,0:T(8,128)S(1)}, f32[384,256]{1,0:T(8,128)S(1)}, u32[]{:S(2)}, u32[]{:S(2)}) collective-permute-start(f32[384,256]{1,0:T(8,128)S(1)} %constant_dynamic-update-slice_fusion.2), channel_id=1, source_target_pairs={{0,32},{32,64},{64,96},{96,0},{1,33},{33,65},{65,97},{97,1},{2,34}... | collective-permute-start | bytes 1179656 | tf_op jit(solution)/shard_map/ppermute | solution.py:345
  12.4 9.3 %collective-permute-start.10 = (f32[384,256]{1,0:T(8,128)S(1)}, f32[384,256]{1,0:T(8,128)S(1)}, u32[]{:S(2)}, u32[]{:S(2)}) collective-permute-start(f32[384,256]{1,0:T(8,128)S(1)} %constant_dynamic-update-slice_fusion.2), channel_id=1, source_target_pairs={{0,96},{32,0},{64,32},{96,64},{1,97},{33,1},{65,33},{97,65},{2,98}... | collective-permute-start | bytes 1179656 | tf_op jit(solution)/shard_map/ppermute | solution.py:345
  16.6 16.6 %collective-permute-start.13 = (f32[400,256]{1,0:T(8,128)S(1)}, f32[400,256]{1,0:T(8,128)S(1)}, u32[]{:S(2)}, u32[]{:S(2)}) collective-permute-start(f32[400,256]{1,0:T(8,128)S(1)} %constant_dynamic-update-slice_fusion), channel_id=1, source_target_pairs={{0,1},{1,0},{2,3},{3,2},{4,5},{5,4},{6,7},{7,6},{8,9},{9,8},{10,11... | collective-permute-start | bytes 1228808 | tf_op jit(solution)/shard_map/ppermute | solution.py:350
  16.7 13.1 %collective-permute-start.3 = (f32[400,256]{1,0:T(8,128)S(1)}, f32[400,256]{1,0:T(8,128)S(1)}, u32[]{:S(2)}, u32[]{:S(2)}) collective-permute-start(f32[400,256]{1,0:T(8,128)S(1)} %constant_dynamic-update-slice_fusion), channel_id=1, source_target_pairs={{0,4},{4,8},{8,12},{12,0},{1,5},{5,9},{9,13},{13,1},{2,6},{6,10},{... | collective-permute-start | bytes 1228808 | tf_op jit(solution)/shard_map/ppermute | solution.py:348
  18.2 11.9 %collective-permute-start.1 = (f32[400,256]{1,0:T(8,128)S(1)}, f32[400,256]{1,0:T(8,128)S(1)}, u32[]{:S(2)}, u32[]{:S(2)}) collective-permute-start(f32[400,256]{1,0:T(8,128)S(1)} %constant_dynamic-update-slice_fusion), channel_id=1, source_target_pairs={{0,12},{4,0},{8,4},{12,8},{1,13},{5,1},{9,5},{13,9},{2,14},{6,2},{... | collective-permute-start | bytes 1228808 | tf_op jit(solution)/shard_map/ppermute | solution.py:348
  21.4 11.8 %collective-permute-start.11 = (f32[192,256]{1,0:T(8,128)S(1)}, f32[192,256]{1,0:T(8,128)S(1)}, u32[]{:S(2)}, u32[]{:S(2)}) collective-permute-start(f32[192,256]{1,0:T(8,128)S(1)} %get-tuple-element.83.refs_1_), channel_id=1, source_target_pairs={{0,32},{32,64},{64,96},{96,0},{1,33},{33,65},{65,97},{97,1},{2,34}... | collective-permute-start | bytes 589832 | tf_op jit(solution)/shard_map/ppermute | solution.py:346
  21.8 12.1 %collective-permute-start.12 = (f32[192,256]{1,0:T(8,128)S(1)}, f32[192,256]{1,0:T(8,128)S(1)}, u32[]{:S(2)}, u32[]{:S(2)}) collective-permute-start(f32[192,256]{1,0:T(8,128)S(1)} %get-tuple-element.80.refs_6_), channel_id=1, source_target_pairs={{0,96},{32,0},{64,32},{96,64},{1,97},{33,1},{65,33},{97,65},{2,98}... | collective-permute-start | bytes 589832 | tf_op jit(solution)/shard_map/ppermute | solution.py:346
  29.8 9.0 %collective-permute-start.4 = (f32[200,256]{1,0:T(8,128)S(1)}, f32[200,256]{1,0:T(8,128)S(1)}, u32[]{:S(2)}, u32[]{:S(2)}) collective-permute-start(f32[200,256]{1,0:T(8,128)S(1)} %get-tuple-element.73.refs_0_), channel_id=1, source_target_pairs={{0,4},{4,8},{8,12},{12,0},{1,5},{5,9},{9,13},{13,1},{2,6},{6,10},{... | collective-permute-start | bytes 614408 | tf_op jit(solution)/shard_map/ppermute | solution.py:349
  30.2 8.7 %collective-permute-start.5 = (f32[200,256]{1,0:T(8,128)S(1)}, f32[200,256]{1,0:T(8,128)S(1)}, u32[]{:S(2)}, u32[]{:S(2)}) collective-permute-start(f32[200,256]{1,0:T(8,128)S(1)} %get-tuple-element.78.refs_1_), channel_id=1, source_target_pairs={{0,12},{4,0},{8,4},{12,8},{1,13},{5,1},{9,5},{13,9},{2,14},{6,2},{... | collective-permute-start | bytes 614408 | tf_op jit(solution)/shard_map/ppermute | solution.py:349
  33.2 6.1 %collective-permute-start.14 = (f32[400,256]{1,0:T(8,128)S(1)}, f32[400,256]{1,0:T(8,128)S(1)}, u32[]{:S(2)}, u32[]{:S(2)}) collective-permute-start(f32[400,256]{1,0:T(8,128)S(1)} %collective-permute-done.3), channel_id=1, source_target_pairs={{0,1},{1,0},{2,3},{3,2},{4,5},{5,4},{6,7},{7,6},{8,9},{9,8},{10,11... | collective-permute-start | bytes 1228808 | tf_op jit(solution)/shard_map/ppermute | solution.py:350
  33.2 6.1 %collective-permute-start.2 = (f32[400,256]{1,0:T(8,128)S(1)}, f32[400,256]{1,0:T(8,128)S(1)}, u32[]{:S(2)}, u32[]{:S(2)}) collective-permute-start(f32[400,256]{1,0:T(8,128)S(1)} %collective-permute-done.1), channel_id=1, source_target_pairs={{0,1},{1,0},{2,3},{3,2},{4,5},{5,4},{6,7},{7,6},{8,9},{9,8},{10,11... | collective-permute-start | bytes 1228808 | tf_op jit(solution)/shard_map/ppermute | solution.py:350
  38.8 5.2 %collective-permute-start.6 = (f32[200,256]{1,0:T(8,128)S(1)}, f32[200,256]{1,0:T(8,128)S(1)}, u32[]{:S(2)}, u32[]{:S(2)}) collective-permute-start(f32[200,256]{1,0:T(8,128)S(1)} %collective-permute-done.4.refs_4_), channel_id=1, source_target_pairs={{0,1},{1,0},{2,3},{3,2},{4,5},{5,4},{6,7},{7,6},{8,9},{9,8},{10,11... | collective-permute-start | bytes 614408 | tf_op jit(solution)/shard_map/ppermute | solution.py:350
  38.8 5.1 %collective-permute-start.7 = (f32[200,256]{1,0:T(8,128)S(1)}, f32[200,256]{1,0:T(8,128)S(1)}, u32[]{:S(2)}, u32[]{:S(2)}) collective-permute-start(f32[200,256]{1,0:T(8,128)S(1)} %collective-permute-done.5.refs_5_), channel_id=1, source_target_pairs={{0,1},{1,0},{2,3},{3,2},{4,5},{5,4},{6,7},{7,6},{8,9},{9,8},{10,11... | collective-permute-start | bytes 614408 | tf_op jit(solution)/shard_map/ppermute | solution.py:350
  77.5 11.4 %collective-permute-start.15 = (f32[200,256]{1,0:T(8,128)S(1)}, f32[200,256]{1,0:T(8,128)S(1)}, u32[]{:S(2)}, u32[]{:S(2)}) collective-permute-start(f32[200,256]{1,0:T(8,128)S(1)} %get-tuple-element.58), channel_id=1, source_target_pairs={{0,96},{32,0},{64,32},{96,64},{1,97},{33,1},{65,33},{97,65},{2,98}... | collective-permute-start | bytes 614408 | tf_op jit(solution)/shard_map/ppermute | solution.py:336
  78.7 12.5 %collective-permute-start.16 = (f32[200,256]{1,0:T(8,128)S(1)}, f32[200,256]{1,0:T(8,128)S(1)}, u32[]{:S(2)}, u32[]{:S(2)}) collective-permute-start(f32[200,256]{1,0:T(8,128)S(1)} %get-tuple-element.59), channel_id=1, source_target_pairs={{0,32},{32,64},{64,96},{96,0},{1,33},{33,65},{65,97},{97,1},{2,34}... | collective-permute-start | bytes 614408 | tf_op jit(solution)/shard_map/ppermute | solution.py:336
  79.6 11.6 %collective-permute-start.17 = (f32[200,256]{1,0:T(8,128)S(1)}, f32[200,256]{1,0:T(8,128)S(1)}, u32[]{:S(2)}, u32[]{:S(2)}) collective-permute-start(f32[200,256]{1,0:T(8,128)S(1)} %get-tuple-element.60), channel_id=1, source_target_pairs={{0,64},{32,96},{64,0},{96,32},{1,65},{33,97},{65,1},{97,33},{2,66}... | collective-permute-start | bytes 614408 | tf_op jit(solution)/shard_map/ppermute | solution.py:335
  86.3 9.2 %collective-permute-start.18 = (f32[200,256]{1,0:T(8,128)S(1)}, f32[200,256]{1,0:T(8,128)S(1)}, u32[]{:S(2)}, u32[]{:S(2)}) collective-permute-start(f32[200,256]{1,0:T(8,128)S(1)} %get-tuple-element.64), channel_id=1, source_target_pairs={{0,96},{32,0},{64,32},{96,64},{1,97},{33,1},{65,33},{97,65},{2,98}... | collective-permute-start | bytes 614408 | tf_op jit(solution)/shard_map/ppermute | solution.py:336
  88.9 11.3 %collective-permute-start.19 = (f32[200,256]{1,0:T(8,128)S(1)}, f32[200,256]{1,0:T(8,128)S(1)}, u32[]{:S(2)}, u32[]{:S(2)}) collective-permute-start(f32[200,256]{1,0:T(8,128)S(1)} %get-tuple-element.65), channel_id=1, source_target_pairs={{0,32},{32,64},{64,96},{96,0},{1,33},{33,65},{65,97},{97,1},{2,34}... | collective-permute-start | bytes 614408 | tf_op jit(solution)/shard_map/ppermute | solution.py:336
  88.9 11.3 %collective-permute-start.20 = (f32[200,256]{1,0:T(8,128)S(1)}, f32[200,256]{1,0:T(8,128)S(1)}, u32[]{:S(2)}, u32[]{:S(2)}) collective-permute-start(f32[200,256]{1,0:T(8,128)S(1)} %get-tuple-element.66), channel_id=1, source_target_pairs={{0,64},{32,96},{64,0},{96,32},{1,65},{33,97},{65,1},{97,33},{2,66}... | collective-permute-start | bytes 614408 | tf_op jit(solution)/shard_map/ppermute | solution.py:335
  91.3 9.0 %collective-permute-start.21 = (f32[200,256]{1,0:T(8,128)S(1)}, f32[200,256]{1,0:T(8,128)S(1)}, u32[]{:S(2)}, u32[]{:S(2)}) collective-permute-start(f32[200,256]{1,0:T(8,128)S(1)} %add_add_fusion), channel_id=1, source_target_pairs={{0,16},{16,0},{1,17},{17,1},{2,18},{18,2},{3,19},{19,3},{4,20},{20... | collective-permute-start | bytes 614408 | tf_op jit(solution)/shard_map/ppermute | solution.py:363

commit v5 on v4

--- a/solution.py
+++ b/solution.py
@@ -333,7 +333,7 @@
 
 def over_y(down, up, across):
     across = lax.ppermute(across, "y", [(i, (i + 2) % 4) for i in range(4)])
-    return lax.ppermute(down, "y", DOWN), lax.ppermute(up, "y", UP), across
+    return across, lax.ppermute(down, "y", DOWN), lax.ppermute(up, "y", UP)
 
 
 def shards(projections, partner):
@@ -341,7 +341,7 @@
     z, block = lax.optimization_barrier((projections, pack(*here)))
     a = lax.ppermute(z, "zl", SWAP)
     b = lax.ppermute(block, "zh", SWAP)
-    c0 = jnp.concatenate([a, z])
+    c0 = jnp.concatenate([a, block[:PER]])
     c1, c2 = lax.ppermute(c0, "y", UP), lax.ppermute(c0, "y", DOWN)
     c3z, c3a = lax.ppermute(c1[PER:], "y", UP), lax.ppermute(c2[:PER], "y", DOWN)
     r0 = jnp.concatenate([b, block])

time: 101 us -> 101 us (level)
    ppermute x4, waiting for transfers between devices: 4.74 us -> 2.96 us  [over_y(): return (across, lax.ppermute(down, 'y', DOWN), lax.ppermute(up, 'y', UP))]
  transfers between devices with their start and end apart: 22 -> 22, of which waited for: 5 -> 6; matrix products, arithmetic and copies ran while one was open for 1% -> 0% of each run, Pallas kernels for 18% -> 19%
where the time goes in v5:
time: 101 us; the launch traced here: 100 us
  Pallas kernels  37.3 us (37%)
  starting transfers between devices  28.9 us (29%)
  blocking collectives  16.8 us (17%)
  waiting for transfers between devices  16.2 us (16%)
    pallas_call x3, Pallas kernels, scores(): pl.pallas_call(functools.partial(score_kernel, start, steps), grid=(steps...  18.4 us
    pallas_call x3, Pallas kernels, gradients(): pl.pallas_call(functools.partial(gradient_kernel, slots, first), grid=(ST...  17 us
    all_to_all x1, blocking collectives, shards(): sums = lax.all_to_all(sums, ALL, 0, 0, tiled=True)  16.8 us
    ppermute x2, waiting for transfers between devices, shards(): r1, r2 = (lax.ppermute(r0, 'x', UP), lax.ppermute(r0, 'x', DOWN))  5.89 us
    ppermute x4, starting transfers between devices, over_y(): return (across, lax.ppermute(down, 'y', DOWN), lax.ppermute(up, 'y', UP))  4.62 us
    ppermute x1, starting transfers between devices, shards(): b = lax.ppermute(block, 'zh', SWAP)  3.58 us
    ppermute x1, waiting for transfers between devices, shards(): b = lax.ppermute(block, 'zh', SWAP)  3.5 us
    ppermute x2, starting transfers between devices, shards(): r1, r2 = (lax.ppermute(r0, 'x', UP), lax.ppermute(r0, 'x', DOWN))  3.31 us
  transfers between devices with their start and end apart: 22, of which 6 were waited for; matrix products, arithmetic and copies ran while one was open for 0% of the time, Pallas kernels for 19%

profile of v5, /device:TPU:0, one launch (start us, length us, event | category | flops | bytes accessed | tf_op | source)
XLA Modules:
  0.0 100.4 jit_solution(8230996799251207248)
XLA Ops:
  0.6 1.0 %shard_map.41.refs_8_ = f32[200,256]{1,0:T(8,128)S(1)} custom-call(f32[192,256]{1,0:T(8,128)} %z_ref.2, s32[192]{0:T(256)} %partner_ref.1), custom_call_target="tpu_custom_call" | custom-call | tf_op jit(solution)/shard_map/pallas_call | solution.py:320
  1.7 2.1 %collective-permute-start.8 = (f32[192,256]{1,0:T(8,128)}, f32[192,256]{1,0:T(8,128)S(1)}, u32[]{:S(2)}, u32[]{:S(2)}) collective-permute-start(f32[192,256]{1,0:T(8,128)} %z_ref.2), channel_id=1, source_target_pairs={{0,16},{16,0},{1,17},{17,1},{2,18},{18,2},{3,19},{19,3},{4,20},{20... | collective-permute-start | bytes 589832 | tf_op jit(solution)/shard_map/ppermute | solution.py:342
  3.7 3.6 %collective-permute-start = (f32[200,256]{1,0:T(8,128)S(1)}, f32[200,256]{1,0:T(8,128)S(1)}, u32[]{:S(2)}, u32[]{:S(2)}) collective-permute-start(f32[200,256]{1,0:T(8,128)S(1)} %shard_map.41.refs_8_), channel_id=1, source_target_pairs={{0,2},{2,0},{1,3},{3,1},{4,6},{6,4},{5,7},{7,5},{8,10},{10,8},{9,1... | collective-permute-start | bytes 614408 | tf_op jit(solution)/shard_map/ppermute | solution.py:343
  7.3 2.4 %collective-permute-done.8.refs_4_ = f32[192,256]{1,0:T(8,128)S(1)} collective-permute-done((f32[192,256]{1,0:T(8,128)}, f32[192,256]{1,0:T(8,128)S(1)}, u32[]{:S(2)}, u32[]{:S(2)}) %collective-permute-start.8) | collective-permute-done | bytes 196640 | tf_op jit(solution)/shard_map/ppermute | solution.py:342
  9.7 1.7 %collective-permute-start.9 = (f32[384,256]{1,0:T(8,128)S(1)}, f32[384,256]{1,0:T(8,128)S(1)}, u32[]{:S(2)}, u32[]{:S(2)}) collective-permute-start(f32[384,256]{1,0:T(8,128)S(1)} %pad_maximum_fusion), channel_id=1, source_target_pairs={{0,32},{32,64},{64,96},{96,0},{1,33},{33,65},{65,97},{97,1},{2,34}... | collective-permute-start | bytes 1179656 | tf_op jit(solution)/shard_map/ppermute | solution.py:345
  11.5 1.6 %collective-permute-start.10 = (f32[384,256]{1,0:T(8,128)S(1)}, f32[384,256]{1,0:T(8,128)S(1)}, u32[]{:S(2)}, u32[]{:S(2)}) collective-permute-start(f32[384,256]{1,0:T(8,128)S(1)} %pad_maximum_fusion), channel_id=1, source_target_pairs={{0,96},{32,0},{64,32},{96,64},{1,97},{33,1},{65,33},{97,65},{2,98}... | collective-permute-start | bytes 1179656 | tf_op jit(solution)/shard_map/ppermute | solution.py:345
  13.0 3.5 %collective-permute-done.refs_9_ = f32[200,256]{1,0:T(8,128)S(1)} collective-permute-done((f32[200,256]{1,0:T(8,128)S(1)}, f32[200,256]{1,0:T(8,128)S(1)}, u32[]{:S(2)}, u32[]{:S(2)}) %collective-permute-start) | collective-permute-done | bytes 204832 | tf_op jit(solution)/shard_map/ppermute | solution.py:343
  16.7 1.6 %collective-permute-start.3 = (f32[400,256]{1,0:T(8,128)S(1)}, f32[400,256]{1,0:T(8,128)S(1)}, u32[]{:S(2)}, u32[]{:S(2)}) collective-permute-start(f32[400,256]{1,0:T(8,128)S(1)} %constant_dynamic-update-slice_fusion), channel_id=1, source_target_pairs={{0,4},{4,8},{8,12},{12,0},{1,5},{5,9},{9,13},{13,1},{2,6},{6,10},{... | collective-permute-start | bytes 1228808 | tf_op jit(solution)/shard_map/ppermute | solution.py:348
  18.2 1.7 %collective-permute-start.1 = (f32[400,256]{1,0:T(8,128)S(1)}, f32[400,256]{1,0:T(8,128)S(1)}, u32[]{:S(2)}, u32[]{:S(2)}) collective-permute-start(f32[400,256]{1,0:T(8,128)S(1)} %constant_dynamic-update-slice_fusion), channel_id=1, source_target_pairs={{0,12},{4,0},{8,4},{12,8},{1,13},{5,1},{9,5},{13,9},{2,14},{6,2},{... | collective-permute-start | bytes 1228808 | tf_op jit(solution)/shard_map/ppermute | solution.py:348
  20.5 1.2 %collective-permute-start.11 = (f32[192,256]{1,0:T(8,128)S(1)}, f32[192,256]{1,0:T(8,128)S(1)}, u32[]{:S(2)}, u32[]{:S(2)}) collective-permute-start(f32[192,256]{1,0:T(8,128)S(1)} %get-tuple-element.83.refs_1_), channel_id=1, source_target_pairs={{0,32},{32,64},{64,96},{96,0},{1,33},{33,65},{65,97},{97,1},{2,34}... | collective-permute-start | bytes 589832 | tf_op jit(solution)/shard_map/ppermute | solution.py:346
  21.7 2.2 %collective-permute-start.12 = (f32[192,256]{1,0:T(8,128)S(1)}, f32[192,256]{1,0:T(8,128)S(1)}, u32[]{:S(2)}, u32[]{:S(2)}) collective-permute-start(f32[192,256]{1,0:T(8,128)S(1)} %get-tuple-element.80.refs_6_), channel_id=1, source_target_pairs={{0,96},{32,0},{64,32},{96,64},{1,97},{33,1},{65,33},{97,65},{2,98}... | collective-permute-start | bytes 589832 | tf_op jit(solution)/shard_map/ppermute | solution.py:346
  23.9 5.9 %collective-permute-done.3 = f32[400,256]{1,0:T(8,128)S(1)} collective-permute-done((f32[400,256]{1,0:T(8,128)S(1)}, f32[400,256]{1,0:T(8,128)S(1)}, u32[]{:S(2)}, u32[]{:S(2)}) %collective-permute-start.3) | collective-permute-done | bytes 409632 | tf_op jit(solution)/shard_map/ppermute | solution.py:348
  30.2 3.0 %collective-permute-start.5 = (f32[200,256]{1,0:T(8,128)S(1)}, f32[200,256]{1,0:T(8,128)S(1)}, u32[]{:S(2)}, u32[]{:S(2)}) collective-permute-start(f32[200,256]{1,0:T(8,128)S(1)} %get-tuple-element.78.refs_1_), channel_id=1, source_target_pairs={{0,12},{4,0},{8,4},{12,8},{1,13},{5,1},{9,5},{13,9},{2,14},{6,2},{... | collective-permute-start | bytes 614408 | tf_op jit(solution)/shard_map/ppermute | solution.py:349
  33.8 4.9 %shard_map.42 = (f32[12,1536,256]{2,1,0:T(8,128)}, bf16[3072,512]{1,0:T(8,128)(2,1)}, f32[4,1,768]{2,1,0:T(1,128)}, f32[1,1,768]{2,1,0:T(1,128)S(1)}, f32[8,128]...) custom-call(f32[192,256]{1,0:T(8,128)S(1)} %copy-done, ...), custom_call_target="tpu_custom_call" | custom-call | flops 1811939328 | bytes 4718592 | tf_op jit(solution)/shard_map/pallas_call | solution.py:176
  39.4 4.6 %shard_map.43 = (f32[12,1536,256]{2,1,0:T(8,128)}, bf16[3072,512]{1,0:T(8,128)(2,1)}, f32[4,1,768]{2,1,0:T(1,128)}, f32[1,1,768]{2,1,0:T(1,128)S(1)}, f32[8,128]{1,0:T(8,128)S(1)}, /*index=5*/f32[1536,128]{1,0:T(8,128)S(1)}) custom-call(f32[200,256]{1,0:T(8,128)S(1)} %get-tuple-element.73.refs_0_, ...), custom_call_target="tpu_custom_call", output_to_operand_aliasing={{0}: (8, {}), {1}: (9, {}), {2}: (10, {})} | custom-call | flops 1811939328 | bytes 4718592 | tf_op jit(solution)/shard_map/pallas_call | solution.py:176
  43.9 8.9 %shard_map.44 = (f32[12,1536,256]{2,1,0:T(8,128)}, bf16[3072,512]{1,0:T(8,128)(2,1)}, f32[4,1,768]{2,1,0:T(1,128)}, f32[128,1,512]{2,1,0:T(1,128)S(1)}) custom-call(f32[200,256]{1,0:T(8,128)S(1)} %get-tuple-element.79.refs_0_, f32[200,256]{1,0:T(8,128)S(1)} %get-tuple-element.78.refs_1_, ...), custom_call_target="tpu_custom_call", output_to_operand_aliasing={{0}: (12, {}), {1}: (13, {}), {2}: (14, {})} | custom-call | flops 3623878656 | bytes 9437184 | tf_op jit(solution)/shard_map/pallas_call | solution.py:176
  52.9 16.8 %all_to_all.5.sums_ref = f32[128,1,512]{2,1,0:T(1,128)S(1)} all-to-all(f32[128,1,512]{2,1,0:T(1,128)S(1)} %get-tuple-element.52), channel_id=1, replica_groups=mesh['y'=4,'zl'=2,'x'=4,'zh'=2,'core'=2] {'y','zl','x','zh','core'}, dimensions={0} | all-to-all | bytes 524288 | tf_op jit(solution)/shard_map/all_to_all | solution.py:356
  69.7 7.8 %shard_map.45 = (f32[200,256]{1,0:T(8,128)S(1)}, f32[200,256]{1,0:T(8,128)S(1)}, f32[200,256]{1,0:T(8,128)S(1)}, f32[200,256]{1,0:T(8,128)S(1)}, f32[1536,128]{1...) custom-call(f32[128,1,512]{2,1,0:T(1,128)S(1)} %all_to_all.5.sums_ref, ...), custom_call_target="tpu_custom_call" | custom-call | flops 3623878656 | bytes 9437184 | tf_op jit(solution)/shard_map/pallas_call | solution.py:275
  78.3 2.6 %collective-permute-start.16 = (f32[200,256]{1,0:T(8,128)S(1)}, f32[200,256]{1,0:T(8,128)S(1)}, u32[]{:S(2)}, u32[]{:S(2)}) collective-permute-start(f32[200,256]{1,0:T(8,128)S(1)} %get-tuple-element.59), channel_id=1, source_target_pairs={{0,96},{32,0},{64,32},{96,64},{1,97},{33,1},{65,33},{97,65},{2,98}... | collective-permute-start | bytes 614408 | tf_op jit(solution)/shard_map/ppermute | solution.py:336
  80.9 5.9 %shard_map.47 = (f32[200,256]{1,0:T(8,128)S(1)}, f32[200,256]{1,0:T(8,128)S(1)}, f32[200,256]{1,0:T(8,128)S(1)}) custom-call(f32[1,256]{1,0:T(1,128)S(1)} %get-tuple-element.61.sums_ref, f32[12,1536,256]{2,1,0:T(8,128)} %get-tuple-element.53.refs_0_.refs_1_.refs_2_.refs_3_, f32[12,1536,256]{2,1,0:T(8,128)} %get-tuple-element.53.refs_0_.refs_1_.refs_2_.refs_3_, ...), custom_call_target="tpu_custom_call" | custom-call | flops 2717908992 | bytes 7077888 | tf_op jit(solution)/shard_map/pallas_call | solution.py:275
  86.9 2.3 %collective-permute-start.18 = (f32[200,256]{1,0:T(8,128)S(1)}, f32[200,256]{1,0:T(8,128)S(1)}, u32[]{:S(2)}, u32[]{:S(2)}) collective-permute-start(f32[200,256]{1,0:T(8,128)S(1)} %get-tuple-element.64), channel_id=1, source_target_pairs={{0,64},{32,96},{64,0},{96,32},{1,65},{33,97},{65,1},{97,33},{2,66}... | collective-permute-start | bytes 614408 | tf_op jit(solution)/shard_map/ppermute | solution.py:335
  89.2 1.1 %collective-permute-start.19 = (f32[200,256]{1,0:T(8,128)S(1)}, f32[200,256]{1,0:T(8,128)S(1)}, u32[]{:S(2)}, u32[]{:S(2)}) collective-permute-start(f32[200,256]{1,0:T(8,128)S(1)} %get-tuple-element.65), channel_id=1, source_target_pairs={{0,96},{32,0},{64,32},{96,64},{1,97},{33,1},{65,33},{97,65},{2,98}... | collective-permute-start | bytes 614408 | tf_op jit(solution)/shard_map/ppermute | solution.py:336
  92.2 3.3 %shard_map.46.refs_0_ = f32[200,256]{1,0:T(8,128)S(1)} custom-call(f32[1,256]{1,0:T(1,128)S(1)} %get-tuple-element.61.sums_ref, f32[12,1536,256]{2,1,0:T(8,128)} %get-tuple-element.53.refs_0_.refs_1_.refs_2_.refs_3_, bf16[3072,512]{1,0:T(8,128)(2,1)} %get-tuple-element.54.refs_4_.refs_1_.refs_3_, f32[4,1,768]{2,1,0:T(1,128)} %get-tuple-element.55.refs_5_.refs_2_.refs_4_, ...), custom_call_target="tpu_custom_call" | custom-call | flops 905969664 | bytes 2359296 | tf_op jit(solution)/shard_map/pallas_call | solution.py:275
  96.4 2.9 %collective-permute-done.19.refs_2_ = f32[200,256]{1,0:T(8,128)S(1)} collective-permute-done((f32[200,256]{1,0:T(8,128)S(1)}, f32[200,256]{1,0:T(8,128)S(1)}, u32[]{:S(2)}, u32[]{:S(2)}) %collective-permute-start.19) | collective-permute-done | bytes 204832 | tf_op jit(solution)/shard_map/ppermute | solution.py:336
  (43 shorter events, 6.8 us)
Async XLA Ops:
  0.6 33.2 %copy-start = (f32[192,256]{1,0:T(8,128)S(1)}, f32[192,256]{1,0:T(8,128)}, u32[]{:S(2)}) copy-start(f32[192,256]{1,0:T(8,128)} %z_ref.2) | copy-start | bytes 589828
  1.7 8.0 %collective-permute-start.8 = (f32[192,256]{1,0:T(8,128)}, f32[192,256]{1,0:T(8,128)S(1)}, u32[]{:S(2)}, u32[]{:S(2)}) collective-permute-start(f32[192,256]{1,0:T(8,128)} %z_ref.2), channel_id=1, source_target_pairs={{0,16},{16,0},{1,17},{17,1},{2,18},{18,2},{3,19},{19,3},{4,20},{20... | collective-permute-start | bytes 589832 | tf_op jit(solution)/shard_map/ppermute | solution.py:342
  3.7 12.8 %collective-permute-start = (f32[200,256]{1,0:T(8,128)S(1)}, f32[200,256]{1,0:T(8,128)S(1)}, u32[]{:S(2)}, u32[]{:S(2)}) collective-permute-start(f32[200,256]{1,0:T(8,128)S(1)} %shard_map.41.refs_8_), channel_id=1, source_target_pairs={{0,2},{2,0},{1,3},{3,1},{4,6},{6,4},{5,7},{7,5},{8,10},{10,8},{9,1... | collective-permute-start | bytes 614408 | tf_op jit(solution)/shard_map/ppermute | solution.py:343
  9.7 10.7 %collective-permute-start.9 = (f32[384,256]{1,0:T(8,128)S(1)}, f32[384,256]{1,0:T(8,128)S(1)}, u32[]{:S(2)}, u32[]{:S(2)}) collective-permute-start(f32[384,256]{1,0:T(8,128)S(1)} %pad_maximum_fusion), channel_id=1, source_target_pairs={{0,32},{32,64},{64,96},{96,0},{1,33},{33,65},{65,97},{97,1},{2,34}... | collective-permute-start | bytes 1179656 | tf_op jit(solution)/shard_map/ppermute | solution.py:345
  11.5 10.2 %collective-permute-start.10 = (f32[384,256]{1,0:T(8,128)S(1)}, f32[384,256]{1,0:T(8,128)S(1)}, u32[]{:S(2)}, u32[]{:S(2)}) collective-permute-start(f32[384,256]{1,0:T(8,128)S(1)} %pad_maximum_fusion), channel_id=1, source_target_pairs={{0,96},{32,0},{64,32},{96,64},{1,97},{33,1},{65,33},{97,65},{2,98}... | collective-permute-start | bytes 1179656 | tf_op jit(solution)/shard_map/ppermute | solution.py:345
  16.6 16.6 %collective-permute-start.13 = (f32[400,256]{1,0:T(8,128)S(1)}, f32[400,256]{1,0:T(8,128)S(1)}, u32[]{:S(2)}, u32[]{:S(2)}) collective-permute-start(f32[400,256]{1,0:T(8,128)S(1)} %constant_dynamic-update-slice_fusion), channel_id=1, source_target_pairs={{0,1},{1,0},{2,3},{3,2},{4,5},{5,4},{6,7},{7,6},{8,9},{9,8},{10,11... | collective-permute-start | bytes 1228808 | tf_op jit(solution)/shard_map/ppermute | solution.py:350
  16.7 13.1 %collective-permute-start.3 = (f32[400,256]{1,0:T(8,128)S(1)}, f32[400,256]{1,0:T(8,128)S(1)}, u32[]{:S(2)}, u32[]{:S(2)}) collective-permute-start(f32[400,256]{1,0:T(8,128)S(1)} %constant_dynamic-update-slice_fusion), channel_id=1, source_target_pairs={{0,4},{4,8},{8,12},{12,0},{1,5},{5,9},{9,13},{13,1},{2,6},{6,10},{... | collective-permute-start | bytes 1228808 | tf_op jit(solution)/shard_map/ppermute | solution.py:348
  18.2 11.9 %collective-permute-start.1 = (f32[400,256]{1,0:T(8,128)S(1)}, f32[400,256]{1,0:T(8,128)S(1)}, u32[]{:S(2)}, u32[]{:S(2)}) collective-permute-start(f32[400,256]{1,0:T(8,128)S(1)} %constant_dynamic-update-slice_fusion), channel_id=1, source_target_pairs={{0,12},{4,0},{8,4},{12,8},{1,13},{5,1},{9,5},{13,9},{2,14},{6,2},{... | collective-permute-start | bytes 1228808 | tf_op jit(solution)/shard_map/ppermute | solution.py:348
  20.5 12.8 %collective-permute-start.11 = (f32[192,256]{1,0:T(8,128)S(1)}, f32[192,256]{1,0:T(8,128)S(1)}, u32[]{:S(2)}, u32[]{:S(2)}) collective-permute-start(f32[192,256]{1,0:T(8,128)S(1)} %get-tuple-element.83.refs_1_), channel_id=1, source_target_pairs={{0,32},{32,64},{64,96},{96,0},{1,33},{33,65},{65,97},{97,1},{2,34}... | collective-permute-start | bytes 589832 | tf_op jit(solution)/shard_map/ppermute | solution.py:346
  21.7 12.2 %collective-permute-start.12 = (f32[192,256]{1,0:T(8,128)S(1)}, f32[192,256]{1,0:T(8,128)S(1)}, u32[]{:S(2)}, u32[]{:S(2)}) collective-permute-start(f32[192,256]{1,0:T(8,128)S(1)} %get-tuple-element.80.refs_6_), channel_id=1, source_target_pairs={{0,96},{32,0},{64,32},{96,64},{1,97},{33,1},{65,33},{97,65},{2,98}... | collective-permute-start | bytes 589832 | tf_op jit(solution)/shard_map/ppermute | solution.py:346
  29.8 9.0 %collective-permute-start.4 = (f32[200,256]{1,0:T(8,128)S(1)}, f32[200,256]{1,0:T(8,128)S(1)}, u32[]{:S(2)}, u32[]{:S(2)}) collective-permute-start(f32[200,256]{1,0:T(8,128)S(1)} %get-tuple-element.73.refs_0_), channel_id=1, source_target_pairs={{0,4},{4,8},{8,12},{12,0},{1,5},{5,9},{9,13},{13,1},{2,6},{6,10},{... | collective-permute-start | bytes 614408 | tf_op jit(solution)/shard_map/ppermute | solution.py:349
  30.2 8.7 %collective-permute-start.5 = (f32[200,256]{1,0:T(8,128)S(1)}, f32[200,256]{1,0:T(8,128)S(1)}, u32[]{:S(2)}, u32[]{:S(2)}) collective-permute-start(f32[200,256]{1,0:T(8,128)S(1)} %get-tuple-element.78.refs_1_), channel_id=1, source_target_pairs={{0,12},{4,0},{8,4},{12,8},{1,13},{5,1},{9,5},{13,9},{2,14},{6,2},{... | collective-permute-start | bytes 614408 | tf_op jit(solution)/shard_map/ppermute | solution.py:349
  33.2 6.1 %collective-permute-start.14 = (f32[400,256]{1,0:T(8,128)S(1)}, f32[400,256]{1,0:T(8,128)S(1)}, u32[]{:S(2)}, u32[]{:S(2)}) collective-permute-start(f32[400,256]{1,0:T(8,128)S(1)} %collective-permute-done.3), channel_id=1, source_target_pairs={{0,1},{1,0},{2,3},{3,2},{4,5},{5,4},{6,7},{7,6},{8,9},{9,8},{10,11... | collective-permute-start | bytes 1228808 | tf_op jit(solution)/shard_map/ppermute | solution.py:350
  33.2 6.1 %collective-permute-start.2 = (f32[400,256]{1,0:T(8,128)S(1)}, f32[400,256]{1,0:T(8,128)S(1)}, u32[]{:S(2)}, u32[]{:S(2)}) collective-permute-start(f32[400,256]{1,0:T(8,128)S(1)} %collective-permute-done.1), channel_id=1, source_target_pairs={{0,1},{1,0},{2,3},{3,2},{4,5},{5,4},{6,7},{7,6},{8,9},{9,8},{10,11... | collective-permute-start | bytes 1228808 | tf_op jit(solution)/shard_map/ppermute | solution.py:350
  38.8 5.2 %collective-permute-start.6 = (f32[200,256]{1,0:T(8,128)S(1)}, f32[200,256]{1,0:T(8,128)S(1)}, u32[]{:S(2)}, u32[]{:S(2)}) collective-permute-start(f32[200,256]{1,0:T(8,128)S(1)} %collective-permute-done.4.refs_4_), channel_id=1, source_target_pairs={{0,1},{1,0},{2,3},{3,2},{4,5},{5,4},{6,7},{7,6},{8,9},{9,8},{10,11... | collective-permute-start | bytes 614408 | tf_op jit(solution)/shard_map/ppermute | solution.py:350
  38.8 5.1 %collective-permute-start.7 = (f32[200,256]{1,0:T(8,128)S(1)}, f32[200,256]{1,0:T(8,128)S(1)}, u32[]{:S(2)}, u32[]{:S(2)}) collective-permute-start(f32[200,256]{1,0:T(8,128)S(1)} %collective-permute-done.5.refs_5_), channel_id=1, source_target_pairs={{0,1},{1,0},{2,3},{3,2},{4,5},{5,4},{6,7},{7,6},{8,9},{9,8},{10,11... | collective-permute-start | bytes 614408 | tf_op jit(solution)/shard_map/ppermute | solution.py:350
  77.5 12.8 %collective-permute-start.15 = (f32[200,256]{1,0:T(8,128)S(1)}, f32[200,256]{1,0:T(8,128)S(1)}, u32[]{:S(2)}, u32[]{:S(2)}) collective-permute-start(f32[200,256]{1,0:T(8,128)S(1)} %get-tuple-element.58), channel_id=1, source_target_pairs={{0,64},{32,96},{64,0},{96,32},{1,65},{33,97},{65,1},{97,33},{2,66}... | collective-permute-start | bytes 614408 | tf_op jit(solution)/shard_map/ppermute | solution.py:335
  78.3 12.9 %collective-permute-start.16 = (f32[200,256]{1,0:T(8,128)S(1)}, f32[200,256]{1,0:T(8,128)S(1)}, u32[]{:S(2)}, u32[]{:S(2)}) collective-permute-start(f32[200,256]{1,0:T(8,128)S(1)} %get-tuple-element.59), channel_id=1, source_target_pairs={{0,96},{32,0},{64,32},{96,64},{1,97},{33,1},{65,33},{97,65},{2,98}... | collective-permute-start | bytes 614408 | tf_op jit(solution)/shard_map/ppermute | solution.py:336
  80.9 10.3 %collective-permute-start.17 = (f32[200,256]{1,0:T(8,128)S(1)}, f32[200,256]{1,0:T(8,128)S(1)}, u32[]{:S(2)}, u32[]{:S(2)}) collective-permute-start(f32[200,256]{1,0:T(8,128)S(1)} %get-tuple-element.60), channel_id=1, source_target_pairs={{0,32},{32,64},{64,96},{96,0},{1,33},{33,65},{65,97},{97,1},{2,34}... | collective-permute-start | bytes 614408 | tf_op jit(solution)/shard_map/ppermute | solution.py:336
  86.9 9.6 %collective-permute-start.18 = (f32[200,256]{1,0:T(8,128)S(1)}, f32[200,256]{1,0:T(8,128)S(1)}, u32[]{:S(2)}, u32[]{:S(2)}) collective-permute-start(f32[200,256]{1,0:T(8,128)S(1)} %get-tuple-element.64), channel_id=1, source_target_pairs={{0,64},{32,96},{64,0},{96,32},{1,65},{33,97},{65,1},{97,33},{2,66}... | collective-permute-start | bytes 614408 | tf_op jit(solution)/shard_map/ppermute | solution.py:335
  89.2 10.2 %collective-permute-start.19 = (f32[200,256]{1,0:T(8,128)S(1)}, f32[200,256]{1,0:T(8,128)S(1)}, u32[]{:S(2)}, u32[]{:S(2)}) collective-permute-start(f32[200,256]{1,0:T(8,128)S(1)} %get-tuple-element.65), channel_id=1, source_target_pairs={{0,96},{32,0},{64,32},{96,64},{1,97},{33,1},{65,33},{97,65},{2,98}... | collective-permute-start | bytes 614408 | tf_op jit(solution)/shard_map/ppermute | solution.py:336
  90.3 9.1 %collective-permute-start.20 = (f32[200,256]{1,0:T(8,128)S(1)}, f32[200,256]{1,0:T(8,128)S(1)}, u32[]{:S(2)}, u32[]{:S(2)}) collective-permute-start(f32[200,256]{1,0:T(8,128)S(1)} %get-tuple-element.66), channel_id=1, source_target_pairs={{0,32},{32,64},{64,96},{96,0},{1,33},{33,65},{65,97},{97,1},{2,34}... | collective-permute-start | bytes 614408 | tf_op jit(solution)/shard_map/ppermute | solution.py:336
  91.3 8.1 %collective-permute-start.21 = (f32[200,256]{1,0:T(8,128)S(1)}, f32[200,256]{1,0:T(8,128)S(1)}, u32[]{:S(2)}, u32[]{:S(2)}) collective-permute-start(f32[200,256]{1,0:T(8,128)S(1)} %add_add_fusion), channel_id=1, source_target_pairs={{0,16},{16,0},{1,17},{17,1},{2,18},{18,2},{3,19},{19,3},{4,20},{20... | collective-permute-start | bytes 614408 | tf_op jit(solution)/shard_map/ppermute | solution.py:363

commit v6 on v5

--- a/solution.py
+++ b/solution.py
@@ -57,14 +57,15 @@
     place = places()
     first, last = start == 0, start + steps == STEPS
     if first:
-        columns, blocks, refs = refs[:C_BLOCKS], refs[C_BLOCKS : C_BLOCKS + 4], refs[C_BLOCKS + 4 :]
+        columns, refs = refs[:C_BLOCKS], refs[C_BLOCKS:]
+        blocks, refs = refs[: 4 * steps], refs[4 * steps :]
         e_ref, zr_ref, partner_ref, rsum_ref, pos_ref, cacc_ref, a_ref, cid_ref, b_ref = refs
     else:
         blocks, refs = refs[: 4 * steps], refs[4 * steps :]
         a_ref, cid_ref, pos_in_ref, cacc_in_ref = refs[:4]
         refs = refs[7:]
         if last:
-            earlier, refs = refs[:start], refs[start:]
+            earlier_ref, refs = refs[0], refs[1:]
             e_ref, zr_ref, partner_ref, send_ref, b_ref, rsum_ref, pos_ref, cacc_ref, rows_ref = refs
         else:
             e_ref, zr_ref, partner_ref, rsum_ref, pos_ref, cacc_ref, b_ref = refs
@@ -132,7 +133,7 @@
             positives = jnp.full((R_BLOCKS, 256 - PER), jnp.sum(pos_ref[...]), f32)
             for s in range(R_BLOCKS):
                 step, b = divmod(s, 4)
-                sums = earlier[step][0] if step < start else rsum_ref[step - start]
+                sums = earlier_ref[step] if step < start else rsum_ref[step - start]
                 rows_ref[place[C_BLOCKS + s], 0:1, 0:PER] = sums[:, b * PER : (b + 1) * PER]
             of_rows = jnp.concatenate([rows_ref[c, 0:1, 0:PER] for c in range(R_BLOCKS)])
             for s in range(C_BLOCKS):
@@ -158,7 +159,7 @@
     sums = [pltpu.VMEM((steps, 1, SPAN), f32), pltpu.VMEM((8, 128), f32), pltpu.VMEM((C, 128), f32)]
     scratch = [pltpu.VMEM((SPAN, 3 * D), bf16)]
     if first:
-        given, in_specs, aliases = (*columns, *blocks), [vmem] * (C_BLOCKS + 4), {}
+        given, in_specs, aliases = (*columns, *blocks), [vmem] * (C_BLOCKS + len(blocks)), {}
         made = sums + [pltpu.VMEM((C, 3 * D), bf16), pltpu.VMEM((C, 128), f32)]
     else:
         e, zr, partners, rsums, pos, cacc, a, cid = carried
@@ -349,10 +350,11 @@
     r3z, r3b = lax.ppermute(r1[BLOCK:], "x", UP), lax.ppermute(r2[:BLOCK], "x", DOWN)
     swap = lambda r: lax.ppermute(r, "core", SWAP)
     columns = (z, c1[PER:], c2[PER:], c3z, a, c1[:PER], c2[:PER], c3a)
-    rows = [(r[BLOCK:], r[:BLOCK], q[BLOCK:], q[:BLOCK]) for r, q in ((r, swap(r)) for r in (r0, r1, r2))]
-    carried = scores(0, rows[0], columns)
-    carried = scores(1, rows[1], carried=carried)
-    e, zr, partners, sums = scores(2, (*rows[2], r3z, r3b, swap(r3z), swap(r3b)), carried=carried)
+    pieces = lambda r, q: (r[BLOCK:], r[:BLOCK], q[BLOCK:], q[:BLOCK])
+    s0, s1, s2 = swap(r0), swap(r1), swap(r2)
+    carried = scores(0, (*pieces(r0, s0), *pieces(r1, s1)), columns)
+    r3z, r3b, carried = lax.optimization_barrier((r3z, r3b, carried))
+    e, zr, partners, sums = scores(2, (*pieces(r2, s2), r3z, r3b, swap(r3z), swap(r3b)), carried=carried)
     sums = lax.all_to_all(sums, ALL, 0, 0, tiled=True)
     e, zr, partners = (pltpu.with_memory_space_constraint(v, pltpu.HBM) for v in (e, zr, partners))
     here, *away, uc, ur, logs = gradients((4, 5, 6, 7), sums, e, zr, partners)

time: 101 us -> 100 us (0.990)
  Pallas kernels: 37.3 us -> 35.8 us
  waiting for transfers between devices: 16.2 us -> 17.3 us
    pallas_call x3 -> x2, Pallas kernels: 18.4 us -> 16.9 us  [scores(): pl.pallas_call(functools.partial(score_kernel, start, steps), grid=(steps...]
    ppermute x1, starting transfers between devices: 2.19 us -> 3.45 us  [shards(): lax.ppermute(c2[:PER], 'y', DOWN)]
    ppermute x5, waiting for transfers between devices: 0.01 us -> 1.21 us  [shards(): swap = lambda r: lax.ppermute(r, 'core', SWAP)]
    ppermute x1, starting transfers between devices: 1.18 us -> 0.07 us  [shards(): lax.ppermute(c1[PER:], 'y', UP)]
  transfers between devices with their start and end apart: 22 -> 22, of which waited for: 6 -> 7; matrix products, arithmetic and copies ran while one was open for 0% -> 0% of each run, Pallas kernels for 19% -> 18%
where the time goes in v6:
time: 100 us; the launch traced here: 99.8 us
  Pallas kernels  35.8 us (36%)
  starting transfers between devices  28.7 us (29%)
  waiting for transfers between devices  17.3 us (17%)
  blocking collectives  16.8 us (17%)
    pallas_call x3, Pallas kernels, gradients(): pl.pallas_call(functools.partial(gradient_kernel, slots, first), grid=(ST...  17 us
    pallas_call x2, Pallas kernels, scores(): pl.pallas_call(functools.partial(score_kernel, start, steps), grid=(steps...  16.9 us
    all_to_all x1, blocking collectives, shards(): sums = lax.all_to_all(sums, ALL, 0, 0, tiled=True)  16.8 us
    ppermute x2, waiting for transfers between devices, shards(): r1, r2 = (lax.ppermute(r0, 'x', UP), lax.ppermute(r0, 'x', DOWN))  6.19 us
    ppermute x4, starting transfers between devices, over_y(): return (across, lax.ppermute(down, 'y', DOWN), lax.ppermute(up, 'y', UP))  4.62 us
    ppermute x1, waiting for transfers between devices, shards(): b = lax.ppermute(block, 'zh', SWAP)  3.62 us
    ppermute x1, starting transfers between devices, shards(): b = lax.ppermute(block, 'zh', SWAP)  3.58 us
    ppermute x1, starting transfers between devices, shards(): lax.ppermute(c2[:PER], 'y', DOWN)  3.45 us
  transfers between devices with their start and end apart: 22, of which 7 were waited for; matrix products, arithmetic and copies ran while one was open for 0% of the time, Pallas kernels for 18%

profile of v6, /device:TPU:0, one launch (start us, length us, event | category | flops | bytes accessed | tf_op | source)
XLA Modules:
  0.0 99.8 jit_solution(2743339213926263752)
XLA Ops:
  0.6 0.9 shard_map.41.refs_8_
  1.6 2.1 %collective-permute-start.6 = (f32[192,256]{1,0:T(8,128)}, f32[192,256]{1,0:T(8,128)S(1)}, u32[]{:S(2)}, u32[]{:S(2)}) collective-permute-start(f32[192,256]{1,0:T(8,128)} %z_ref.2), channel_id=1, source_target_pairs={{0,16},{16,0},{1,17},{17,1},{2,18},{18,2},{3,19},{19,3},{4,20},{20... | collective-permute-start | bytes 589832 | tf_op jit(solution)/shard_map/ppermute | solution.py:343
  3.7 3.6 %collective-permute-start = (f32[200,256]{1,0:T(8,128)S(1)}, f32[200,256]{1,0:T(8,128)S(1)}, u32[]{:S(2)}, u32[]{:S(2)}) collective-permute-start(f32[200,256]{1,0:T(8,128)S(1)} %shard_map.41.refs_8_), channel_id=1, source_target_pairs={{0,2},{2,0},{1,3},{3,1},{4,6},{6,4},{5,7},{7,5},{8,10},{10,8},{9,1... | collective-permute-start | bytes 614408 | tf_op jit(solution)/shard_map/ppermute | solution.py:344
  7.3 2.4 %collective-permute-done.6.refs_4_ = f32[192,256]{1,0:T(8,128)S(1)} collective-permute-done((f32[192,256]{1,0:T(8,128)}, f32[192,256]{1,0:T(8,128)S(1)}, u32[]{:S(2)}, u32[]{:S(2)}) %collective-permute-start.6) | collective-permute-done | bytes 196640 | tf_op jit(solution)/shard_map/ppermute | solution.py:343
  9.7 3.2 %collective-permute-start.8 = (f32[384,256]{1,0:T(8,128)S(1)}, f32[384,256]{1,0:T(8,128)S(1)}, u32[]{:S(2)}, u32[]{:S(2)}) collective-permute-start(f32[384,256]{1,0:T(8,128)S(1)} %pad_maximum_fusion), channel_id=1, source_target_pairs={{0,96},{32,0},{64,32},{96,64},{1,97},{33,1},{65,33},{97,65},{2,98}... | collective-permute-start | bytes 1179656 | tf_op jit(solution)/shard_map/ppermute | solution.py:346
  12.8 3.6 %collective-permute-done.refs_9_ = f32[200,256]{1,0:T(8,128)S(1)} collective-permute-done((f32[200,256]{1,0:T(8,128)S(1)}, f32[200,256]{1,0:T(8,128)S(1)}, u32[]{:S(2)}, u32[]{:S(2)}) %collective-permute-start) | collective-permute-done | bytes 204832 | tf_op jit(solution)/shard_map/ppermute | solution.py:344
  16.6 1.6 %collective-permute-start.3 = (f32[400,256]{1,0:T(8,128)S(1)}, f32[400,256]{1,0:T(8,128)S(1)}, u32[]{:S(2)}, u32[]{:S(2)}) collective-permute-start(f32[400,256]{1,0:T(8,128)S(1)} %constant_dynamic-update-slice_fusion), channel_id=1, source_target_pairs={{0,4},{4,8},{8,12},{12,0},{1,5},{5,9},{9,13},{13,1},{2,6},{6,10},{... | collective-permute-start | bytes 1228808 | tf_op jit(solution)/shard_map/ppermute | solution.py:349
  18.2 1.7 %collective-permute-start.1 = (f32[400,256]{1,0:T(8,128)S(1)}, f32[400,256]{1,0:T(8,128)S(1)}, u32[]{:S(2)}, u32[]{:S(2)}) collective-permute-start(f32[400,256]{1,0:T(8,128)S(1)} %constant_dynamic-update-slice_fusion), channel_id=1, source_target_pairs={{0,12},{4,0},{8,4},{12,8},{1,13},{5,1},{9,5},{13,9},{2,14},{6,2},{... | collective-permute-start | bytes 1228808 | tf_op jit(solution)/shard_map/ppermute | solution.py:349
  19.9 3.5 %collective-permute-start.10 = (f32[192,256]{1,0:T(8,128)S(1)}, f32[192,256]{1,0:T(8,128)S(1)}, u32[]{:S(2)}, u32[]{:S(2)}) collective-permute-start(f32[192,256]{1,0:T(8,128)S(1)} %get-tuple-element.88.refs_6_), channel_id=1, source_target_pairs={{0,96},{32,0},{64,32},{96,64},{1,97},{33,1},{65,33},{97,65},{2,98}... | collective-permute-start | bytes 589832 | tf_op jit(solution)/shard_map/ppermute | solution.py:347
  23.5 6.2 %collective-permute-done.3 = f32[400,256]{1,0:T(8,128)S(1)} collective-permute-done((f32[400,256]{1,0:T(8,128)S(1)}, f32[400,256]{1,0:T(8,128)S(1)}, u32[]{:S(2)}, u32[]{:S(2)}) %collective-permute-start.3) | collective-permute-done | bytes 409632 | tf_op jit(solution)/shard_map/ppermute | solution.py:349
  30.1 3.0 %collective-permute-start.5 = (f32[200,256]{1,0:T(8,128)S(1)}, f32[200,256]{1,0:T(8,128)S(1)}, u32[]{:S(2)}, u32[]{:S(2)}) collective-permute-start(f32[200,256]{1,0:T(8,128)S(1)} %get-tuple-element.86.refs_1_), channel_id=1, source_target_pairs={{0,12},{4,0},{8,4},{12,8},{1,13},{5,1},{9,5},{13,9},{2,14},{6,2},{... | collective-permute-start | bytes 614408 | tf_op jit(solution)/shard_map/ppermute | solution.py:350
  33.5 8.3 %shard_map.42 = (f32[12,1536,256]{2,1,0:T(8,128)}, bf16[3072,512]{1,0:T(8,128)(2,1)}, f32[4,1,768]{2,1,0:T(1,128)}, f32[2,1,768]{2,1,0:T(1,128)S(1)}, f32[8,128]...) custom-call(f32[192,256]{1,0:T(8,128)S(1)} %copy-done, ...), custom_call_target="tpu_custom_call" | custom-call | flops 3623878656 | bytes 9437184 | tf_op jit(solution)/shard_map/pallas_call | solution.py:177
  43.6 8.7 %shard_map.43 = (f32[12,1536,256]{2,1,0:T(8,128)}, bf16[3072,512]{1,0:T(8,128)(2,1)}, f32[4,1,768]{2,1,0:T(1,128)}, f32[128,1,512]{2,1,0:T(1,128)S(1)}) custom-call(f32[200,256]{1,0:T(8,128)S(1)} %get-tuple-element.87.refs_0_, f32[200,256]{1,0:T(8,128)S(1)} %get-tuple-element.86.refs_1_, ...), custom_call_target="tpu_custom_call", output_to_operand_aliasing={{0}: (12, {}), {1}: (13, {}), {2}: (14, {})} | custom-call | flops 3623878656 | bytes 9437184 | tf_op jit(solution)/shard_map/pallas_call | solution.py:177
  52.3 16.8 %all_to_all.5.sums_ref = f32[128,1,512]{2,1,0:T(1,128)S(1)} all-to-all(f32[128,1,512]{2,1,0:T(1,128)S(1)} %get-tuple-element.60), channel_id=1, replica_groups=mesh['y'=4,'zl'=2,'x'=4,'zh'=2,'core'=2] {'y','zl','x','zh','core'}, dimensions={0} | all-to-all | bytes 524288 | tf_op jit(solution)/shard_map/all_to_all | solution.py:358
  69.1 7.8 %shard_map.44 = (f32[200,256]{1,0:T(8,128)S(1)}, f32[200,256]{1,0:T(8,128)S(1)}, f32[200,256]{1,0:T(8,128)S(1)}, f32[200,256]{1,0:T(8,128)S(1)}, f32[1536,128]{1...) custom-call(f32[128,1,512]{2,1,0:T(1,128)S(1)} %all_to_all.5.sums_ref, ...), custom_call_target="tpu_custom_call" | custom-call | flops 3623878656 | bytes 9437184 | tf_op jit(solution)/shard_map/pallas_call | solution.py:276
  77.7 2.6 %collective-permute-start.16 = (f32[200,256]{1,0:T(8,128)S(1)}, f32[200,256]{1,0:T(8,128)S(1)}, u32[]{:S(2)}, u32[]{:S(2)}) collective-permute-start(f32[200,256]{1,0:T(8,128)S(1)} %get-tuple-element.67), channel_id=1, source_target_pairs={{0,96},{32,0},{64,32},{96,64},{1,97},{33,1},{65,33},{97,65},{2,98}... | collective-permute-start | bytes 614408 | tf_op jit(solution)/shard_map/ppermute | solution.py:337
  80.3 5.9 %shard_map.46 = (f32[200,256]{1,0:T(8,128)S(1)}, f32[200,256]{1,0:T(8,128)S(1)}, f32[200,256]{1,0:T(8,128)S(1)}) custom-call(f32[1,256]{1,0:T(1,128)S(1)} %get-tuple-element.69.sums_ref, f32[12,1536,256]{2,1,0:T(8,128)} %get-tuple-element.61.refs_0_.refs_1_.refs_2_.refs_3_, f32[12,1536,256]{2,1,0:T(8,128)} %get-tuple-element.61.refs_0_.refs_1_.refs_2_.refs_3_, ...), custom_call_target="tpu_custom_call" | custom-call | flops 2717908992 | bytes 7077888 | tf_op jit(solution)/shard_map/pallas_call | solution.py:276
  86.2 2.3 %collective-permute-start.18 = (f32[200,256]{1,0:T(8,128)S(1)}, f32[200,256]{1,0:T(8,128)S(1)}, u32[]{:S(2)}, u32[]{:S(2)}) collective-permute-start(f32[200,256]{1,0:T(8,128)S(1)} %get-tuple-element.72), channel_id=1, source_target_pairs={{0,64},{32,96},{64,0},{96,32},{1,65},{33,97},{65,1},{97,33},{2,66}... | collective-permute-start | bytes 614408 | tf_op jit(solution)/shard_map/ppermute | solution.py:336
  88.5 1.1 %collective-permute-start.19 = (f32[200,256]{1,0:T(8,128)S(1)}, f32[200,256]{1,0:T(8,128)S(1)}, u32[]{:S(2)}, u32[]{:S(2)}) collective-permute-start(f32[200,256]{1,0:T(8,128)S(1)} %get-tuple-element.73), channel_id=1, source_target_pairs={{0,96},{32,0},{64,32},{96,64},{1,97},{33,1},{65,33},{97,65},{2,98}... | collective-permute-start | bytes 614408 | tf_op jit(solution)/shard_map/ppermute | solution.py:337
  89.6 0.9 collective-permute-start.20
  90.6 0.9 collective-permute-start.21
  91.6 3.3 %shard_map.45.refs_0_ = f32[200,256]{1,0:T(8,128)S(1)} custom-call(f32[1,256]{1,0:T(1,128)S(1)} %get-tuple-element.69.sums_ref, f32[12,1536,256]{2,1,0:T(8,128)} %get-tuple-element.61.refs_0_.refs_1_.refs_2_.refs_3_, bf16[3072,512]{1,0:T(8,128)(2,1)} %get-tuple-element.62.refs_4_.refs_1_.refs_3_, f32[4,1,768]{2,1,0:T(1,128)} %get-tuple-element.63.refs_5_.refs_2_.refs_4_, ...), custom_call_target="tpu_custom_call" | custom-call | flops 905969664 | bytes 2359296 | tf_op jit(solution)/shard_map/pallas_call | solution.py:276
  94.9 1.0 collective-permute-done.18.refs_1_
  95.8 2.9 %collective-permute-done.19.refs_2_ = f32[200,256]{1,0:T(8,128)S(1)} collective-permute-done((f32[200,256]{1,0:T(8,128)S(1)}, f32[200,256]{1,0:T(8,128)S(1)}, u32[]{:S(2)}, u32[]{:S(2)}) %collective-permute-start.19) | collective-permute-done | bytes 204832 | tf_op jit(solution)/shard_map/ppermute | solution.py:337
  (42 shorter events, 4.7 us)
Async XLA Ops:
  1.6 8.0 %collective-permute-start.6 = (f32[192,256]{1,0:T(8,128)}, f32[192,256]{1,0:T(8,128)S(1)}, u32[]{:S(2)}, u32[]{:S(2)}) collective-permute-start(f32[192,256]{1,0:T(8,128)} %z_ref.2), channel_id=1, source_target_pairs={{0,16},{16,0},{1,17},{17,1},{2,18},{18,2},{3,19},{19,3},{4,20},{20... | collective-permute-start | bytes 589832 | tf_op jit(solution)/shard_map/ppermute | solution.py:343
  3.7 12.8 %collective-permute-start = (f32[200,256]{1,0:T(8,128)S(1)}, f32[200,256]{1,0:T(8,128)S(1)}, u32[]{:S(2)}, u32[]{:S(2)}) collective-permute-start(f32[200,256]{1,0:T(8,128)S(1)} %shard_map.41.refs_8_), channel_id=1, source_target_pairs={{0,2},{2,0},{1,3},{3,1},{4,6},{6,4},{5,7},{7,5},{8,10},{10,8},{9,1... | collective-permute-start | bytes 614408 | tf_op jit(solution)/shard_map/ppermute | solution.py:344
  7.3 26.3 %copy-start = (f32[192,256]{1,0:T(8,128)S(1)}, f32[192,256]{1,0:T(8,128)}, u32[]{:S(2)}) copy-start(f32[192,256]{1,0:T(8,128)} %z_ref.2) | copy-start | bytes 589828
  9.7 10.2 %collective-permute-start.8 = (f32[384,256]{1,0:T(8,128)S(1)}, f32[384,256]{1,0:T(8,128)S(1)}, u32[]{:S(2)}, u32[]{:S(2)}) collective-permute-start(f32[384,256]{1,0:T(8,128)S(1)} %pad_maximum_fusion), channel_id=1, source_target_pairs={{0,96},{32,0},{64,32},{96,64},{1,97},{33,1},{65,33},{97,65},{2,98}... | collective-permute-start | bytes 1179656 | tf_op jit(solution)/shard_map/ppermute | solution.py:346
  12.8 10.6 %collective-permute-start.7 = (f32[384,256]{1,0:T(8,128)S(1)}, f32[384,256]{1,0:T(8,128)S(1)}, u32[]{:S(2)}, u32[]{:S(2)}) collective-permute-start(f32[384,256]{1,0:T(8,128)S(1)} %pad_maximum_fusion), channel_id=1, source_target_pairs={{0,32},{32,64},{64,96},{96,0},{1,33},{33,65},{65,97},{97,1},{2,34}... | collective-permute-start | bytes 1179656 | tf_op jit(solution)/shard_map/ppermute | solution.py:346
  16.5 13.6 %collective-permute-start.11 = (f32[400,256]{1,0:T(8,128)S(1)}, f32[400,256]{1,0:T(8,128)S(1)}, u32[]{:S(2)}, u32[]{:S(2)}) collective-permute-start(f32[400,256]{1,0:T(8,128)S(1)} %constant_dynamic-update-slice_fusion), channel_id=1, source_target_pairs={{0,1},{1,0},{2,3},{3,2},{4,5},{5,4},{6,7},{7,6},{8,9},{9,8},{10,11... | collective-permute-start | bytes 1228808 | tf_op jit(solution)/shard_map/ppermute | solution.py:351
  16.6 13.1 %collective-permute-start.3 = (f32[400,256]{1,0:T(8,128)S(1)}, f32[400,256]{1,0:T(8,128)S(1)}, u32[]{:S(2)}, u32[]{:S(2)}) collective-permute-start(f32[400,256]{1,0:T(8,128)S(1)} %constant_dynamic-update-slice_fusion), channel_id=1, source_target_pairs={{0,4},{4,8},{8,12},{12,0},{1,5},{5,9},{9,13},{13,1},{2,6},{6,10},{... | collective-permute-start | bytes 1228808 | tf_op jit(solution)/shard_map/ppermute | solution.py:349
  18.2 11.9 %collective-permute-start.1 = (f32[400,256]{1,0:T(8,128)S(1)}, f32[400,256]{1,0:T(8,128)S(1)}, u32[]{:S(2)}, u32[]{:S(2)}) collective-permute-start(f32[400,256]{1,0:T(8,128)S(1)} %constant_dynamic-update-slice_fusion), channel_id=1, source_target_pairs={{0,12},{4,0},{8,4},{12,8},{1,13},{5,1},{9,5},{13,9},{2,14},{6,2},{... | collective-permute-start | bytes 1228808 | tf_op jit(solution)/shard_map/ppermute | solution.py:349
  19.9 13.6 %collective-permute-start.10 = (f32[192,256]{1,0:T(8,128)S(1)}, f32[192,256]{1,0:T(8,128)S(1)}, u32[]{:S(2)}, u32[]{:S(2)}) collective-permute-start(f32[192,256]{1,0:T(8,128)S(1)} %get-tuple-element.88.refs_6_), channel_id=1, source_target_pairs={{0,96},{32,0},{64,32},{96,64},{1,97},{33,1},{65,33},{97,65},{2,98}... | collective-permute-start | bytes 589832 | tf_op jit(solution)/shard_map/ppermute | solution.py:347
  23.4 10.1 %collective-permute-start.9 = (f32[192,256]{1,0:T(8,128)S(1)}, f32[192,256]{1,0:T(8,128)S(1)}, u32[]{:S(2)}, u32[]{:S(2)}) collective-permute-start(f32[192,256]{1,0:T(8,128)S(1)} %get-tuple-element.91.refs_1_), channel_id=1, source_target_pairs={{0,32},{32,64},{64,96},{96,0},{1,33},{33,65},{65,97},{97,1},{2,34}... | collective-permute-start | bytes 589832 | tf_op jit(solution)/shard_map/ppermute | solution.py:347
  29.7 12.1 %collective-permute-start.4 = (f32[200,256]{1,0:T(8,128)S(1)}, f32[200,256]{1,0:T(8,128)S(1)}, u32[]{:S(2)}, u32[]{:S(2)}) collective-permute-start(f32[200,256]{1,0:T(8,128)S(1)} %get-tuple-element.81.refs_12_), channel_id=1, source_target_pairs={{0,4},{4,8},{8,12},{12,0},{1,5},{5,9},{9,13},{13,1},{2,6},{6,10},{... | collective-permute-start | bytes 614408 | tf_op jit(solution)/shard_map/ppermute | solution.py:350
  30.1 3.1 %collective-permute-start.12 = (f32[400,256]{1,0:T(8,128)S(1)}, f32[400,256]{1,0:T(8,128)S(1)}, u32[]{:S(2)}, u32[]{:S(2)}) collective-permute-start(f32[400,256]{1,0:T(8,128)S(1)} %collective-permute-done.3), channel_id=1, source_target_pairs={{0,1},{1,0},{2,3},{3,2},{4,5},{5,4},{6,7},{7,6},{8,9},{9,8},{10,11... | collective-permute-start | bytes 1228808 | tf_op jit(solution)/shard_map/ppermute | solution.py:351
  30.1 11.7 %collective-permute-start.5 = (f32[200,256]{1,0:T(8,128)S(1)}, f32[200,256]{1,0:T(8,128)S(1)}, u32[]{:S(2)}, u32[]{:S(2)}) collective-permute-start(f32[200,256]{1,0:T(8,128)S(1)} %get-tuple-element.86.refs_1_), channel_id=1, source_target_pairs={{0,12},{4,0},{8,4},{12,8},{1,13},{5,1},{9,5},{13,9},{2,14},{6,2},{... | collective-permute-start | bytes 614408 | tf_op jit(solution)/shard_map/ppermute | solution.py:350
  33.2 9.2 %collective-permute-start.2 = (f32[400,256]{1,0:T(8,128)S(1)}, f32[400,256]{1,0:T(8,128)S(1)}, u32[]{:S(2)}, u32[]{:S(2)}) collective-permute-start(f32[400,256]{1,0:T(8,128)S(1)} %collective-permute-done.1), channel_id=1, source_target_pairs={{0,1},{1,0},{2,3},{3,2},{4,5},{5,4},{6,7},{7,6},{8,9},{9,8},{10,11... | collective-permute-start | bytes 1228808 | tf_op jit(solution)/shard_map/ppermute | solution.py:351
  41.8 1.5 %collective-permute-start.13 = (f32[200,256]{1,0:T(8,128)S(1)}, f32[200,256]{1,0:T(8,128)S(1)}, u32[]{:S(2)}, u32[]{:S(2)}) collective-permute-start(f32[200,256]{1,0:T(8,128)S(1)} %collective-permute-done.4.refs_4_), channel_id=1, source_target_pairs={{0,1},{1,0},{2,3},{3,2},{4,5},{5,4},{6,7},{7,6},{8,9},{9,8},{10,11... | collective-permute-start | bytes 614408 | tf_op jit(solution)/shard_map/ppermute | solution.py:351
  42.2 1.5 %collective-permute-start.14 = (f32[200,256]{1,0:T(8,128)S(1)}, f32[200,256]{1,0:T(8,128)S(1)}, u32[]{:S(2)}, u32[]{:S(2)}) collective-permute-start(f32[200,256]{1,0:T(8,128)S(1)} %collective-permute-done.5.refs_5_), channel_id=1, source_target_pairs={{0,1},{1,0},{2,3},{3,2},{4,5},{5,4},{6,7},{7,6},{8,9},{9,8},{10,11... | collective-permute-start | bytes 614408 | tf_op jit(solution)/shard_map/ppermute | solution.py:351
  76.9 12.8 %collective-permute-start.15 = (f32[200,256]{1,0:T(8,128)S(1)}, f32[200,256]{1,0:T(8,128)S(1)}, u32[]{:S(2)}, u32[]{:S(2)}) collective-permute-start(f32[200,256]{1,0:T(8,128)S(1)} %get-tuple-element.66), channel_id=1, source_target_pairs={{0,64},{32,96},{64,0},{96,32},{1,65},{33,97},{65,1},{97,33},{2,66}... | collective-permute-start | bytes 614408 | tf_op jit(solution)/shard_map/ppermute | solution.py:336
  77.7 12.9 %collective-permute-start.16 = (f32[200,256]{1,0:T(8,128)S(1)}, f32[200,256]{1,0:T(8,128)S(1)}, u32[]{:S(2)}, u32[]{:S(2)}) collective-permute-start(f32[200,256]{1,0:T(8,128)S(1)} %get-tuple-element.67), channel_id=1, source_target_pairs={{0,96},{32,0},{64,32},{96,64},{1,97},{33,1},{65,33},{97,65},{2,98}... | collective-permute-start | bytes 614408 | tf_op jit(solution)/shard_map/ppermute | solution.py:337
  80.3 10.3 %collective-permute-start.17 = (f32[200,256]{1,0:T(8,128)S(1)}, f32[200,256]{1,0:T(8,128)S(1)}, u32[]{:S(2)}, u32[]{:S(2)}) collective-permute-start(f32[200,256]{1,0:T(8,128)S(1)} %get-tuple-element.68), channel_id=1, source_target_pairs={{0,32},{32,64},{64,96},{96,0},{1,33},{33,65},{65,97},{97,1},{2,34}... | collective-permute-start | bytes 614408 | tf_op jit(solution)/shard_map/ppermute | solution.py:337
  86.2 9.6 %collective-permute-start.18 = (f32[200,256]{1,0:T(8,128)S(1)}, f32[200,256]{1,0:T(8,128)S(1)}, u32[]{:S(2)}, u32[]{:S(2)}) collective-permute-start(f32[200,256]{1,0:T(8,128)S(1)} %get-tuple-element.72), channel_id=1, source_target_pairs={{0,64},{32,96},{64,0},{96,32},{1,65},{33,97},{65,1},{97,33},{2,66}... | collective-permute-start | bytes 614408 | tf_op jit(solution)/shard_map/ppermute | solution.py:336
  88.5 10.2 %collective-permute-start.19 = (f32[200,256]{1,0:T(8,128)S(1)}, f32[200,256]{1,0:T(8,128)S(1)}, u32[]{:S(2)}, u32[]{:S(2)}) collective-permute-start(f32[200,256]{1,0:T(8,128)S(1)} %get-tuple-element.73), channel_id=1, source_target_pairs={{0,96},{32,0},{64,32},{96,64},{1,97},{33,1},{65,33},{97,65},{2,98}... | collective-permute-start | bytes 614408 | tf_op jit(solution)/shard_map/ppermute | solution.py:337
  89.6 9.1 %collective-permute-start.20 = (f32[200,256]{1,0:T(8,128)S(1)}, f32[200,256]{1,0:T(8,128)S(1)}, u32[]{:S(2)}, u32[]{:S(2)}) collective-permute-start(f32[200,256]{1,0:T(8,128)S(1)} %get-tuple-element.74), channel_id=1, source_target_pairs={{0,32},{32,64},{64,96},{96,0},{1,33},{33,65},{65,97},{97,1},{2,34}... | collective-permute-start | bytes 614408 | tf_op jit(solution)/shard_map/ppermute | solution.py:337
  90.6 8.1 %collective-permute-start.21 = (f32[200,256]{1,0:T(8,128)S(1)}, f32[200,256]{1,0:T(8,128)S(1)}, u32[]{:S(2)}, u32[]{:S(2)}) collective-permute-start(f32[200,256]{1,0:T(8,128)S(1)} %add_add_fusion), channel_id=1, source_target_pairs={{0,16},{16,0},{1,17},{17,1},{2,18},{18,2},{3,19},{19,3},{4,20},{20... | collective-permute-start | bytes 614408 | tf_op jit(solution)/shard_map/ppermute | solution.py:365

commit v7 on v6

--- a/solution.py
+++ b/solution.py
@@ -65,7 +65,7 @@
         a_ref, cid_ref, pos_in_ref, cacc_in_ref = refs[:4]
         refs = refs[7:]
         if last:
-            earlier_ref, refs = refs[0], refs[1:]
+            *earlier, refs = refs[0], refs[1], refs[2:]
             e_ref, zr_ref, partner_ref, send_ref, b_ref, rsum_ref, pos_ref, cacc_ref, rows_ref = refs
         else:
             e_ref, zr_ref, partner_ref, rsum_ref, pos_ref, cacc_ref, b_ref = refs
@@ -133,7 +133,7 @@
             positives = jnp.full((R_BLOCKS, 256 - PER), jnp.sum(pos_ref[...]), f32)
             for s in range(R_BLOCKS):
                 step, b = divmod(s, 4)
-                sums = earlier_ref[step] if step < start else rsum_ref[step - start]
+                sums = (earlier[0][0], earlier[0][1], earlier[1][0], rsum_ref[0])[step]
                 rows_ref[place[C_BLOCKS + s], 0:1, 0:PER] = sums[:, b * PER : (b + 1) * PER]
             of_rows = jnp.concatenate([rows_ref[c, 0:1, 0:PER] for c in range(R_BLOCKS)])
             for s in range(C_BLOCKS):
@@ -354,7 +354,8 @@
     s0, s1, s2 = swap(r0), swap(r1), swap(r2)
     carried = scores(0, (*pieces(r0, s0), *pieces(r1, s1)), columns)
     r3z, r3b, carried = lax.optimization_barrier((r3z, r3b, carried))
-    e, zr, partners, sums = scores(2, (*pieces(r2, s2), r3z, r3b, swap(r3z), swap(r3b)), carried=carried)
+    carried = scores(2, pieces(r2, s2), carried=carried)
+    e, zr, partners, sums = scores(3, (r3z, r3b, swap(r3z), swap(r3b)), carried=carried)
     sums = lax.all_to_all(sums, ALL, 0, 0, tiled=True)
     e, zr, partners = (pltpu.with_memory_space_constraint(v, pltpu.HBM) for v in (e, zr, partners))
     here, *away, uc, ur, logs = gradients((4, 5, 6, 7), sums, e, zr, partners)

time: 100 us -> 101 us (1.010)
  Pallas kernels: 35.8 us -> 37 us
    pallas_call x2 -> x3, Pallas kernels: 16.9 us -> 18.2 us  [scores(): pl.pallas_call(functools.partial(score_kernel, start, steps), grid=(steps...]
  transfers between devices with their start and end apart: 22 -> 22, of which waited for: 7 -> 7; matrix products, arithmetic and copies ran while one was open for 0% -> 0% of each run, Pallas kernels for 18% -> 22%
where the time goes in v7:
time: 101 us
  Pallas kernels  37 us (37%)
  starting transfers between devices  28.8 us (29%)
  blocking collectives  17.1 us (17%)
  waiting for transfers between devices  16.9 us (17%)
    pallas_call x3, Pallas kernels, scores(): pl.pallas_call(functools.partial(score_kernel, start, steps), grid=(steps...  18.2 us
    all_to_all x1, blocking collectives, shards(): sums = lax.all_to_all(sums, ALL, 0, 0, tiled=True)  17.1 us
    pallas_call x3, Pallas kernels, gradients(): pl.pallas_call(functools.partial(gradient_kernel, slots, first), grid=(ST...  17 us
    ppermute x2, waiting for transfers between devices, shards(): r1, r2 = (lax.ppermute(r0, 'x', UP), lax.ppermute(r0, 'x', DOWN))  5.25 us
    ppermute x4, starting transfers between devices, over_y(): return (across, lax.ppermute(down, 'y', DOWN), lax.ppermute(up, 'y', UP))  4.61 us
    ppermute x1, starting transfers between devices, shards(): lax.ppermute(c2[:PER], 'y', DOWN)  3.76 us
    ppermute x1, starting transfers between devices, shards(): lax.ppermute(r2[:BLOCK], 'x', DOWN)  3.76 us
    ppermute x1, waiting for transfers between devices, shards(): b = lax.ppermute(block, 'zh', SWAP)  3.62 us
  transfers between devices with their start and end apart: 22, of which 7 were waited for; matrix products, arithmetic and copies ran while one was open for 0% of the time, Pallas kernels for 22%

profile of v7, /device:TPU:0, one launch (start us, length us, event | category | flops | bytes accessed | tf_op | source)
XLA Modules:
  0.0 101.1 jit_solution(14496975653831928159)
XLA Ops:
  0.6 0.9 shard_map.41.refs_8_
  1.6 2.1 %collective-permute-start.5 = (f32[192,256]{1,0:T(8,128)}, f32[192,256]{1,0:T(8,128)S(1)}, u32[]{:S(2)}, u32[]{:S(2)}) collective-permute-start(f32[192,256]{1,0:T(8,128)} %z_ref.2), channel_id=1, source_target_pairs={{0,16},{16,0},{1,17},{17,1},{2,18},{18,2},{3,19},{19,3},{4,20},{20... | collective-permute-start | bytes 589832 | tf_op jit(solution)/shard_map/ppermute | solution.py:343
  3.7 3.6 %collective-permute-start = (f32[200,256]{1,0:T(8,128)S(1)}, f32[200,256]{1,0:T(8,128)S(1)}, u32[]{:S(2)}, u32[]{:S(2)}) collective-permute-start(f32[200,256]{1,0:T(8,128)S(1)} %shard_map.41.refs_8_), channel_id=1, source_target_pairs={{0,2},{2,0},{1,3},{3,1},{4,6},{6,4},{5,7},{7,5},{8,10},{10,8},{9,1... | collective-permute-start | bytes 614408 | tf_op jit(solution)/shard_map/ppermute | solution.py:344
  7.3 2.4 %collective-permute-done.5.refs_4_ = f32[192,256]{1,0:T(8,128)S(1)} collective-permute-done((f32[192,256]{1,0:T(8,128)}, f32[192,256]{1,0:T(8,128)S(1)}, u32[]{:S(2)}, u32[]{:S(2)}) %collective-permute-start.5) | collective-permute-done | bytes 196640 | tf_op jit(solution)/shard_map/ppermute | solution.py:343
  9.7 3.2 %collective-permute-start.7 = (f32[384,256]{1,0:T(8,128)S(1)}, f32[384,256]{1,0:T(8,128)S(1)}, u32[]{:S(2)}, u32[]{:S(2)}) collective-permute-start(f32[384,256]{1,0:T(8,128)S(1)} %pad_maximum_fusion), channel_id=1, source_target_pairs={{0,96},{32,0},{64,32},{96,64},{1,97},{33,1},{65,33},{97,65},{2,98}... | collective-permute-start | bytes 1179656 | tf_op jit(solution)/shard_map/ppermute | solution.py:346
  12.8 3.6 %collective-permute-done.refs_9_ = f32[200,256]{1,0:T(8,128)S(1)} collective-permute-done((f32[200,256]{1,0:T(8,128)S(1)}, f32[200,256]{1,0:T(8,128)S(1)}, u32[]{:S(2)}, u32[]{:S(2)}) %collective-permute-start) | collective-permute-done | bytes 204832 | tf_op jit(solution)/shard_map/ppermute | solution.py:344
  16.6 2.8 %collective-permute-start.3 = (f32[400,256]{1,0:T(8,128)S(1)}, f32[400,256]{1,0:T(8,128)S(1)}, u32[]{:S(2)}, u32[]{:S(2)}) collective-permute-start(f32[400,256]{1,0:T(8,128)S(1)} %constant_dynamic-update-slice_fusion), channel_id=1, source_target_pairs={{0,12},{4,0},{8,4},{12,8},{1,13},{5,1},{9,5},{13,9},{2,14},{6,2},{... | collective-permute-start | bytes 1228808 | tf_op jit(solution)/shard_map/ppermute | solution.py:349
  19.6 3.8 %collective-permute-start.9 = (f32[192,256]{1,0:T(8,128)S(1)}, f32[192,256]{1,0:T(8,128)S(1)}, u32[]{:S(2)}, u32[]{:S(2)}) collective-permute-start(f32[192,256]{1,0:T(8,128)S(1)} %get-tuple-element.100.refs_6_), channel_id=1, source_target_pairs={{0,96},{32,0},{64,32},{96,64},{1,97},{33,1},{65,33},{97,65},{2,98}... | collective-permute-start | bytes 589832 | tf_op jit(solution)/shard_map/ppermute | solution.py:347
  23.5 5.3 %collective-permute-done.3 = f32[400,256]{1,0:T(8,128)S(1)} collective-permute-done((f32[400,256]{1,0:T(8,128)S(1)}, f32[400,256]{1,0:T(8,128)S(1)}, u32[]{:S(2)}, u32[]{:S(2)}) %collective-permute-start.3) | collective-permute-done | bytes 409632 | tf_op jit(solution)/shard_map/ppermute | solution.py:349
  28.8 3.8 %collective-permute-start.4 = (f32[200,256]{1,0:T(8,128)S(1)}, f32[200,256]{1,0:T(8,128)S(1)}, u32[]{:S(2)}, u32[]{:S(2)}) collective-permute-start(f32[200,256]{1,0:T(8,128)S(1)} %get-tuple-element.93.refs_1_), channel_id=1, source_target_pairs={{0,12},{4,0},{8,4},{12,8},{1,13},{5,1},{9,5},{13,9},{2,14},{6,2},{... | collective-permute-start | bytes 614408 | tf_op jit(solution)/shard_map/ppermute | solution.py:350
  32.7 1.6 %collective-permute-done.11 = f32[400,256]{1,0:T(8,128)S(1)} collective-permute-done((f32[400,256]{1,0:T(8,128)S(1)}, f32[400,256]{1,0:T(8,128)S(1)}, u32[]{:S(2)}, u32[]{:S(2)}) %collective-permute-start.11) | collective-permute-done | bytes 409632 | tf_op jit(solution)/shard_map/ppermute | solution.py:351
  34.5 8.2 %shard_map.42 = (f32[12,1536,256]{2,1,0:T(8,128)}, bf16[3072,512]{1,0:T(8,128)(2,1)}, f32[4,1,768]{2,1,0:T(1,128)}, f32[2,1,768]{2,1,0:T(1,128)S(1)}, f32[8,128]...) custom-call(f32[192,256]{1,0:T(8,128)S(1)} %copy-done, ...), custom_call_target="tpu_custom_call" | custom-call | flops 3623878656 | bytes 9437184 | tf_op jit(solution)/shard_map/pallas_call | solution.py:177
  43.4 4.4 %shard_map.43 = (f32[12,1536,256]{2,1,0:T(8,128)}, bf16[3072,512]{1,0:T(8,128)(2,1)}, f32[4,1,768]{2,1,0:T(1,128)}, f32[1,1,768]{2,1,0:T(1,128)S(1)}, f32[8,128]{1,0:T(8,128)S(1)}, /*index=5*/f32[1536,128]{1,0:T(8,128)S(1)}) custom-call(f32[200,256]{1,0:T(8,128)S(1)} %get-tuple-element.92.refs_0_, ...), custom_call_target="tpu_custom_call", output_to_operand_aliasing={{0}: (8, {}), {1}: (9, {}), {2}: (10, {})} | custom-call | flops 1811939328 | bytes 4718592 | tf_op jit(solution)/shard_map/pallas_call | solution.py:177
  47.7 5.6 %shard_map.44 = (f32[12,1536,256]{2,1,0:T(8,128)}, bf16[3072,512]{1,0:T(8,128)(2,1)}, f32[4,1,768]{2,1,0:T(1,128)}, f32[128,1,512]{2,1,0:T(1,128)S(1)}) custom-call(f32[200,256]{1,0:T(8,128)S(1)} %collective-permute-done.2.refs_0_, f32[200,256]{1,0:T(8,128)S(1)} %collective-permute-done.4.refs_1_, ...), custom_call_target="tpu_custom_call", output_to_operand_aliasing={{0}: (8, {}), {1}: (9, {}), {2}: (10, {})} | custom-call | flops 1811939328 | bytes 4718592 | tf_op jit(solution)/shard_map/pallas_call | solution.py:177
  53.3 17.1 %all_to_all.5.sums_ref = f32[128,1,512]{2,1,0:T(1,128)S(1)} all-to-all(f32[128,1,512]{2,1,0:T(1,128)S(1)} %get-tuple-element.72), channel_id=1, replica_groups=mesh['y'=4,'zl'=2,'x'=4,'zh'=2,'core'=2] {'y','zl','x','zh','core'}, dimensions={0} | all-to-all | bytes 524288 | tf_op jit(solution)/shard_map/all_to_all | solution.py:359
  70.4 7.8 %shard_map.45 = (f32[200,256]{1,0:T(8,128)S(1)}, f32[200,256]{1,0:T(8,128)S(1)}, f32[200,256]{1,0:T(8,128)S(1)}, f32[200,256]{1,0:T(8,128)S(1)}, f32[1536,128]{1...) custom-call(f32[128,1,512]{2,1,0:T(1,128)S(1)} %all_to_all.5.sums_ref, ...), custom_call_target="tpu_custom_call" | custom-call | flops 3623878656 | bytes 9437184 | tf_op jit(solution)/shard_map/pallas_call | solution.py:276
  79.0 2.6 %collective-permute-start.16 = (f32[200,256]{1,0:T(8,128)S(1)}, f32[200,256]{1,0:T(8,128)S(1)}, u32[]{:S(2)}, u32[]{:S(2)}) collective-permute-start(f32[200,256]{1,0:T(8,128)S(1)} %get-tuple-element.79), channel_id=1, source_target_pairs={{0,96},{32,0},{64,32},{96,64},{1,97},{33,1},{65,33},{97,65},{2,98}... | collective-permute-start | bytes 614408 | tf_op jit(solution)/shard_map/ppermute | solution.py:337
  81.6 5.9 %shard_map.47 = (f32[200,256]{1,0:T(8,128)S(1)}, f32[200,256]{1,0:T(8,128)S(1)}, f32[200,256]{1,0:T(8,128)S(1)}) custom-call(f32[1,256]{1,0:T(1,128)S(1)} %get-tuple-element.81.sums_ref, f32[12,1536,256]{2,1,0:T(8,128)} %get-tuple-element.73.refs_0_.refs_1_.refs_2_.refs_3_, f32[12,1536,256]{2,1,0:T(8,128)} %get-tuple-element.73.refs_0_.refs_1_.refs_2_.refs_3_, ...), custom_call_target="tpu_custom_call" | custom-call | flops 2717908992 | bytes 7077888 | tf_op jit(solution)/shard_map/pallas_call | solution.py:276
  87.5 2.3 %collective-permute-start.18 = (f32[200,256]{1,0:T(8,128)S(1)}, f32[200,256]{1,0:T(8,128)S(1)}, u32[]{:S(2)}, u32[]{:S(2)}) collective-permute-start(f32[200,256]{1,0:T(8,128)S(1)} %get-tuple-element.84), channel_id=1, source_target_pairs={{0,64},{32,96},{64,0},{96,32},{1,65},{33,97},{65,1},{97,33},{2,66}... | collective-permute-start | bytes 614408 | tf_op jit(solution)/shard_map/ppermute | solution.py:336
  89.8 1.1 %collective-permute-start.19 = (f32[200,256]{1,0:T(8,128)S(1)}, f32[200,256]{1,0:T(8,128)S(1)}, u32[]{:S(2)}, u32[]{:S(2)}) collective-permute-start(f32[200,256]{1,0:T(8,128)S(1)} %get-tuple-element.85), channel_id=1, source_target_pairs={{0,96},{32,0},{64,32},{96,64},{1,97},{33,1},{65,33},{97,65},{2,98}... | collective-permute-start | bytes 614408 | tf_op jit(solution)/shard_map/ppermute | solution.py:337
  90.9 0.9 collective-permute-start.20
  92.8 3.3 %shard_map.46.refs_0_ = f32[200,256]{1,0:T(8,128)S(1)} custom-call(f32[1,256]{1,0:T(1,128)S(1)} %get-tuple-element.81.sums_ref, f32[12,1536,256]{2,1,0:T(8,128)} %get-tuple-element.73.refs_0_.refs_1_.refs_2_.refs_3_, bf16[3072,512]{1,0:T(8,128)(2,1)} %get-tuple-element.74.refs_4_.refs_1_.refs_3_, f32[4,1,768]{2,1,0:T(1,128)} %get-tuple-element.75.refs_5_.refs_2_.refs_4_, ...), custom_call_target="tpu_custom_call" | custom-call | flops 905969664 | bytes 2359296 | tf_op jit(solution)/shard_map/pallas_call | solution.py:276
  96.1 1.0 collective-permute-done.18.refs_1_
  97.1 3.0 %collective-permute-done.19.refs_2_ = f32[200,256]{1,0:T(8,128)S(1)} collective-permute-done((f32[200,256]{1,0:T(8,128)S(1)}, f32[200,256]{1,0:T(8,128)S(1)}, u32[]{:S(2)}, u32[]{:S(2)}) %collective-permute-start.19) | collective-permute-done | bytes 204832 | tf_op jit(solution)/shard_map/ppermute | solution.py:337
  (43 shorter events, 4.1 us)
Async XLA Ops:
  1.6 8.0 %collective-permute-start.5 = (f32[192,256]{1,0:T(8,128)}, f32[192,256]{1,0:T(8,128)S(1)}, u32[]{:S(2)}, u32[]{:S(2)}) collective-permute-start(f32[192,256]{1,0:T(8,128)} %z_ref.2), channel_id=1, source_target_pairs={{0,16},{16,0},{1,17},{17,1},{2,18},{18,2},{3,19},{19,3},{4,20},{20... | collective-permute-start | bytes 589832 | tf_op jit(solution)/shard_map/ppermute | solution.py:343
  3.7 12.8 %collective-permute-start = (f32[200,256]{1,0:T(8,128)S(1)}, f32[200,256]{1,0:T(8,128)S(1)}, u32[]{:S(2)}, u32[]{:S(2)}) collective-permute-start(f32[200,256]{1,0:T(8,128)S(1)} %shard_map.41.refs_8_), channel_id=1, source_target_pairs={{0,2},{2,0},{1,3},{3,1},{4,6},{6,4},{5,7},{7,5},{8,10},{10,8},{9,1... | collective-permute-start | bytes 614408 | tf_op jit(solution)/shard_map/ppermute | solution.py:344
  7.3 27.2 %copy-start = (f32[192,256]{1,0:T(8,128)S(1)}, f32[192,256]{1,0:T(8,128)}, u32[]{:S(2)}) copy-start(f32[192,256]{1,0:T(8,128)} %z_ref.2) | copy-start | bytes 589828
  9.7 9.9 %collective-permute-start.7 = (f32[384,256]{1,0:T(8,128)S(1)}, f32[384,256]{1,0:T(8,128)S(1)}, u32[]{:S(2)}, u32[]{:S(2)}) collective-permute-start(f32[384,256]{1,0:T(8,128)S(1)} %pad_maximum_fusion), channel_id=1, source_target_pairs={{0,96},{32,0},{64,32},{96,64},{1,97},{33,1},{65,33},{97,65},{2,98}... | collective-permute-start | bytes 1179656 | tf_op jit(solution)/shard_map/ppermute | solution.py:346
  12.8 10.6 %collective-permute-start.6 = (f32[384,256]{1,0:T(8,128)S(1)}, f32[384,256]{1,0:T(8,128)S(1)}, u32[]{:S(2)}, u32[]{:S(2)}) collective-permute-start(f32[384,256]{1,0:T(8,128)S(1)} %pad_maximum_fusion), channel_id=1, source_target_pairs={{0,32},{32,64},{64,96},{96,0},{1,33},{33,65},{65,97},{97,1},{2,34}... | collective-permute-start | bytes 1179656 | tf_op jit(solution)/shard_map/ppermute | solution.py:346
  16.5 16.1 %collective-permute-start.10 = (f32[400,256]{1,0:T(8,128)S(1)}, f32[400,256]{1,0:T(8,128)S(1)}, u32[]{:S(2)}, u32[]{:S(2)}) collective-permute-start(f32[400,256]{1,0:T(8,128)S(1)} %constant_dynamic-update-slice_fusion), channel_id=1, source_target_pairs={{0,1},{1,0},{2,3},{3,2},{4,5},{5,4},{6,7},{7,6},{8,9},{9,8},{10,11... | collective-permute-start | bytes 1228808 | tf_op jit(solution)/shard_map/ppermute | solution.py:351
  16.6 12.2 %collective-permute-start.3 = (f32[400,256]{1,0:T(8,128)S(1)}, f32[400,256]{1,0:T(8,128)S(1)}, u32[]{:S(2)}, u32[]{:S(2)}) collective-permute-start(f32[400,256]{1,0:T(8,128)S(1)} %constant_dynamic-update-slice_fusion), channel_id=1, source_target_pairs={{0,12},{4,0},{8,4},{12,8},{1,13},{5,1},{9,5},{13,9},{2,14},{6,2},{... | collective-permute-start | bytes 1228808 | tf_op jit(solution)/shard_map/ppermute | solution.py:349
  19.4 13.1 %collective-permute-start.1 = (f32[400,256]{1,0:T(8,128)S(1)}, f32[400,256]{1,0:T(8,128)S(1)}, u32[]{:S(2)}, u32[]{:S(2)}) collective-permute-start(f32[400,256]{1,0:T(8,128)S(1)} %constant_dynamic-update-slice_fusion), channel_id=1, source_target_pairs={{0,4},{4,8},{8,12},{12,0},{1,5},{5,9},{9,13},{13,1},{2,6},{6,10},{... | collective-permute-start | bytes 1228808 | tf_op jit(solution)/shard_map/ppermute | solution.py:349
  19.6 14.8 %collective-permute-start.9 = (f32[192,256]{1,0:T(8,128)S(1)}, f32[192,256]{1,0:T(8,128)S(1)}, u32[]{:S(2)}, u32[]{:S(2)}) collective-permute-start(f32[192,256]{1,0:T(8,128)S(1)} %get-tuple-element.100.refs_6_), channel_id=1, source_target_pairs={{0,96},{32,0},{64,32},{96,64},{1,97},{33,1},{65,33},{97,65},{2,98}... | collective-permute-start | bytes 589832 | tf_op jit(solution)/shard_map/ppermute | solution.py:347
  23.4 11.1 %collective-permute-start.8 = (f32[192,256]{1,0:T(8,128)S(1)}, f32[192,256]{1,0:T(8,128)S(1)}, u32[]{:S(2)}, u32[]{:S(2)}) collective-permute-start(f32[192,256]{1,0:T(8,128)S(1)} %get-tuple-element.103.refs_1_), channel_id=1, source_target_pairs={{0,32},{32,64},{64,96},{96,0},{1,33},{33,65},{65,97},{97,1},{2,34}... | collective-permute-start | bytes 589832 | tf_op jit(solution)/shard_map/ppermute | solution.py:347
  28.8 13.9 %collective-permute-start.4 = (f32[200,256]{1,0:T(8,128)S(1)}, f32[200,256]{1,0:T(8,128)S(1)}, u32[]{:S(2)}, u32[]{:S(2)}) collective-permute-start(f32[200,256]{1,0:T(8,128)S(1)} %get-tuple-element.93.refs_1_), channel_id=1, source_target_pairs={{0,12},{4,0},{8,4},{12,8},{1,13},{5,1},{9,5},{13,9},{2,14},{6,2},{... | collective-permute-start | bytes 614408 | tf_op jit(solution)/shard_map/ppermute | solution.py:350
  32.5 1.7 %collective-permute-start.11 = (f32[400,256]{1,0:T(8,128)S(1)}, f32[400,256]{1,0:T(8,128)S(1)}, u32[]{:S(2)}, u32[]{:S(2)}) collective-permute-start(f32[400,256]{1,0:T(8,128)S(1)} %collective-permute-done.1), channel_id=1, source_target_pairs={{0,1},{1,0},{2,3},{3,2},{4,5},{5,4},{6,7},{7,6},{8,9},{9,8},{10,11... | collective-permute-start | bytes 1228808 | tf_op jit(solution)/shard_map/ppermute | solution.py:351
  32.6 10.1 %collective-permute-start.2 = (f32[200,256]{1,0:T(8,128)S(1)}, f32[200,256]{1,0:T(8,128)S(1)}, u32[]{:S(2)}, u32[]{:S(2)}) collective-permute-start(f32[200,256]{1,0:T(8,128)S(1)} %get-tuple-element.97.refs_12_), channel_id=1, source_target_pairs={{0,4},{4,8},{8,12},{12,0},{1,5},{5,9},{9,13},{13,1},{2,6},{6,10},{... | collective-permute-start | bytes 614408 | tf_op jit(solution)/shard_map/ppermute | solution.py:350
  34.3 9.0 %collective-permute-start.14 = (f32[400,256]{1,0:T(8,128)S(1)}, f32[400,256]{1,0:T(8,128)S(1)}, u32[]{:S(2)}, u32[]{:S(2)}) collective-permute-start(f32[400,256]{1,0:T(8,128)S(1)} %collective-permute-done.3), channel_id=1, source_target_pairs={{0,1},{1,0},{2,3},{3,2},{4,5},{5,4},{6,7},{7,6},{8,9},{9,8},{10,11... | collective-permute-start | bytes 1228808 | tf_op jit(solution)/shard_map/ppermute | solution.py:351
  42.7 5.0 %collective-permute-start.12 = (f32[200,256]{1,0:T(8,128)S(1)}, f32[200,256]{1,0:T(8,128)S(1)}, u32[]{:S(2)}, u32[]{:S(2)}) collective-permute-start(f32[200,256]{1,0:T(8,128)S(1)} %collective-permute-done.2.refs_0_), channel_id=1, source_target_pairs={{0,1},{1,0},{2,3},{3,2},{4,5},{5,4},{6,7},{7,6},{8,9},{9,8},{10,11... | collective-permute-start | bytes 614408 | tf_op jit(solution)/shard_map/ppermute | solution.py:351
  43.2 4.6 %collective-permute-start.13 = (f32[200,256]{1,0:T(8,128)S(1)}, f32[200,256]{1,0:T(8,128)S(1)}, u32[]{:S(2)}, u32[]{:S(2)}) collective-permute-start(f32[200,256]{1,0:T(8,128)S(1)} %collective-permute-done.4.refs_1_), channel_id=1, source_target_pairs={{0,1},{1,0},{2,3},{3,2},{4,5},{5,4},{6,7},{7,6},{8,9},{9,8},{10,11... | collective-permute-start | bytes 614408 | tf_op jit(solution)/shard_map/ppermute | solution.py:351
  78.2 12.8 %collective-permute-start.15 = (f32[200,256]{1,0:T(8,128)S(1)}, f32[200,256]{1,0:T(8,128)S(1)}, u32[]{:S(2)}, u32[]{:S(2)}) collective-permute-start(f32[200,256]{1,0:T(8,128)S(1)} %get-tuple-element.78), channel_id=1, source_target_pairs={{0,64},{32,96},{64,0},{96,32},{1,65},{33,97},{65,1},{97,33},{2,66}... | collective-permute-start | bytes 614408 | tf_op jit(solution)/shard_map/ppermute | solution.py:336
  79.0 12.9 %collective-permute-start.16 = (f32[200,256]{1,0:T(8,128)S(1)}, f32[200,256]{1,0:T(8,128)S(1)}, u32[]{:S(2)}, u32[]{:S(2)}) collective-permute-start(f32[200,256]{1,0:T(8,128)S(1)} %get-tuple-element.79), channel_id=1, source_target_pairs={{0,96},{32,0},{64,32},{96,64},{1,97},{33,1},{65,33},{97,65},{2,98}... | collective-permute-start | bytes 614408 | tf_op jit(solution)/shard_map/ppermute | solution.py:337
  81.6 10.3 %collective-permute-start.17 = (f32[200,256]{1,0:T(8,128)S(1)}, f32[200,256]{1,0:T(8,128)S(1)}, u32[]{:S(2)}, u32[]{:S(2)}) collective-permute-start(f32[200,256]{1,0:T(8,128)S(1)} %get-tuple-element.80), channel_id=1, source_target_pairs={{0,32},{32,64},{64,96},{96,0},{1,33},{33,65},{65,97},{97,1},{2,34}... | collective-permute-start | bytes 614408 | tf_op jit(solution)/shard_map/ppermute | solution.py:337
  87.5 9.6 %collective-permute-start.18 = (f32[200,256]{1,0:T(8,128)S(1)}, f32[200,256]{1,0:T(8,128)S(1)}, u32[]{:S(2)}, u32[]{:S(2)}) collective-permute-start(f32[200,256]{1,0:T(8,128)S(1)} %get-tuple-element.84), channel_id=1, source_target_pairs={{0,64},{32,96},{64,0},{96,32},{1,65},{33,97},{65,1},{97,33},{2,66}... | collective-permute-start | bytes 614408 | tf_op jit(solution)/shard_map/ppermute | solution.py:336
  89.8 10.2 %collective-permute-start.19 = (f32[200,256]{1,0:T(8,128)S(1)}, f32[200,256]{1,0:T(8,128)S(1)}, u32[]{:S(2)}, u32[]{:S(2)}) collective-permute-start(f32[200,256]{1,0:T(8,128)S(1)} %get-tuple-element.85), channel_id=1, source_target_pairs={{0,96},{32,0},{64,32},{96,64},{1,97},{33,1},{65,33},{97,65},{2,98}... | collective-permute-start | bytes 614408 | tf_op jit(solution)/shard_map/ppermute | solution.py:337
  90.9 9.1 %collective-permute-start.20 = (f32[200,256]{1,0:T(8,128)S(1)}, f32[200,256]{1,0:T(8,128)S(1)}, u32[]{:S(2)}, u32[]{:S(2)}) collective-permute-start(f32[200,256]{1,0:T(8,128)S(1)} %get-tuple-element.86), channel_id=1, source_target_pairs={{0,32},{32,64},{64,96},{96,0},{1,33},{33,65},{65,97},{97,1},{2,34}... | collective-permute-start | bytes 614408 | tf_op jit(solution)/shard_map/ppermute | solution.py:337
  91.9 8.1 %collective-permute-start.21 = (f32[200,256]{1,0:T(8,128)S(1)}, f32[200,256]{1,0:T(8,128)S(1)}, u32[]{:S(2)}, u32[]{:S(2)}) collective-permute-start(f32[200,256]{1,0:T(8,128)S(1)} %add_add_fusion), channel_id=1, source_target_pairs={{0,16},{16,0},{1,17},{17,1},{2,18},{18,2},{3,19},{19,3},{4,20},{20... | collective-permute-start | bytes 614408 | tf_op jit(solution)/shard_map/ppermute | solution.py:366
